TPU v7x, 512 devices: a whole 4x4x16 slice. The times are simulated.
512 devices in a mesh: dp: 4 (over x), fsdp: 128 (over y, z, core).
Axes of the slice: x: 4, y: 4, z: 16, core: 2. Of those that a mesh axis runs over, the one named last changes fastest.
Arguments:
- grads: bfloat16 [4, 64, 2048, 768], P('dp', None, 'fsdp'), may hold values from -400 to 400, as said below
- owners: int32 [64], replicated, may hold values from 0 to 126, as said below
Outputs:
- updates: bfloat16 [64, 2048, 768], P('dp', 'fsdp')
- owner_rms: float32 [4, 128], P('dp', 'fsdp')
Inputs may be any that keep to these rules, and one draw needn't show every extreme that they name: Matrix m is updated by replica m // 16; every owner is even; within each aligned block of 16 matrices the owners are distinct. `grads`: gradients are finite reals.
All inputs are finite; a program needn't handle non-finite values.
Results may differ from a plain program's by a relative error of at most 0.015.
Values may be sent and summed in bfloat16 or wider, within the bound.
No kernel may reach another device: no remote copies, remote signals or barrier semaphores. Data moves between devices by JAX's collectives and lax.ppermute only.
A program may use at most 128 MiB of HBM per device.

v0:
```python
import math

import jax
import jax.numpy as jnp
from jax import lax
from jax.sharding import PartitionSpec as P

ITERS = 2


COEF_A = 3.4445
COEF_B = -4.775
COEF_C = 2.0315
EPS = 1e-07


def from_partner(value, axis, distance):
    mask = 2**distance
    pairs = [(source, source ^ mask) for source in range(lax.axis_size(axis))]
    return lax.ppermute(value, axis, pairs)


def pair_total(partial_gram):
    return partial_gram + from_partner(partial_gram.astype(jnp.bfloat16), "fsdp", 0).astype(
        partial_gram.dtype
    )


def normalize(half_rows):
    wide = half_rows.astype(jnp.float32)
    partial_sq = jnp.sum(wide * wide)
    total = partial_sq + from_partner(partial_sq, "fsdp", 0)
    norm = jnp.sqrt(total)
    return ((wide / (norm + EPS)).astype(jnp.bfloat16), norm)


def iterate(current, full_rows, combine):
    result = None
    for step in range(ITERS):
        partial_gram = jnp.dot(current.T, current, preferred_element_type=jnp.float32)
        gram = combine(partial_gram).astype(jnp.bfloat16)
        square = jnp.dot(gram, gram, preferred_element_type=jnp.float32)
        poly = (COEF_B * gram.astype(jnp.float32) + COEF_C * square).astype(jnp.bfloat16)
        nxt = COEF_A * current.astype(jnp.float32) + jnp.dot(
            current, poly, preferred_element_type=jnp.float32
        )
        if step + 1 < ITERS:
            current = nxt.astype(jnp.bfloat16)
        else:
            result = (math.sqrt(full_rows) * nxt).astype(jnp.bfloat16)
    return result


def route(slabs):
    return lax.all_to_all(slabs, "fsdp", split_axis=0, concat_axis=0, tiled=True)


def on_device(grads, owners):
    rows_dev = grads.shape[2]
    width = grads.shape[3]
    fsdp_n = lax.axis_size("fsdp")
    dp_n = lax.axis_size("dp")
    half_n = fsdp_n // 2
    block = owners.shape[0] // dp_n
    full_rows = fsdp_n * rows_dev
    replica = lax.axis_index("dp")
    column = lax.axis_index("fsdp")
    upper = (column >= half_n).astype(jnp.int32)
    parity = column % 2
    peers = jnp.arange(fsdp_n, dtype=jnp.int32)
    mine = lax.dynamic_slice_in_dim(owners, replica * block, block)
    select = ((mine + upper)[None, :] == peers[:, None]).astype(jnp.bfloat16)
    own_norm = None
    summed = lax.psum_scatter(
        grads[0].astype(jnp.float32).astype(jnp.bfloat16), "dp", scatter_dimension=0, tiled=True
    )
    outgoing = jnp.einsum("pk,krc->prc", select, summed, preferred_element_type=jnp.bfloat16)
    arrived = route(outgoing)
    half_rows = lax.dynamic_slice_in_dim(arrived, parity * half_n, half_n, 0).reshape(
        half_n * rows_dev, width
    )
    start, own_norm = normalize(half_rows)
    update = iterate(start, full_rows, pair_total)
    placed = lax.dynamic_update_slice_in_dim(
        jnp.zeros((fsdp_n, rows_dev, width), jnp.bfloat16),
        update.reshape(half_n, rows_dev, width),
        parity * half_n,
        0,
    )
    returned = lax.all_to_all(placed, "fsdp", split_axis=0, concat_axis=0, tiled=True)
    updates = jnp.einsum("pk,prc->krc", select, returned, preferred_element_type=jnp.bfloat16)
    owner_rms = (own_norm / math.sqrt(full_rows * width)).reshape(1, 1)
    return (updates, owner_rms)


def solution(mesh):
    in_specs = (P("dp", None, "fsdp", None), P())
    out_specs = (P("dp", "fsdp", None), P("dp", "fsdp"))
    return jax.shard_map(
        on_device, mesh=mesh, in_specs=in_specs, out_specs=out_specs, check_vma=False
    )
```

profile of v0, /device:TPU:1, one launch (start us, length us, event | category | flops | bytes accessed | tf_op | source)
XLA Modules:
  0.0 419.6 jit_solution(1418456823064853539)
XLA Ops:
  7.2 0.0 reduce-scatter.2.cloned.1.call-start
  7.2 0.7 reduce-scatter.2.cloned.1.call-update
  7.9 0.7 dynamic-slice_add_fusion
  8.6 39.9 %reduce-scatter.2.cloned.1.call-done = bf16[16,16,768]{2,1,0:T(8,128)(2,1)} async-done(((bf16[64,16,768]{2,1,0:T(8,128)(2,1)}), bf16[16,16,768]{2,1,0:T(8,128)(2,1)}) %reduce-scatter.2.cloned.1.call-update) | async-done | bytes 393232 | tf_op jit(solution)/shard_map/reduce_scatter | solution.py:74
  48.5 2.1 fusion.8
  50.6 3.4 copy.12
  54.0 18.1 %all-to-all-start = ((bf16[128,16,768]{2,1,0:T(8,128)(2,1)}), bf16[128,16,768]{2,1,0:T(8,128)(2,1)}, u32[]{:S(2)}, u32[]{:S(2)}) async-start(bf16[128,16,768]{2,1,0:T(8,128)(2,1)} %copy.12), calls=%async_computation.1 | async-start | bytes 6291456 | tf_op jit(solution)/shard_map/all_to_all | solution.py:55
  72.1 142.5 %all-to-all-done = bf16[128,16,768]{2,1,0:T(8,128)(2,1)} async-done(((bf16[128,16,768]{2,1,0:T(8,128)(2,1)}), bf16[128,16,768]{2,1,0:T(8,128)(2,1)}, u32[]{:S(2)}, u32[]{:S(2)}) %all-to-all-start) | async-done | bytes 3145760 | tf_op jit(solution)/shard_map/all_to_all | solution.py:55
  214.6 1.5 constant_dynamic-slice_fusion
  216.1 1.4 fusion
  217.5 3.2 collective-permute-start
  220.7 0.9 collective-permute-done
  223.0 0.6 fusion.1
  223.6 2.9 bitcast_convert_fusion
  226.5 2.4 collective-permute-start.1
  228.8 0.9 copy.14
  229.7 1.5 collective-permute-done.1
  231.2 6.9 %add_convert_fusion = bf16[1024,768]{1,0:T(8,128)(2,1)} fusion(bf16[1024,768]{1,0:T(8,128)(2,1)S(1)} %bitcast.28, bf16[768,768]{1,0:T(8,128)(2,1)S(1)} %collective-permute-done.1, f32[768,768,1]{1,0,2:T(8,128)} %get-tuple-element.9), kind=kOutput, calls=%fused_computation.7 | convolution fusion | flops 2123563008 | bytes 6684672 | tf_op jit(solution)/shard_map/dot_general | solution.py:44
  238.1 4.7 %fusion.19 = (bf16[768,768]{1,0:T(8,128)(2,1)S(1)}, f32[768,768]{1,0:T(8,128)}) fusion(bf16[1024,768]{1,0:T(8,128)(2,1)} %add_convert_fusion), kind=kOutput, calls=%fused_computation.27 | convolution fusion | flops 1208549376 | bytes 5111808 | tf_op jit(solution)/shard_map/dot_general | solution.py:40
  242.8 2.2 collective-permute-start.2
  245.0 2.5 collective-permute-done.2
  247.5 6.6 %multiply_convert_fusion = bf16[1024,768]{1,0:T(8,128)(2,1)S(1)} fusion(bf16[1024,768]{1,0:T(8,128)(2,1)} %add_convert_fusion, f32[768,768]{1,0:T(8,128)} %get-tuple-element.11, bf16[768,768]{1,0:T(8,128)(2,1)S(1)} %collective-permute-done.2), kind=kOutput, calls=%fused_computation.6 | convolution fusion | flops 2124349440 | bytes 6684672 | tf_op jit(solution)/shard_map/dot_general | solution.py:44
  254.1 1.9 broadcast_in_dim.2
  256.0 1.3 constant_dynamic-update-slice_fusion
  257.2 9.0 %all-to-all-start.1 = ((bf16[128,16,768]{2,1,0:T(8,128)(2,1)}), bf16[128,16,768]{2,1,0:T(8,128)(2,1)S(1)}, u32[]{:S(2)}, u32[]{:S(2)}) async-start(bf16[128,16,768]{2,1,0:T(8,128)(2,1)} %constant_dynamic-update-slice_fusion), calls=%async_computation.2 | async-start | bytes 6291456 | tf_op jit(solution)/shard_map/all_to_all | solution.py:90
  266.2 142.8 %all-to-all-done.1 = bf16[128,16,768]{2,1,0:T(8,128)(2,1)S(1)} async-done(((bf16[128,16,768]{2,1,0:T(8,128)(2,1)}), bf16[128,16,768]{2,1,0:T(8,128)(2,1)S(1)}, u32[]{:S(2)}, u32[]{:S(2)}) %all-to-all-start.1) | async-done | bytes 3145760 | tf_op jit(solution)/shard_map/all_to_all | solution.py:90
  409.0 1.8 fusion.2
  410.8 0.9 copy.16
Async XLA Ops:
  7.2 41.4 %reduce-scatter.2.cloned.1.call-start = ((), (), s32[]{:S(2)}) async-start(), calls=%async_computation.3 | async-start | bytes 1966080 | tf_op jit(solution)/shard_map/reduce_scatter | solution.py:74
  54.0 160.5 %all-to-all-start = ((bf16[128,16,768]{2,1,0:T(8,128)(2,1)}), bf16[128,16,768]{2,1,0:T(8,128)(2,1)}, u32[]{:S(2)}, u32[]{:S(2)}) async-start(bf16[128,16,768]{2,1,0:T(8,128)(2,1)} %copy.12), calls=%async_computation.1 | async-start | bytes 6291456 | tf_op jit(solution)/shard_map/all_to_all | solution.py:55
  217.5 4.1 collective-permute-start
  226.5 4.7 %collective-permute-start.1 = (bf16[768,768]{1,0:T(8,128)(2,1)S(1)}, bf16[768,768]{1,0:T(8,128)(2,1)S(1)}, u32[]{:S(2)}, u32[]{:S(2)}) collective-permute-start(bf16[768,768]{1,0:T(8,128)(2,1)S(1)} %get-tuple-element.8), channel_id=1, source_target_pairs={{0,1},{1,0},{2,3},{3,2},{4,5},{5,4},{6,7},{7,6},{8,9},{9,8},{10,11... | collective-permute-start | bytes 3538952 | tf_op jit(solution)/shard_map/ppermute | solution.py:20
  242.8 4.7 %collective-permute-start.2 = (bf16[768,768]{1,0:T(8,128)(2,1)S(1)}, bf16[768,768]{1,0:T(8,128)(2,1)S(1)}, u32[]{:S(2)}, u32[]{:S(2)}) collective-permute-start(bf16[768,768]{1,0:T(8,128)(2,1)S(1)} %get-tuple-element.10), channel_id=1, source_target_pairs={{0,1},{1,0},{2,3},{3,2},{4,5},{5,4},{6,7},{7,6},{8,9},{9,8},{10,11... | collective-permute-start | bytes 3538952 | tf_op jit(solution)/shard_map/ppermute | solution.py:20
  257.2 151.8 %all-to-all-start.1 = ((bf16[128,16,768]{2,1,0:T(8,128)(2,1)}), bf16[128,16,768]{2,1,0:T(8,128)(2,1)S(1)}, u32[]{:S(2)}, u32[]{:S(2)}) async-start(bf16[128,16,768]{2,1,0:T(8,128)(2,1)} %constant_dynamic-update-slice_fusion), calls=%async_computation.2 | async-start | bytes 6291456 | tf_op jit(solution)/shard_map/all_to_all | solution.py:90
Sparse Core Ops, SparseCore 0:
  10.8 37.6 reduce-scatter.1
where the time goes:
time: 420 us
  waiting for transfers between devices  331 us (79%)
  starting transfers between devices  34.8 us (8%)
  matrix products  24.9 us (6%)
  between operations  16.6 us (4%)
  local copies, waits for them, and re-layouts  9.79 us (2%)
    all_to_all x1, waiting for transfers between devices, on_device(): lax.all_to_all(placed, 'fsdp', split_axis=0, concat_axis=0, tiled=True)  143 us
    all_to_all x1, waiting for transfers between devices, route(): lax.all_to_all(slabs, 'fsdp', split_axis=0, concat_axis=0, tiled=True)  142 us
    reduce_scatter x1, waiting for transfers between devices, on_device(): lax.psum_scatter(grads[0].astype(jnp.float32).astype(jnp.bfloat16), 'dp',...  39.9 us
    all_to_all x1, starting transfers between devices, route(): lax.all_to_all(slabs, 'fsdp', split_axis=0, concat_axis=0, tiled=True)  18.1 us
    dot_general x2, matrix products, iterate(): jnp.dot(current, poly, preferred_element_type=jnp.float32)  13.4 us
    all_to_all x1, starting transfers between devices, on_device(): lax.all_to_all(placed, 'fsdp', split_axis=0, concat_axis=0, tiled=True)  8.98 us
  transfers between devices with their start and end apart: 6, of which 6 were waited for; matrix products, arithmetic and copies ran while one was open for 0% of the time, Pallas kernels for 0%

commit v1 on v0

v1 whole, which is shorter than its diff:
```python
import functools
import math

import jax
import jax.numpy as jnp
from jax import lax
from jax.experimental import pallas as pl
from jax.experimental.pallas import tpu as pltpu
from jax.sharding import Mesh
from jax.sharding import PartitionSpec as P

COEF_A = 3.4445
COEF_B = -4.775
COEF_C = 2.0315
EPS = 1e-07

BF16 = jnp.bfloat16
F32 = jnp.float32
VMEM = pl.BlockSpec(memory_space=pltpu.VMEM)
TILE = 256


def columns(i):
    return pl.ds(pl.multiple_of(i * TILE, TILE), TILE)


def dot(a, b):
    return jnp.dot(a, b, preferred_element_type=F32)


def gram_kernel(*refs):
    *pieces, wide_ref, sent_ref, stack = refs
    rows = pieces[0].shape[0]
    for i, piece in enumerate(pieces):
        stack[i * rows : (i + 1) * rows, :] = piece[...]

    @pl.loop(0, wide_ref.shape[1] // TILE)
    def _(n):
        part = lax.dot_general(
            stack[...], stack[:, columns(n)], (((0,), (0,)), ((), ())), preferred_element_type=F32
        )
        wide_ref[:, columns(n)] = part
        sent_ref[:, columns(n)] = part.astype(BF16)


def gram(pieces):
    rows, width = pieces[0].shape
    return pl.pallas_call(
        gram_kernel,
        out_shape=(
            jax.ShapeDtypeStruct((width, width), F32),
            jax.ShapeDtypeStruct((width, width), BF16),
        ),
        in_specs=[VMEM] * len(pieces),
        out_specs=(VMEM, VMEM),
        scratch_shapes=[pltpu.VMEM((rows * len(pieces), width), BF16)],
        compiler_params=pltpu.CompilerParams(vmem_limit_bytes=32 * 2**20),
        cost_estimate=pl.CostEstimate(
            flops=2 * rows * len(pieces) * width * width,
            bytes_accessed=rows * len(pieces) * width * 2 + width * width * 6,
            transcendentals=0,
        ),
    )(*pieces)


def polynomial_kernel(scale, halves, *refs):
    own_ref, other_ref = refs[:2]
    x_refs = refs[2 : 2 + halves]
    u_refs = refs[2 + halves : 2 + 2 * halves]
    norm_ref = refs[2 + 2 * halves]
    g, p, s, s_wide, g1, q = refs[3 + 2 * halves :]
    width = g.shape[0]
    steps = width // TILE

    total = jnp.zeros((), F32)
    for n in range(steps):
        sl = slice(n * TILE, (n + 1) * TILE)
        d = own_ref[sl, sl] + other_ref[sl, sl].astype(F32)
        r = lax.broadcasted_iota(jnp.int32, d.shape, 0)
        c = lax.broadcasted_iota(jnp.int32, d.shape, 1)
        total = total + jnp.sum(jnp.where(r == c, d, 0.0))
    norm = jnp.sqrt(jnp.full(norm_ref.shape, total, F32))
    norm_ref[...] = norm
    inv = 1.0 / (norm + EPS)
    inv = inv[:1, :1]

    @pl.loop(0, steps)
    def _(n):
        sl = columns(n)
        g[:, sl] = ((own_ref[:, sl] + other_ref[:, sl].astype(F32)) * (inv * inv)).astype(BF16)

    @pl.loop(0, steps)
    def _(n):
        sl = columns(n)
        col = g[:, sl]
        p[:, sl] = (COEF_B * col.astype(F32) + COEF_C * dot(g[...], col)).astype(BF16)

    @pl.loop(0, steps)
    def _(n):
        sl = columns(n)
        part = dot(g[...], p[:, sl])
        s[:, sl] = part.astype(BF16)
        s_wide[:, sl] = (2 * COEF_A) * part + (COEF_A * COEF_A) * g[:, sl].astype(F32)

    @pl.loop(0, steps)
    def _(n):
        sl = columns(n)
        g1[:, sl] = (s_wide[:, sl] + dot(p[...], s[:, sl])).astype(BF16)

    @pl.loop(0, steps)
    def _(n):
        sl = columns(n)
        col = g1[:, sl]
        q[:, sl] = (COEF_B * col.astype(F32) + COEF_C * dot(g1[...], col)).astype(BF16)

    for x_ref, u_ref in zip(x_refs, u_refs):
        x = x_ref[...]
        x1 = (inv * (COEF_A * x.astype(F32) + dot(x, p[...]))).astype(BF16)
        u_ref[...] = (scale * (COEF_A * x1.astype(F32) + dot(x1, q[...]))).astype(BF16)


def polynomial(own, other, xs, full_rows):
    width = own.shape[0]
    rows = sum(x.shape[0] for x in xs)
    mat = pltpu.VMEM((width, width), BF16)
    *updates, norm = pl.pallas_call(
        functools.partial(polynomial_kernel, math.sqrt(full_rows), len(xs)),
        out_shape=tuple(jax.ShapeDtypeStruct(x.shape, BF16) for x in xs)
        + (jax.ShapeDtypeStruct((8, 128), F32),),
        in_specs=[VMEM] * (2 + len(xs)),
        out_specs=(VMEM,) * (1 + len(xs)),
        scratch_shapes=[mat, mat, mat, pltpu.VMEM((width, width), F32), mat, mat],
        compiler_params=pltpu.CompilerParams(vmem_limit_bytes=32 * 2**20),
        cost_estimate=pl.CostEstimate(
            flops=8 * width**3 + 4 * rows * width * width,
            bytes_accessed=width * width * 6 + rows * width * 4,
            transcendentals=0,
        ),
    )(own, other, *xs)
    return updates, norm


def shift(value, axis, distance):
    n = lax.axis_size(axis)
    return lax.ppermute(value, axis, [(i, (i + distance) % n) for i in range(n)])


def on_device(grads, owners):
    block = grads[0]
    mats, rows_dev, width = block.shape
    dp_n = lax.axis_size("dp")
    y_n, z_n, core_n = lax.axis_size("y"), lax.axis_size("z"), lax.axis_size("core")
    mats_dp = mats // dp_n
    full_rows = y_n * z_n * core_n * rows_dev
    halves = 2
    part = rows_dev // halves

    own, pieces = [], []
    for h in range(halves):
        slabs = block[:, h * part : (h + 1) * part, :].reshape(dp_n, mats_dp, part, width)
        replicas = lax.all_to_all(slabs, "dp", 0, 0, tiled=True)
        summed = jnp.sum(replicas.astype(F32), axis=0).astype(BF16)
        mine = lax.all_to_all(summed, "z", 0, 0, tiled=True).reshape(z_n * part, width)
        own.append(mine)
        pieces += [mine] + [shift(mine, "y", k) for k in range(1, y_n)]

    gram_wide, gram_sent = gram(pieces)
    gram_other = shift(gram_sent, "core", 1)
    updates, norm = polynomial(gram_wide, gram_other, own, full_rows)

    lanes = 128
    tiles = width // lanes
    slab = jnp.stack([u.reshape(z_n, part, tiles, lanes) for u in updates], axis=1)
    slab = slab.transpose(0, 1, 3, 2, 4).reshape(z_n, rows_dev * tiles, lanes)
    high = norm.astype(BF16)
    low = (norm - high.astype(F32)).astype(BF16)
    note = jnp.concatenate([high[:4], low[:4]], axis=0)
    slab = jnp.concatenate([slab, jnp.broadcast_to(note, (z_n, 8, lanes))], axis=1)
    back = lax.all_to_all(slab, "z", 0, 0, tiled=True)
    out = back[:, : rows_dev * tiles].reshape(z_n, halves, tiles, part, lanes)
    out = out.transpose(0, 1, 3, 2, 4).reshape(z_n, rows_dev, width)
    norms = (back[:, rows_dev * tiles, 0].astype(F32) + back[:, rows_dev * tiles + 4, 0].astype(F32))

    index = (lax.axis_index("y") * z_n + lax.axis_index("z")) * core_n + lax.axis_index("core")
    mine = lax.dynamic_slice_in_dim(owners, lax.axis_index("dp") * mats_dp, mats_dp)
    hits = mine == index - index % core_n
    owner_rms = jnp.sum(jnp.where(hits, norms, 0.0)) / math.sqrt(full_rows * width)
    return out, owner_rms.reshape(1, 1)


def solution(mesh):
    dp_n, fsdp_n = mesh.devices.shape
    grid = Mesh(mesh.devices.reshape(dp_n, 4, fsdp_n // 8, 2), ("dp", "y", "z", "core"))
    fsdp = ("y", "z", "core")
    in_specs = (P("dp", None, fsdp, None), P())
    out_specs = (P("dp", fsdp, None), P("dp", fsdp))
    return jax.shard_map(
        on_device, mesh=grid, in_specs=in_specs, out_specs=out_specs, check_vma=False
    )
```

time: 420 us -> 151 us (0.36)
  the two profiles are of different devices: /device:TPU:1 before, /device:TPU:8 now
where the time goes in v1:
time: 151 us; the launch traced here: 150 us
  waiting for transfers between devices  62.5 us (41%)
  starting transfers between devices  52.6 us (35%)
  blocking collectives  16.4 us (11%)
  Pallas kernels  9.32 us (6%)
  other arithmetic  3.36 us (2%)
  local copies, waits for them, and re-layouts  3.18 us (2%)
  between operations  2.63 us (2%)
    all_to_all x1, waiting for transfers between devices, on_device(): back = lax.all_to_all(slab, 'z', 0, 0, tiled=True)  25.6 us
    ppermute x7, starting transfers between devices, shift(): lax.ppermute(value, axis, [(i, (i + distance) % n) for i in range(n)])  23.2 us
    all_to_all x2, waiting for transfers between devices, on_device(): lax.all_to_all(summed, 'z', 0, 0, tiled=True).reshape(z_n * part, width)  19.6 us
    all_to_all x2, starting transfers between devices, on_device(): lax.all_to_all(summed, 'z', 0, 0, tiled=True).reshape(z_n * part, width)  18.7 us
    all_to_all x1, blocking collectives, on_device(): replicas = lax.all_to_all(slabs, 'dp', 0, 0, tiled=True)  16.4 us
    all_to_all x1, waiting for transfers between devices, on_device(): replicas = lax.all_to_all(slabs, 'dp', 0, 0, tiled=True)  10.5 us
    pallas_call x1, Pallas kernels, polynomial(): pl.pallas_call(functools.partial(polynomial_kernel, math.sqrt(full_rows),...  7.35 us
    all_to_all x1, starting transfers between devices, on_device(): back = lax.all_to_all(slab, 'z', 0, 0, tiled=True)  7.16 us
  transfers between devices with their start and end apart: 11, of which 7 were waited for; matrix products, arithmetic and copies ran while one was open for 1% of the time, Pallas kernels for 0%

profile of v1, /device:TPU:8, one launch (start us, length us, event | category | flops | bytes accessed | tf_op | source)
XLA Modules:
  0.0 150.0 jit_solution(1396977238631211671)
XLA Ops:
  0.6 2.4 %fusion.3 = (bf16[64,8,768]{2,1,0:T(8,128)(2,1)}, bf16[64,8,768]{2,1,0:T(8,128)(2,1)S(1)}) fusion(bf16[64,16,768]{2,1,0:T(8,128)(2,1)} %bitcast.29), kind=kLoop, calls=%fused_computation.10 | loop fusion | bytes 3145728 | tf_op jit(solution)/shard_map/slice | solution.py:160
  3.0 16.4 %all_to_all.25 = bf16[4,16,8,768]{3,2,1,0:T(8,128)(2,1)S(1)} all-to-all(bf16[4,16,8,768]{3,2,1,0:T(8,128)(2,1)S(1)} %bitcast.28), channel_id=1, replica_groups=mesh['dp'=4,'y'=4,'z'=16,'core'=2] {'dp'}, dimensions={0} | all-to-all | bytes 1572864 | tf_op jit(solution)/shard_map/all_to_all | solution.py:161
  19.4 3.5 %all-to-all-start.2 = ((bf16[4,16,8,768]{3,2,1,0:T(8,128)(2,1)}), bf16[4,16,8,768]{3,2,1,0:T(8,128)(2,1)S(1)}, u32[]{:S(2)}, u32[]{:S(2)}) async-start(bf16[4,16,8,768]{3,2,1,0:T(8,128)(2,1)} %bitcast.3), calls=%async_computation.2 | async-start | bytes 1572864 | tf_op jit(solution)/shard_map/all_to_all | solution.py:161
  22.9 0.8 reduce_sum.33
  23.7 10.5 %all-to-all-done.2 = bf16[4,16,8,768]{3,2,1,0:T(8,128)(2,1)S(1)} async-done(((bf16[4,16,8,768]{3,2,1,0:T(8,128)(2,1)}), bf16[4,16,8,768]{3,2,1,0:T(8,128)(2,1)S(1)}, u32[]{:S(2)}, u32[]{:S(2)}) %all-to-all-start.2) | async-done | bytes 786464 | tf_op jit(solution)/shard_map/all_to_all | solution.py:161
  34.2 15.2 %all-to-all-start.1 = ((bf16[16,8,768]{2,1,0:T(8,128)(2,1)}), bf16[16,8,768]{2,1,0:T(8,128)(2,1)S(1)}, u32[]{:S(2)}, u32[]{:S(2)}) async-start(bf16[16,8,768]{2,1,0:T(8,128)(2,1)} %reduce_sum.33), calls=%async_computation.1 | async-start | bytes 393216 | tf_op jit(solution)/shard_map/all_to_all | solution.py:163
  49.4 0.8 reduce_sum.34
  50.2 14.6 %all-to-all-done.1 = bf16[16,8,768]{2,1,0:T(8,128)(2,1)S(1)} async-done(((bf16[16,8,768]{2,1,0:T(8,128)(2,1)}), bf16[16,8,768]{2,1,0:T(8,128)(2,1)S(1)}, u32[]{:S(2)}, u32[]{:S(2)}) %all-to-all-start.1) | async-done | bytes 196640 | tf_op jit(solution)/shard_map/all_to_all | solution.py:163
  64.8 3.5 %all-to-all-start.3 = ((bf16[16,8,768]{2,1,0:T(8,128)(2,1)}), bf16[16,8,768]{2,1,0:T(8,128)(2,1)S(1)}, u32[]{:S(2)}, u32[]{:S(2)}) async-start(bf16[16,8,768]{2,1,0:T(8,128)(2,1)} %reduce_sum.34), calls=%async_computation.3 | async-start | bytes 393216 | tf_op jit(solution)/shard_map/all_to_all | solution.py:163
  68.4 3.5 %collective-permute-start = (bf16[128,768]{1,0:T(8,128)(2,1)S(1)}, bf16[128,768]{1,0:T(8,128)(2,1)S(1)}, u32[]{:S(2)}, u32[]{:S(2)}) collective-permute-start(bf16[128,768]{1,0:T(8,128)(2,1)S(1)} %bitcast.16), channel_id=1, source_target_pairs={{0,32},{32,64},{64,96},{96,0},{1,33},{33,65},{65,97},{97,1},{2,34}... | collective-permute-start | bytes 589832 | tf_op jit(solution)/shard_map/ppermute | solution.py:145
  71.9 2.8 %collective-permute-start.1 = (bf16[128,768]{1,0:T(8,128)(2,1)S(1)}, bf16[128,768]{1,0:T(8,128)(2,1)S(1)}, u32[]{:S(2)}, u32[]{:S(2)}) collective-permute-start(bf16[128,768]{1,0:T(8,128)(2,1)S(1)} %bitcast.17), channel_id=1, source_target_pairs={{0,64},{32,96},{64,0},{96,32},{1,65},{33,97},{65,1},{97,33},{2,66}... | collective-permute-start | bytes 589832 | tf_op jit(solution)/shard_map/ppermute | solution.py:145
  74.7 4.3 %collective-permute-start.2 = (bf16[128,768]{1,0:T(8,128)(2,1)S(1)}, bf16[128,768]{1,0:T(8,128)(2,1)S(1)}, u32[]{:S(2)}, u32[]{:S(2)}) collective-permute-start(bf16[128,768]{1,0:T(8,128)(2,1)S(1)} %bitcast.18), channel_id=1, source_target_pairs={{0,96},{32,0},{64,32},{96,64},{1,97},{33,1},{65,33},{97,65},{2,98}... | collective-permute-start | bytes 589832 | tf_op jit(solution)/shard_map/ppermute | solution.py:145
  79.0 5.0 %all-to-all-done.3 = bf16[16,8,768]{2,1,0:T(8,128)(2,1)S(1)} async-done(((bf16[16,8,768]{2,1,0:T(8,128)(2,1)}), bf16[16,8,768]{2,1,0:T(8,128)(2,1)S(1)}, u32[]{:S(2)}, u32[]{:S(2)}) %all-to-all-start.3) | async-done | bytes 196640 | tf_op jit(solution)/shard_map/all_to_all | solution.py:163
  84.1 3.5 %collective-permute-start.3 = (bf16[128,768]{1,0:T(8,128)(2,1)S(1)}, bf16[128,768]{1,0:T(8,128)(2,1)S(1)}, u32[]{:S(2)}, u32[]{:S(2)}) collective-permute-start(bf16[128,768]{1,0:T(8,128)(2,1)S(1)} %bitcast.21), channel_id=1, source_target_pairs={{0,32},{32,64},{64,96},{96,0},{1,33},{33,65},{65,97},{97,1},{2,34}... | collective-permute-start | bytes 589832 | tf_op jit(solution)/shard_map/ppermute | solution.py:145
  87.5 2.8 %collective-permute-start.4 = (bf16[128,768]{1,0:T(8,128)(2,1)S(1)}, bf16[128,768]{1,0:T(8,128)(2,1)S(1)}, u32[]{:S(2)}, u32[]{:S(2)}) collective-permute-start(bf16[128,768]{1,0:T(8,128)(2,1)S(1)} %bitcast.22), channel_id=1, source_target_pairs={{0,64},{32,96},{64,0},{96,32},{1,65},{33,97},{65,1},{97,33},{2,66}... | collective-permute-start | bytes 589832 | tf_op jit(solution)/shard_map/ppermute | solution.py:145
  90.4 0.0 collective-permute-done.refs_1_
  90.4 4.3 %collective-permute-start.5 = (bf16[128,768]{1,0:T(8,128)(2,1)S(1)}, bf16[128,768]{1,0:T(8,128)(2,1)S(1)}, u32[]{:S(2)}, u32[]{:S(2)}) collective-permute-start(bf16[128,768]{1,0:T(8,128)(2,1)S(1)} %bitcast.23), channel_id=1, source_target_pairs={{0,96},{32,0},{64,32},{96,64},{1,97},{33,1},{65,33},{97,65},{2,98}... | collective-permute-start | bytes 589832 | tf_op jit(solution)/shard_map/ppermute | solution.py:145
  94.7 0.0 collective-permute-done.2.refs_3_
  94.7 0.0 collective-permute-done.3.refs_5_
  94.8 1.9 %collective-permute-done.4.refs_6_ = bf16[128,768]{1,0:T(8,128)(2,1)S(1)} collective-permute-done((bf16[128,768]{1,0:T(8,128)(2,1)S(1)}, bf16[128,768]{1,0:T(8,128)(2,1)S(1)}, u32[]{:S(2)}, u32[]{:S(2)}) %collective-permute-start.4) | collective-permute-done | bytes 196640 | tf_op jit(solution)/shard_map/ppermute | solution.py:145
  96.7 2.0 %collective-permute-done.5.refs_7_ = bf16[128,768]{1,0:T(8,128)(2,1)S(1)} collective-permute-done((bf16[128,768]{1,0:T(8,128)(2,1)S(1)}, bf16[128,768]{1,0:T(8,128)(2,1)S(1)}, u32[]{:S(2)}, u32[]{:S(2)}) %collective-permute-start.5) | collective-permute-done | bytes 196640 | tf_op jit(solution)/shard_map/ppermute | solution.py:145
  98.7 2.0 %shard_map.41 = (f32[768,768]{1,0:T(8,128)S(1)}, bf16[768,768]{1,0:T(8,128)(2,1)S(1)}) custom-call(bf16[128,768]{1,0:T(8,128)(2,1)S(1)} %bitcast.19, bf16[128,768]{1,0:T(8,128)(2,1)S(1)} %collective-permute-done.refs_1_, bf16[128,768]{1,0:T(8,128)(2,1)S(1)} %collective-permute-done.1.refs_2_, bf16[128,768]{1,0:T(8,128)(2,1)S(1)} %collective-permute-done.2.refs_3_, ...), custom_call_target="tpu_custom_call" | custom-call | flops 1207959552 | bytes 5111808 | tf_op jit(solution)/shard_map/pallas_call | solution.py:48
  100.7 1.9 %collective-permute-start.6 = (bf16[768,768]{1,0:T(8,128)(2,1)S(1)}, bf16[768,768]{1,0:T(8,128)(2,1)S(1)}, u32[]{:S(2)}, u32[]{:S(2)}) collective-permute-start(bf16[768,768]{1,0:T(8,128)(2,1)S(1)} %get-tuple-element.8), channel_id=1, source_target_pairs={{0,1},{1,0},{2,3},{3,2},{4,5},{5,4},{6,7},{7,6},{8,9},{9,8},{10,11... | collective-permute-start | bytes 3538952 | tf_op jit(solution)/shard_map/ppermute | solution.py:145
  102.6 2.8 %collective-permute-done.6.refs_1_ = bf16[768,768]{1,0:T(8,128)(2,1)S(1)} collective-permute-done((bf16[768,768]{1,0:T(8,128)(2,1)S(1)}, bf16[768,768]{1,0:T(8,128)(2,1)S(1)}, u32[]{:S(2)}, u32[]{:S(2)}) %collective-permute-start.6) | collective-permute-done | bytes 1179680 | tf_op jit(solution)/shard_map/ppermute | solution.py:145
  105.4 7.4 %shard_map.42 = (bf16[128,768]{1,0:T(8,128)(2,1)S(1)}, bf16[128,768]{1,0:T(8,128)(2,1)S(1)}, f32[8,128]{1,0:T(8,128)S(1)}) custom-call(f32[768,768]{1,0:T(8,128)S(1)} %get-tuple-element.7.refs_0_, bf16[768,768]{1,0:T(8,128)(2,1)S(1)} %collective-permute-done.6.refs_1_, bf16[128,768]{1,0:T(8,128)(2,1)S(1)} %bitcast.20, bf16[128,768]{1,0:T(8,128)(2,1)S(1)} %bitcast.25), custom_call_target="tpu_custom_call" | custom-call | flops 4227858432 | bytes 4325376 | tf_op jit(solution)/shard_map/pallas_call | solution.py:126
  112.8 0.0 copy-start
  112.9 0.8 pad_maximum_fusion
  113.7 7.2 %all-to-all-start.4 = ((bf16[16,104,128]{2,1,0:T(8,128)(2,1)}), bf16[16,104,128]{2,1,0:T(8,128)(2,1)S(1)}, u32[]{:S(2)}, u32[]{:S(2)}) async-start(bf16[16,104,128]{2,1,0:T(8,128)(2,1)} %pad_maximum_fusion), calls=%async_computation.4 | async-start | bytes 851968 | tf_op jit(solution)/shard_map/all_to_all | solution.py:179
  120.9 25.6 %all-to-all-done.4 = bf16[16,104,128]{2,1,0:T(8,128)(2,1)S(1)} async-done(((bf16[16,104,128]{2,1,0:T(8,128)(2,1)}), bf16[16,104,128]{2,1,0:T(8,128)(2,1)S(1)}, u32[]{:S(2)}, u32[]{:S(2)}) %all-to-all-start.4) | async-done | bytes 426016 | tf_op jit(solution)/shard_map/all_to_all | solution.py:179
  146.6 0.2 fusion.1
  146.8 0.7 fusion.2
  148.1 0.8 slice.30
  (9 shorter events, 0.1 us)
Async XLA Ops:
  19.4 14.8 %all-to-all-start.2 = ((bf16[4,16,8,768]{3,2,1,0:T(8,128)(2,1)}), bf16[4,16,8,768]{3,2,1,0:T(8,128)(2,1)S(1)}, u32[]{:S(2)}, u32[]{:S(2)}) async-start(bf16[4,16,8,768]{3,2,1,0:T(8,128)(2,1)} %bitcast.3), calls=%async_computation.2 | async-start | bytes 1572864 | tf_op jit(solution)/shard_map/all_to_all | solution.py:161
  34.2 30.6 %all-to-all-start.1 = ((bf16[16,8,768]{2,1,0:T(8,128)(2,1)}), bf16[16,8,768]{2,1,0:T(8,128)(2,1)S(1)}, u32[]{:S(2)}, u32[]{:S(2)}) async-start(bf16[16,8,768]{2,1,0:T(8,128)(2,1)} %reduce_sum.33), calls=%async_computation.1 | async-start | bytes 393216 | tf_op jit(solution)/shard_map/all_to_all | solution.py:163
  64.8 19.2 %all-to-all-start.3 = ((bf16[16,8,768]{2,1,0:T(8,128)(2,1)}), bf16[16,8,768]{2,1,0:T(8,128)(2,1)S(1)}, u32[]{:S(2)}, u32[]{:S(2)}) async-start(bf16[16,8,768]{2,1,0:T(8,128)(2,1)} %reduce_sum.34), calls=%async_computation.3 | async-start | bytes 393216 | tf_op jit(solution)/shard_map/all_to_all | solution.py:163
  68.4 22.0 %collective-permute-start = (bf16[128,768]{1,0:T(8,128)(2,1)S(1)}, bf16[128,768]{1,0:T(8,128)(2,1)S(1)}, u32[]{:S(2)}, u32[]{:S(2)}) collective-permute-start(bf16[128,768]{1,0:T(8,128)(2,1)S(1)} %bitcast.16), channel_id=1, source_target_pairs={{0,32},{32,64},{64,96},{96,0},{1,33},{33,65},{65,97},{97,1},{2,34}... | collective-permute-start | bytes 589832 | tf_op jit(solution)/shard_map/ppermute | solution.py:145
  71.9 22.9 %collective-permute-start.1 = (bf16[128,768]{1,0:T(8,128)(2,1)S(1)}, bf16[128,768]{1,0:T(8,128)(2,1)S(1)}, u32[]{:S(2)}, u32[]{:S(2)}) collective-permute-start(bf16[128,768]{1,0:T(8,128)(2,1)S(1)} %bitcast.17), channel_id=1, source_target_pairs={{0,64},{32,96},{64,0},{96,32},{1,65},{33,97},{65,1},{97,33},{2,66}... | collective-permute-start | bytes 589832 | tf_op jit(solution)/shard_map/ppermute | solution.py:145
  74.7 20.0 %collective-permute-start.2 = (bf16[128,768]{1,0:T(8,128)(2,1)S(1)}, bf16[128,768]{1,0:T(8,128)(2,1)S(1)}, u32[]{:S(2)}, u32[]{:S(2)}) collective-permute-start(bf16[128,768]{1,0:T(8,128)(2,1)S(1)} %bitcast.18), channel_id=1, source_target_pairs={{0,96},{32,0},{64,32},{96,64},{1,97},{33,1},{65,33},{97,65},{2,98}... | collective-permute-start | bytes 589832 | tf_op jit(solution)/shard_map/ppermute | solution.py:145
  84.1 10.7 %collective-permute-start.3 = (bf16[128,768]{1,0:T(8,128)(2,1)S(1)}, bf16[128,768]{1,0:T(8,128)(2,1)S(1)}, u32[]{:S(2)}, u32[]{:S(2)}) collective-permute-start(bf16[128,768]{1,0:T(8,128)(2,1)S(1)} %bitcast.21), channel_id=1, source_target_pairs={{0,32},{32,64},{64,96},{96,0},{1,33},{33,65},{65,97},{97,1},{2,34}... | collective-permute-start | bytes 589832 | tf_op jit(solution)/shard_map/ppermute | solution.py:145
  87.5 9.1 %collective-permute-start.4 = (bf16[128,768]{1,0:T(8,128)(2,1)S(1)}, bf16[128,768]{1,0:T(8,128)(2,1)S(1)}, u32[]{:S(2)}, u32[]{:S(2)}) collective-permute-start(bf16[128,768]{1,0:T(8,128)(2,1)S(1)} %bitcast.22), channel_id=1, source_target_pairs={{0,64},{32,96},{64,0},{96,32},{1,65},{33,97},{65,1},{97,33},{2,66}... | collective-permute-start | bytes 589832 | tf_op jit(solution)/shard_map/ppermute | solution.py:145
  90.4 8.3 %collective-permute-start.5 = (bf16[128,768]{1,0:T(8,128)(2,1)S(1)}, bf16[128,768]{1,0:T(8,128)(2,1)S(1)}, u32[]{:S(2)}, u32[]{:S(2)}) collective-permute-start(bf16[128,768]{1,0:T(8,128)(2,1)S(1)} %bitcast.23), channel_id=1, source_target_pairs={{0,96},{32,0},{64,32},{96,64},{1,97},{33,1},{65,33},{97,65},{2,98}... | collective-permute-start | bytes 589832 | tf_op jit(solution)/shard_map/ppermute | solution.py:145
  100.7 4.7 %collective-permute-start.6 = (bf16[768,768]{1,0:T(8,128)(2,1)S(1)}, bf16[768,768]{1,0:T(8,128)(2,1)S(1)}, u32[]{:S(2)}, u32[]{:S(2)}) collective-permute-start(bf16[768,768]{1,0:T(8,128)(2,1)S(1)} %get-tuple-element.8), channel_id=1, source_target_pairs={{0,1},{1,0},{2,3},{3,2},{4,5},{5,4},{6,7},{7,6},{8,9},{9,8},{10,11... | collective-permute-start | bytes 3538952 | tf_op jit(solution)/shard_map/ppermute | solution.py:145
  112.8 33.9 %copy-start = (s32[64]{0:T(128)S(1)}, s32[64]{0:T(128)}, u32[]{:S(2)}) copy-start(s32[64]{0:T(128)} %param.3) | copy-start | bytes 772
  113.7 32.8 %all-to-all-start.4 = ((bf16[16,104,128]{2,1,0:T(8,128)(2,1)}), bf16[16,104,128]{2,1,0:T(8,128)(2,1)S(1)}, u32[]{:S(2)}, u32[]{:S(2)}) async-start(bf16[16,104,128]{2,1,0:T(8,128)(2,1)} %pad_maximum_fusion), calls=%async_computation.4 | async-start | bytes 851968 | tf_op jit(solution)/shard_map/all_to_all | solution.py:179

commit v2 on v1

v2 whole, which is shorter than its diff:
```python
import functools
import math

import jax
import jax.numpy as jnp
from jax import lax
from jax.experimental import pallas as pl
from jax.experimental.pallas import tpu as pltpu
from jax.sharding import Mesh
from jax.sharding import PartitionSpec as P

COEF_A = 3.4445
COEF_B = -4.775
COEF_C = 2.0315
EPS = 1e-07

BF16 = jnp.bfloat16
F32 = jnp.float32
VMEM = pl.BlockSpec(memory_space=pltpu.VMEM)
SMEM = pl.BlockSpec(memory_space=pltpu.SMEM)
TILE = 256
LANES = 128
NOTE = 8


def dot(a, b):
    return jnp.dot(a, b, preferred_element_type=F32)


def gram_of(a, b):
    return lax.dot_general(a, b, (((0,), (0,)), ((), ())), preferred_element_type=F32)


def lower(width):
    return [(slice(j, width), slice(j, j + TILE)) for j in range(0, width, TILE)]


def store_symmetric(ref, rows, cols, value):
    ref[rows, cols] = value
    if cols.stop < rows.stop:
        ref[cols, cols.stop : rows.stop] = value[TILE:].T


def gram_kernel(*refs):
    *pieces, total_ref, stack = refs
    rows = pieces[0].shape[0]
    for i, piece in enumerate(pieces):
        stack[i * rows : (i + 1) * rows, :] = piece[...]
    for down, cols in lower(total_ref.shape[0]):
        total_ref[down, cols] = gram_of(stack[:, down], stack[:, cols])


def gram(pieces):
    rows, width = pieces[0].shape
    return pl.pallas_call(
        gram_kernel,
        out_shape=jax.ShapeDtypeStruct((width, width), F32),
        in_specs=[VMEM] * len(pieces),
        out_specs=VMEM,
        scratch_shapes=[pltpu.VMEM((rows * len(pieces), width), BF16)],
        compiler_params=pltpu.CompilerParams(vmem_limit_bytes=32 * 2**20),
        cost_estimate=pl.CostEstimate(
            flops=2 * rows * len(pieces) * width * width,
            bytes_accessed=rows * len(pieces) * width * 2 + width * width * 4,
            transcendentals=0,
        ),
    )(*pieces)


def polynomial_kernel(scale, count, *refs):
    total_ref, x_ref = refs[:2]
    pieces = refs[2 : 2 + count]
    slab_ref = refs[2 + count]
    stack, wide, g, p, s = refs[3 + count :]
    width = g.shape[0]
    rows = pieces[0].shape[0]

    for i, piece in enumerate(pieces):
        stack[i * rows : (i + 1) * rows, :] = piece[...]
    trace = jnp.zeros((1, 1), F32)
    for down, cols in lower(width):
        part = total_ref[down, cols] + gram_of(stack[:, down], stack[:, cols])
        wide[down, cols] = part
        d = part[:TILE]
        r = lax.broadcasted_iota(jnp.int32, d.shape, 0)
        c = lax.broadcasted_iota(jnp.int32, d.shape, 1)
        trace = trace + jnp.sum(jnp.where(r == c, d, 0.0), keepdims=True)
    norm = jnp.sqrt(trace)
    inv = 1.0 / (norm + EPS)

    for down, cols in lower(width):
        store_symmetric(g, down, cols, (wide[down, cols] * (inv * inv)).astype(BF16))
    for down, cols in lower(width):
        part = COEF_B * g[down, cols].astype(F32) + COEF_C * dot(g[down, :], g[:, cols])
        store_symmetric(p, down, cols, part.astype(BF16))
    for down, cols in lower(width):
        part = dot(g[down, :], p[:, cols])
        wide[down, cols] = (2 * COEF_A) * part + (COEF_A * COEF_A) * g[down, cols].astype(F32)
        store_symmetric(s, down, cols, part.astype(BF16))
    for down, cols in lower(width):
        part = wide[down, cols] + dot(p[down, :], s[:, cols])
        store_symmetric(g, down, cols, part.astype(BF16))
    for down, cols in lower(width):
        part = COEF_B * g[down, cols].astype(F32) + COEF_C * dot(g[down, :], g[:, cols])
        store_symmetric(s, down, cols, part.astype(BF16))

    x = x_ref[...]
    x1 = (inv * (COEF_A * x.astype(F32) + dot(x, p[...]))).astype(BF16)
    update = (scale * (COEF_A * x1.astype(F32) + dot(x1, s[...]))).astype(BF16)
    blocks, high, _ = slab_ref.shape
    tall = update.shape[0] // blocks
    for i in range(width // LANES):
        slab_ref[:, i * tall : (i + 1) * tall, :] = update[:, i * LANES : (i + 1) * LANES].reshape(
            blocks, tall, LANES
        )
    first = norm.astype(BF16).astype(F32)
    second = norm - first
    note = lax.broadcasted_iota(jnp.int32, (NOTE, LANES), 0)
    note = jnp.where(note < NOTE // 2, first, second).astype(BF16)
    slab_ref[:, high - NOTE :, :] = jnp.broadcast_to(note, (blocks, NOTE, LANES))


def polynomial(total, x, pieces, full_rows, blocks):
    width = total.shape[0]
    rows = x.shape[0]
    mat = pltpu.VMEM((width, width), BF16)
    high = rows // blocks * width // LANES + NOTE
    return pl.pallas_call(
        functools.partial(polynomial_kernel, math.sqrt(full_rows), len(pieces)),
        out_shape=jax.ShapeDtypeStruct((blocks, high, LANES), BF16),
        in_specs=[VMEM] * (2 + len(pieces)),
        out_specs=VMEM,
        scratch_shapes=[
            pltpu.VMEM((len(pieces) * pieces[0].shape[0], width), BF16),
            pltpu.VMEM((width, width), F32),
            mat,
            mat,
            mat,
        ],
        compiler_params=pltpu.CompilerParams(vmem_limit_bytes=32 * 2**20),
        cost_estimate=pl.CostEstimate(
            flops=6 * width**3 + 6 * rows * width * width,
            bytes_accessed=width * width * 4 + rows * width * 8,
            transcendentals=0,
        ),
    )(total, x, *pieces)


def place_kernel(count, back_ref, hit_ref, out_ref, rms_ref):
    blocks, tall, width = out_ref.shape
    for i in range(width // LANES):
        out_ref[:, :, i * LANES : (i + 1) * LANES] = back_ref[:, i * tall : (i + 1) * tall, :]
    note = back_ref[:, back_ref.shape[1] - NOTE :, :].astype(F32)
    norms = note[:, :1, :1] + note[:, NOTE // 2 : NOTE // 2 + 1, :1]
    rms_ref[0, 0] = jnp.sum(jnp.where(hit_ref[...] > 0, norms, 0.0)) / math.sqrt(count)


def place(back, hits, tall, width, full_rows):
    blocks = back.shape[0]
    return pl.pallas_call(
        functools.partial(place_kernel, full_rows * width),
        out_shape=(
            jax.ShapeDtypeStruct((blocks, tall, width), BF16),
            jax.ShapeDtypeStruct((1, 1), F32),
        ),
        in_specs=[VMEM, VMEM],
        out_specs=(VMEM, SMEM),
    )(back, hits.astype(jnp.int32).reshape(blocks, 1, 1))


def shift(value, axis, distance):
    n = lax.axis_size(axis)
    return lax.ppermute(value, axis, [(i, (i + distance) % n) for i in range(n)])


def on_device(grads, owners):
    block = grads[0]
    mats, rows_dev, width = block.shape
    dp_n = lax.axis_size("dp")
    y_n, z_n, core_n = lax.axis_size("y"), lax.axis_size("z"), lax.axis_size("core")
    mats_dp = mats // dp_n
    full_rows = y_n * z_n * core_n * rows_dev

    slabs = block.reshape(dp_n, mats_dp, rows_dev, width)
    replicas = lax.all_to_all(slabs, "dp", 0, 0, tiled=True)
    summed = jnp.sum(replicas.astype(F32), axis=0).astype(BF16)
    mine = lax.all_to_all(summed, "z", 0, 0, tiled=True).reshape(z_n * rows_dev, width)

    far = shift(mine, "y", 2)
    near = [mine, shift(mine, "y", 1), shift(mine, "y", 3)]
    near += [shift(piece, "core", 1) for piece in near]
    far = [far, shift(far, "core", 1)]
    slab = polynomial(gram(near), mine, far, full_rows, z_n)
    back = lax.all_to_all(slab, "z", 0, 0, tiled=True)

    index = (lax.axis_index("y") * z_n + lax.axis_index("z")) * core_n + lax.axis_index("core")
    owned = lax.dynamic_slice_in_dim(owners, lax.axis_index("dp") * mats_dp, mats_dp)
    hits = owned == index - index % core_n
    return place(back, hits, rows_dev, width, full_rows)


def solution(mesh):
    dp_n, fsdp_n = mesh.devices.shape
    grid = Mesh(mesh.devices.reshape(dp_n, 4, fsdp_n // 8, 2), ("dp", "y", "z", "core"))
    fsdp = ("y", "z", "core")
    in_specs = (P("dp", None, fsdp, None), P())
    out_specs = (P("dp", fsdp, None), P("dp", fsdp))
    return jax.shard_map(
        on_device, mesh=grid, in_specs=in_specs, out_specs=out_specs, check_vma=False
    )
```

time: 151 us -> 133 us (0.88)
  the two profiles are of different devices: /device:TPU:8 before, /device:TPU:24 now
where the time goes in v2:
time: 133 us; the launch traced here: 132 us
  blocking collectives  62.4 us (47%)
  waiting for transfers between devices  30.4 us (23%)
  starting transfers between devices  28.6 us (22%)
  Pallas kernels  8.4 us (6%)
  local copies, waits for them, and re-layouts  1.44 us (1%)
    all_to_all x1, blocking collectives, on_device(): lax.all_to_all(summed, 'z', 0, 0, tiled=True).reshape(z_n * rows_dev, width)  37.4 us
    all_to_all x1, waiting for transfers between devices, on_device(): back = lax.all_to_all(slab, 'z', 0, 0, tiled=True)  25.1 us
    all_to_all x1, blocking collectives, on_device(): replicas = lax.all_to_all(slabs, 'dp', 0, 0, tiled=True)  25 us
    ppermute x7, starting transfers between devices, shift(): lax.ppermute(value, axis, [(i, (i + distance) % n) for i in range(n)])  17.1 us
    all_to_all x1, starting transfers between devices, on_device(): back = lax.all_to_all(slab, 'z', 0, 0, tiled=True)  11.5 us
    ppermute x7, waiting for transfers between devices, shift(): lax.ppermute(value, axis, [(i, (i + distance) % n) for i in range(n)])  5.35 us
    pallas_call x1, Pallas kernels, polynomial(): pl.pallas_call(functools.partial(polynomial_kernel, math.sqrt(full_rows),...  5.13 us
  transfers between devices with their start and end apart: 8, of which 3 were waited for; matrix products, arithmetic and copies ran while one was open for 1% of the time, Pallas kernels for 1%

profile of v2, /device:TPU:24, one launch (start us, length us, event | category | flops | bytes accessed | tf_op | source)
XLA Modules:
  0.0 132.5 jit_solution(11230152658885280790)
XLA Ops:
  0.6 25.0 %all_to_all.15 = bf16[4,16,16,768]{3,2,1,0:T(8,128)(2,1)S(1)} all-to-all(bf16[4,16,16,768]{3,2,1,0:T(8,128)(2,1)} %bitcast.10), channel_id=1, replica_groups=mesh['dp'=4,'y'=4,'z'=16,'core'=2] {'dp'}, dimensions={0} | all-to-all | bytes 3145728 | tf_op jit(solution)/shard_map/all_to_all | solution.py:185
  25.6 0.4 reduce_sum.12
  26.0 37.4 %all_to_all.16 = bf16[16,16,768]{2,1,0:T(8,128)(2,1)S(1)} all-to-all(bf16[16,16,768]{2,1,0:T(8,128)(2,1)S(1)} %reduce_sum.12), channel_id=1, replica_groups=mesh['dp'=4,'y'=4,'z'=16,'core'=2] {'z'}, dimensions={0} | all-to-all | bytes 786432 | tf_op jit(solution)/shard_map/all_to_all | solution.py:187
  63.4 2.1 %collective-permute-start = (bf16[256,768]{1,0:T(8,128)(2,1)S(1)}, bf16[256,768]{1,0:T(8,128)(2,1)S(1)}, u32[]{:S(2)}, u32[]{:S(2)}) collective-permute-start(bf16[256,768]{1,0:T(8,128)(2,1)S(1)} %bitcast.4), channel_id=1, source_target_pairs={{0,32},{32,64},{64,96},{96,0},{1,33},{33,65},{65,97},{97,1},{2,34}... | collective-permute-start | bytes 1179656 | tf_op jit(solution)/shard_map/ppermute | solution.py:173
  65.5 3.7 %collective-permute-start.1 = (bf16[256,768]{1,0:T(8,128)(2,1)S(1)}, bf16[256,768]{1,0:T(8,128)(2,1)S(1)}, u32[]{:S(2)}, u32[]{:S(2)}) collective-permute-start(bf16[256,768]{1,0:T(8,128)(2,1)S(1)} %bitcast.5), channel_id=1, source_target_pairs={{0,96},{32,0},{64,32},{96,64},{1,97},{33,1},{65,33},{97,65},{2,98}... | collective-permute-start | bytes 1179656 | tf_op jit(solution)/shard_map/ppermute | solution.py:173
  69.2 3.1 %collective-permute-start.5 = (bf16[256,768]{1,0:T(8,128)(2,1)S(1)}, bf16[256,768]{1,0:T(8,128)(2,1)S(1)}, u32[]{:S(2)}, u32[]{:S(2)}) collective-permute-start(bf16[256,768]{1,0:T(8,128)(2,1)S(1)} %bitcast.6), channel_id=1, source_target_pairs={{0,64},{32,96},{64,0},{96,32},{1,65},{33,97},{65,1},{97,33},{2,66}... | collective-permute-start | bytes 1179656 | tf_op jit(solution)/shard_map/ppermute | solution.py:173
  72.4 1.9 %collective-permute-start.2 = (bf16[256,768]{1,0:T(8,128)(2,1)S(1)}, bf16[256,768]{1,0:T(8,128)(2,1)S(1)}, u32[]{:S(2)}, u32[]{:S(2)}) collective-permute-start(bf16[256,768]{1,0:T(8,128)(2,1)S(1)} %bitcast.7), channel_id=1, source_target_pairs={{0,1},{1,0},{2,3},{3,2},{4,5},{5,4},{6,7},{7,6},{8,9},{9,8},{10,11... | collective-permute-start | bytes 1179656 | tf_op jit(solution)/shard_map/ppermute | solution.py:173
  74.3 1.3 collective-permute-done.refs_1_
  75.6 1.9 %collective-permute-start.3 = (bf16[256,768]{1,0:T(8,128)(2,1)S(1)}, bf16[256,768]{1,0:T(8,128)(2,1)S(1)}, u32[]{:S(2)}, u32[]{:S(2)}) collective-permute-start(bf16[256,768]{1,0:T(8,128)(2,1)S(1)} %collective-permute-done.refs_1_), channel_id=1, source_target_pairs={{0,1},{1,0},{2,3},{3,2},{4,5},{5,4},{6,7},{7,6},{8,9},{9,8},{10,11... | collective-permute-start | bytes 1179656 | tf_op jit(solution)/shard_map/ppermute | solution.py:173
  77.6 4.0 %collective-permute-done.1.refs_2_ = bf16[256,768]{1,0:T(8,128)(2,1)S(1)} collective-permute-done((bf16[256,768]{1,0:T(8,128)(2,1)S(1)}, bf16[256,768]{1,0:T(8,128)(2,1)S(1)}, u32[]{:S(2)}, u32[]{:S(2)}) %collective-permute-start.1) | collective-permute-done | bytes 393248 | tf_op jit(solution)/shard_map/ppermute | solution.py:173
  81.6 1.9 %collective-permute-start.4 = (bf16[256,768]{1,0:T(8,128)(2,1)S(1)}, bf16[256,768]{1,0:T(8,128)(2,1)S(1)}, u32[]{:S(2)}, u32[]{:S(2)}) collective-permute-start(bf16[256,768]{1,0:T(8,128)(2,1)S(1)} %collective-permute-done.1.refs_2_), channel_id=1, source_target_pairs={{0,1},{1,0},{2,3},{3,2},{4,5},{5,4},{6,7},{7,6},{8,9},{9,8},{10,11... | collective-permute-start | bytes 1179656 | tf_op jit(solution)/shard_map/ppermute | solution.py:173
  83.5 0.0 collective-permute-done.5.refs_2_
  83.5 2.4 %collective-permute-start.6 = (bf16[256,768]{1,0:T(8,128)(2,1)S(1)}, bf16[256,768]{1,0:T(8,128)(2,1)S(1)}, u32[]{:S(2)}, u32[]{:S(2)}) collective-permute-start(bf16[256,768]{1,0:T(8,128)(2,1)S(1)} %collective-permute-done.5.refs_2_), channel_id=1, source_target_pairs={{0,1},{1,0},{2,3},{3,2},{4,5},{5,4},{6,7},{7,6},{8,9},{9,8},{10,11... | collective-permute-start | bytes 1179656 | tf_op jit(solution)/shard_map/ppermute | solution.py:173
  85.9 0.0 collective-permute-done.2.refs_3_
  85.9 0.0 collective-permute-done.3.refs_4_
  85.9 0.0 collective-permute-done.4.refs_5_
  86.0 1.4 %shard_map.41.refs_0_ = f32[768,768]{1,0:T(8,128)S(1)} custom-call(bf16[256,768]{1,0:T(8,128)(2,1)S(1)} %bitcast.8, bf16[256,768]{1,0:T(8,128)(2,1)S(1)} %collective-permute-done.refs_1_, bf16[256,768]{1,0:T(8,128)(2,1)S(1)} %collective-permute-done.1.refs_2_, bf16[256,768]{1,0:T(8,128)(2,1)S(1)} %collective-permute-done.2.refs_3_, ...), custom_call_target="tpu_custom_call" | custom-call | flops 1811939328 | bytes 4718592 | tf_op jit(solution)/shard_map/pallas_call | solution.py:55
  87.4 0.0 copy-start.1
  87.4 0.0 collective-permute-done.6.refs_3_
  87.4 5.1 %shard_map.42 = bf16[16,104,128]{2,1,0:T(8,128)(2,1)} custom-call(f32[768,768]{1,0:T(8,128)S(1)} %shard_map.41.refs_0_, bf16[256,768]{1,0:T(8,128)(2,1)S(1)} %bitcast.9, bf16[256,768]{1,0:T(8,128)(2,1)S(1)} %collective-permute-done.5.refs_2_, bf16[256,768]{1,0:T(8,128)(2,1)S(1)} %collective-permute-done.6.refs_3_), custom_call_target="tpu_custom_call" | custom-call | flops 3623878656 | bytes 3932160 | tf_op jit(solution)/shard_map/pallas_call | solution.py:128
  92.5 11.5 %all-to-all-start.2 = ((bf16[16,104,128]{2,1,0:T(8,128)(2,1)}), bf16[16,104,128]{2,1,0:T(8,128)(2,1)S(1)}, u32[]{:S(2)}, u32[]{:S(2)}) async-start(bf16[16,104,128]{2,1,0:T(8,128)(2,1)} %shard_map.42), calls=%async_computation.2 | async-start | bytes 851968 | tf_op jit(solution)/shard_map/all_to_all | solution.py:194
  104.1 0.0 copy-done.1
  104.1 0.1 fusion
  104.2 0.7 copy.4.hit_ref
  104.8 25.1 %all-to-all-done.2.back_ref = bf16[16,104,128]{2,1,0:T(8,128)(2,1)S(1)} async-done(((bf16[16,104,128]{2,1,0:T(8,128)(2,1)}), bf16[16,104,128]{2,1,0:T(8,128)(2,1)S(1)}, u32[]{:S(2)}, u32[]{:S(2)}) %all-to-all-start.2) | async-done | bytes 426016 | tf_op jit(solution)/shard_map/all_to_all | solution.py:194
  129.9 0.0 copy-start
  129.9 0.8 copy-done
  130.7 1.8 %shard_map.43 = (bf16[16,16,768]{2,1,0:T(8,128)(2,1)}, f32[1,1]{1,0:T(1,128)}) custom-call(bf16[16,104,128]{2,1,0:T(8,128)(2,1)} %copy-done, s32[16,1,1]{2,1,0:T(1,128)} %copy.4.hit_ref), custom_call_target="tpu_custom_call" | custom-call | tf_op jit(solution)/shard_map/pallas_call | solution.py:160
Async XLA Ops:
  63.4 12.3 %collective-permute-start = (bf16[256,768]{1,0:T(8,128)(2,1)S(1)}, bf16[256,768]{1,0:T(8,128)(2,1)S(1)}, u32[]{:S(2)}, u32[]{:S(2)}) collective-permute-start(bf16[256,768]{1,0:T(8,128)(2,1)S(1)} %bitcast.4), channel_id=1, source_target_pairs={{0,32},{32,64},{64,96},{96,0},{1,33},{33,65},{65,97},{97,1},{2,34}... | collective-permute-start | bytes 1179656 | tf_op jit(solution)/shard_map/ppermute | solution.py:173
  65.5 16.1 %collective-permute-start.1 = (bf16[256,768]{1,0:T(8,128)(2,1)S(1)}, bf16[256,768]{1,0:T(8,128)(2,1)S(1)}, u32[]{:S(2)}, u32[]{:S(2)}) collective-permute-start(bf16[256,768]{1,0:T(8,128)(2,1)S(1)} %bitcast.5), channel_id=1, source_target_pairs={{0,96},{32,0},{64,32},{96,64},{1,97},{33,1},{65,33},{97,65},{2,98}... | collective-permute-start | bytes 1179656 | tf_op jit(solution)/shard_map/ppermute | solution.py:173
  69.2 14.3 %collective-permute-start.5 = (bf16[256,768]{1,0:T(8,128)(2,1)S(1)}, bf16[256,768]{1,0:T(8,128)(2,1)S(1)}, u32[]{:S(2)}, u32[]{:S(2)}) collective-permute-start(bf16[256,768]{1,0:T(8,128)(2,1)S(1)} %bitcast.6), channel_id=1, source_target_pairs={{0,64},{32,96},{64,0},{96,32},{1,65},{33,97},{65,1},{97,33},{2,66}... | collective-permute-start | bytes 1179656 | tf_op jit(solution)/shard_map/ppermute | solution.py:173
  72.4 13.5 %collective-permute-start.2 = (bf16[256,768]{1,0:T(8,128)(2,1)S(1)}, bf16[256,768]{1,0:T(8,128)(2,1)S(1)}, u32[]{:S(2)}, u32[]{:S(2)}) collective-permute-start(bf16[256,768]{1,0:T(8,128)(2,1)S(1)} %bitcast.7), channel_id=1, source_target_pairs={{0,1},{1,0},{2,3},{3,2},{4,5},{5,4},{6,7},{7,6},{8,9},{9,8},{10,11... | collective-permute-start | bytes 1179656 | tf_op jit(solution)/shard_map/ppermute | solution.py:173
  75.6 10.3 %collective-permute-start.3 = (bf16[256,768]{1,0:T(8,128)(2,1)S(1)}, bf16[256,768]{1,0:T(8,128)(2,1)S(1)}, u32[]{:S(2)}, u32[]{:S(2)}) collective-permute-start(bf16[256,768]{1,0:T(8,128)(2,1)S(1)} %collective-permute-done.refs_1_), channel_id=1, source_target_pairs={{0,1},{1,0},{2,3},{3,2},{4,5},{5,4},{6,7},{7,6},{8,9},{9,8},{10,11... | collective-permute-start | bytes 1179656 | tf_op jit(solution)/shard_map/ppermute | solution.py:173
  81.6 4.4 %collective-permute-start.4 = (bf16[256,768]{1,0:T(8,128)(2,1)S(1)}, bf16[256,768]{1,0:T(8,128)(2,1)S(1)}, u32[]{:S(2)}, u32[]{:S(2)}) collective-permute-start(bf16[256,768]{1,0:T(8,128)(2,1)S(1)} %collective-permute-done.1.refs_2_), channel_id=1, source_target_pairs={{0,1},{1,0},{2,3},{3,2},{4,5},{5,4},{6,7},{7,6},{8,9},{9,8},{10,11... | collective-permute-start | bytes 1179656 | tf_op jit(solution)/shard_map/ppermute | solution.py:173
  83.5 3.9 %collective-permute-start.6 = (bf16[256,768]{1,0:T(8,128)(2,1)S(1)}, bf16[256,768]{1,0:T(8,128)(2,1)S(1)}, u32[]{:S(2)}, u32[]{:S(2)}) collective-permute-start(bf16[256,768]{1,0:T(8,128)(2,1)S(1)} %collective-permute-done.5.refs_2_), channel_id=1, source_target_pairs={{0,1},{1,0},{2,3},{3,2},{4,5},{5,4},{6,7},{7,6},{8,9},{9,8},{10,11... | collective-permute-start | bytes 1179656 | tf_op jit(solution)/shard_map/ppermute | solution.py:173
  87.4 16.7 %copy-start.1 = (s32[64]{0:T(128)S(1)}, s32[64]{0:T(128)}, u32[]{:S(2)}) copy-start(s32[64]{0:T(128)} %param.3) | copy-start | bytes 772
  92.5 37.4 %all-to-all-start.2 = ((bf16[16,104,128]{2,1,0:T(8,128)(2,1)}), bf16[16,104,128]{2,1,0:T(8,128)(2,1)S(1)}, u32[]{:S(2)}, u32[]{:S(2)}) async-start(bf16[16,104,128]{2,1,0:T(8,128)(2,1)} %shard_map.42), calls=%async_computation.2 | async-start | bytes 851968 | tf_op jit(solution)/shard_map/all_to_all | solution.py:194
  129.9 0.8 copy-start

commit v3 on v2

v3 whole, which is shorter than its diff:
```python
import functools
import math

import jax
import jax.numpy as jnp
from jax import lax
from jax.experimental import pallas as pl
from jax.experimental.pallas import tpu as pltpu
from jax.sharding import Mesh
from jax.sharding import PartitionSpec as P

COEF_A = 3.4445
COEF_B = -4.775
COEF_C = 2.0315
EPS = 1e-07

BF16 = jnp.bfloat16
F32 = jnp.float32
VMEM = pl.BlockSpec(memory_space=pltpu.VMEM)
SMEM = pl.BlockSpec(memory_space=pltpu.SMEM)
TILE = 256
LANES = 128
NOTE = 8


def dot(a, b):
    return jnp.dot(a, b, preferred_element_type=F32)


def gram_of(a, b):
    return lax.dot_general(a, b, (((0,), (0,)), ((), ())), preferred_element_type=F32)


def lower(width):
    return [(slice(j, width), slice(j, j + TILE)) for j in range(0, width, TILE)]


def store_symmetric(ref, rows, cols, value):
    ref[rows, cols] = value
    if cols.stop < rows.stop:
        ref[cols, cols.stop : rows.stop] = value[TILE:].T


def indices(shape):
    return (lax.broadcasted_iota(jnp.int32, shape, d) for d in range(2))


def diagonal(block):
    row, col = indices(block.shape)
    return jnp.sum(jnp.where(row == col, block, 0.0), axis=0, keepdims=True)


def merge(one, two):
    row, col = indices(one.shape)
    return jnp.where(row >= col, one, two), diagonal(two)


def split(both, second_diagonal):
    row, col = indices(both.shape)
    other = both.T
    two = jnp.where(row < col, both, jnp.where(row == col, second_diagonal, other))
    return jnp.where(row >= col, both, other), two


SMALL = TILE // 2
SPARE = 16
HALF = 2 * TILE + SMALL // 2 + SPARE


def gram_kernel(core_ref, mine_ref, other_ref, wide_ref, sent_ref, stack):
    rows = mine_ref.shape[0]
    stack[:rows, :] = mine_ref[...]
    stack[rows:, :] = other_ref[...]
    first = core_ref[0] == 0
    one, two, three = (stack[:, i * TILE : (i + 1) * TILE] for i in range(3))
    below = gram_of(stack[:, TILE:], one)
    middle = gram_of(stack[:, TILE:], two)
    last = gram_of(three, three)
    corner, corner_diagonal = merge(gram_of(one, one), middle[:TILE])
    tip, tip_diagonal = merge(last[:SMALL, :SMALL], last[SMALL:, SMALL:])

    def store(span, lanes, value):
        wide_ref[span, lanes] = value
        sent_ref[span, lanes] = value.astype(BF16)

    every = slice(0, TILE)
    store(slice(0, TILE), every, jnp.where(first, below[:TILE], middle[TILE:]))
    store(slice(TILE, 2 * TILE), every, jnp.where(first, below[TILE:], corner))
    small = jnp.where(first, tip, last[SMALL:, :SMALL])
    span = slice(2 * TILE, HALF - SPARE)
    store(span, slice(0, SMALL), small[: SMALL // 2])
    store(span, slice(SMALL, TILE), small[SMALL // 2 :])
    span = slice(HALF - SPARE, HALF)
    left, right = corner_diagonal[:, :SMALL], corner_diagonal[:, SMALL:]
    store(span, slice(0, SMALL), jnp.broadcast_to(jnp.where(first, tip_diagonal, left), (SPARE, SMALL)))
    store(span, slice(SMALL, TILE), jnp.broadcast_to(jnp.where(first, 0.0, right), (SPARE, SMALL)))


def half_gram(core, mine, other):
    rows, width = mine.shape
    assert width == 3 * TILE
    shape = (HALF, TILE)
    return pl.pallas_call(
        gram_kernel,
        out_shape=(jax.ShapeDtypeStruct(shape, F32), jax.ShapeDtypeStruct(shape, BF16)),
        in_specs=[SMEM, VMEM, VMEM],
        out_specs=(VMEM, VMEM),
        scratch_shapes=[pltpu.VMEM((2 * rows, width), BF16)],
        compiler_params=pltpu.CompilerParams(vmem_limit_bytes=32 * 2**20),
        cost_estimate=pl.CostEstimate(
            flops=2 * rows * width * width,
            bytes_accessed=rows * width * 4 + shape[0] * TILE * 6,
            transcendentals=0,
        ),
    )(core, mine, other)


def polynomial_kernel(scale, core_ref, own_ref, other_ref, x_ref, slab_ref, wide, g, p, s):
    width = g.shape[0]
    core = core_ref[0]

    def pick(half, span):
        return jnp.where(core == half, own_ref[span, :], other_ref[span, :].astype(F32))

    def place(i, j, value, size=TILE):
        wide[i * size : i * size + value.shape[0], j * size : j * size + value.shape[1]] = value

    def small(half):
        value = pick(half, slice(2 * TILE, HALF - SPARE))
        return jnp.concatenate([value[:, :SMALL], value[:, SMALL:]], axis=0)

    spare = slice(HALF - SPARE, HALF - SPARE + 8)
    tip_diagonal, corner_diagonal = pick(0, spare)[:1, :SMALL], pick(1, spare)[:1]
    corner, tip = pick(1, slice(TILE, 2 * TILE)), small(0)
    place(1, 0, pick(0, slice(0, TILE)))
    place(2, 0, pick(0, slice(TILE, 2 * TILE)))
    place(2, 1, pick(1, slice(0, TILE)))
    one, two = split(corner, corner_diagonal)
    place(0, 0, one)
    place(1, 1, two)
    one, two = split(tip, tip_diagonal)
    bend = small(1)
    place(4, 4, one, SMALL)
    place(5, 5, two, SMALL)
    place(5, 4, bend, SMALL)
    place(4, 5, bend.T, SMALL)
    trace = sum(
        jnp.sum(part, axis=1, keepdims=True)
        for part in (diagonal(corner), corner_diagonal, diagonal(tip), tip_diagonal)
    )
    norm = jnp.sqrt(trace)
    inv = 1.0 / (norm + EPS)

    for down, cols in lower(width):
        store_symmetric(g, down, cols, (wide[down, cols] * (inv * inv)).astype(BF16))
    for down, cols in lower(width):
        part = COEF_B * g[down, cols].astype(F32) + COEF_C * dot(g[down, :], g[:, cols])
        store_symmetric(p, down, cols, part.astype(BF16))
    for down, cols in lower(width):
        part = dot(g[down, :], p[:, cols])
        wide[down, cols] = (2 * COEF_A) * part + (COEF_A * COEF_A) * g[down, cols].astype(F32)
        store_symmetric(s, down, cols, part.astype(BF16))
    for down, cols in lower(width):
        part = wide[down, cols] + dot(p[down, :], s[:, cols])
        store_symmetric(g, down, cols, part.astype(BF16))
    for down, cols in lower(width):
        part = COEF_B * g[down, cols].astype(F32) + COEF_C * dot(g[down, :], g[:, cols])
        store_symmetric(s, down, cols, part.astype(BF16))

    x = x_ref[...]
    x1 = (inv * (COEF_A * x.astype(F32) + dot(x, p[...]))).astype(BF16)
    update = (scale * (COEF_A * x1.astype(F32) + dot(x1, s[...]))).astype(BF16)
    blocks, high, _ = slab_ref.shape
    tall = update.shape[0] // blocks
    for i in range(width // LANES):
        slab_ref[:, i * tall : (i + 1) * tall, :] = update[:, i * LANES : (i + 1) * LANES].reshape(
            blocks, tall, LANES
        )
    first = norm.astype(BF16).astype(F32)
    second = norm - first
    note = lax.broadcasted_iota(jnp.int32, (NOTE, LANES), 0)
    note = jnp.where(note < NOTE // 2, first, second).astype(BF16)
    slab_ref[:, high - NOTE :, :] = jnp.broadcast_to(note, (blocks, NOTE, LANES))


def polynomial(core, own, other, x, full_rows, blocks):
    rows, width = x.shape
    mat = pltpu.VMEM((width, width), BF16)
    high = rows // blocks * width // LANES + NOTE
    return pl.pallas_call(
        functools.partial(polynomial_kernel, math.sqrt(full_rows)),
        out_shape=jax.ShapeDtypeStruct((blocks, high, LANES), BF16),
        in_specs=[SMEM, VMEM, VMEM, VMEM],
        out_specs=VMEM,
        scratch_shapes=[pltpu.VMEM((width, width), F32), mat, mat, mat],
        compiler_params=pltpu.CompilerParams(vmem_limit_bytes=32 * 2**20),
        cost_estimate=pl.CostEstimate(
            flops=6 * width**3 + 4 * rows * width * width,
            bytes_accessed=width * width * 3 + rows * width * 4,
            transcendentals=0,
        ),
    )(core, own, other, x)


def place_kernel(count, back_ref, hit_ref, out_ref, rms_ref):
    tall, width = out_ref.shape[1:]
    for i in range(width // LANES):
        out_ref[:, :, i * LANES : (i + 1) * LANES] = back_ref[:, i * tall : (i + 1) * tall, :]
    note = back_ref[:, back_ref.shape[1] - NOTE :, :].astype(F32)
    norms = note[:, :1, :1] + note[:, NOTE // 2 : NOTE // 2 + 1, :1]
    mine = jnp.sum(jnp.where(hit_ref[...] > 0, norms, 0.0)) / math.sqrt(count)
    step = pl.program_id(0)

    @pl.when(step == 0)
    def _():
        rms_ref[0, 0] = mine

    @pl.when(step > 0)
    def _():
        rms_ref[0, 0] = rms_ref[0, 0] + mine


def place(back, hits, tall, width, full_rows):
    blocks, high, lanes = back.shape
    group = blocks // 2
    return pl.pallas_call(
        functools.partial(place_kernel, full_rows * width),
        grid=(blocks // group,),
        out_shape=(
            jax.ShapeDtypeStruct((blocks, tall, width), BF16),
            jax.ShapeDtypeStruct((1, 1), F32),
        ),
        in_specs=[
            pl.BlockSpec((group, high, lanes), lambda i: (i, 0, 0)),
            pl.BlockSpec((group, 1, 1), lambda i: (i, 0, 0)),
        ],
        out_specs=(pl.BlockSpec((group, tall, width), lambda i: (i, 0, 0)), SMEM),
        compiler_params=pltpu.CompilerParams(vmem_limit_bytes=60 * 2**20),
    )(back, hits.astype(jnp.int32).reshape(blocks, 1, 1))


def shift(value, axis, distance):
    n = lax.axis_size(axis)
    return lax.ppermute(value, axis, [(i, (i + distance) % n) for i in range(n)])


def neighbour(value, axis, turn):
    ring, core_n = lax.axis_size(axis), lax.axis_size("core")
    pairs = []
    for at in range(ring):
        for core in range(core_n):
            other = at ^ 1 if (turn + core) % 2 == 0 else ring - 1 - at
            pairs.append((at * core_n + core, other * core_n + core))
    return lax.ppermute(value, (axis, "core"), pairs)


def on_device(grads, owners):
    block = grads[0]
    mats, rows_dev, width = block.shape
    dp_n = lax.axis_size("dp")
    y_n, core_n = lax.axis_size("y"), lax.axis_size("core")
    zh_n, zl_n = lax.axis_size("zh"), lax.axis_size("zl")
    z_n = y_n * zl_n
    mats_dp = mats // dp_n
    full_rows = zh_n * z_n * core_n * rows_dev

    slabs = block.reshape(dp_n, mats_dp, rows_dev, width)
    replicas = lax.all_to_all(slabs, "dp", 0, 0, tiled=True)
    summed = jnp.sum(replicas.astype(F32), axis=0).astype(BF16)
    mine = lax.all_to_all(summed, ("y", "zl"), 0, 0, tiled=True).reshape(z_n * rows_dev, width)

    core = lax.axis_index("core").astype(jnp.int32).reshape(1)
    total, sent = half_gram(core, mine, shift(mine, "core", 1))
    cut = HALF // 2 // SPARE * SPARE
    totals = [total[:cut], total[cut:]]
    sents = [sent[:cut], sent[cut:]]
    for turn in range(2):
        came = [neighbour(part, "zh", turn + i) for i, part in enumerate(sents)]
        totals = [part + other.astype(F32) for part, other in zip(totals, came)]
        sents = [part.astype(BF16) for part in totals]
    total, sent = jnp.concatenate(totals), jnp.concatenate(sents)
    slab = polynomial(core, total, shift(sent, "core", 1), mine, full_rows, z_n)
    back = lax.all_to_all(slab, ("y", "zl"), 0, 0, tiled=True)

    index = (lax.axis_index("y") * zh_n + lax.axis_index("zh")) * zl_n + lax.axis_index("zl")
    index = index * core_n + lax.axis_index("core")
    owned = lax.dynamic_slice_in_dim(owners, lax.axis_index("dp") * mats_dp, mats_dp)
    hits = owned == index - index % core_n
    return place(back, hits, rows_dev, width, full_rows)


def solution(mesh):
    dp_n, fsdp_n = mesh.devices.shape
    grid = Mesh(mesh.devices.reshape(dp_n, 4, 4, fsdp_n // 32, 2), ("dp", "y", "zh", "zl", "core"))
    fsdp = ("y", "zh", "zl", "core")
    in_specs = (P("dp", None, fsdp, None), P())
    out_specs = (P("dp", fsdp, None), P("dp", fsdp))
    return jax.shard_map(
        on_device, mesh=grid, in_specs=in_specs, out_specs=out_specs, check_vma=False
    )
```

time: 133 us -> 124 us (0.932)
  the two profiles are of different devices: /device:TPU:24 before, /device:TPU:1 now
where the time goes in v3:
time: 124 us; the launch traced here: 123 us
  blocking collectives  45.2 us (36%)
  starting transfers between devices  43.4 us (35%)
  waiting for transfers between devices  25.1 us (20%)
  Pallas kernels  6.89 us (6%)
  local copies, waits for them, and re-layouts  1.46 us (1%)
    ppermute x4, starting transfers between devices, neighbour(): return lax.ppermute(value, (axis, 'core'), pairs)  32.5 us
    all_to_all x1, blocking collectives, on_device(): lax.all_to_all(summed, ('y', 'zl'), 0, 0, tiled=True)  25.4 us
    all_to_all x1, blocking collectives, on_device(): replicas = lax.all_to_all(slabs, 'dp', 0, 0, tiled=True)  19.7 us
    all_to_all x1, waiting for transfers between devices, on_device(): back = lax.all_to_all(slab, ('y', 'zl'), 0, 0, tiled=True)  12.9 us
    ppermute x4, waiting for transfers between devices, neighbour(): return lax.ppermute(value, (axis, 'core'), pairs)  9.75 us
    ppermute x2, starting transfers between devices, shift(): lax.ppermute(value, axis, [(i, (i + distance) % n) for i in range(n)])  7.22 us
    pallas_call x1, Pallas kernels, polynomial(): pl.pallas_call(functools.partial(polynomial_kernel, math.sqrt(full_rows))...  4.46 us
    all_to_all x1, starting transfers between devices, on_device(): back = lax.all_to_all(slab, ('y', 'zl'), 0, 0, tiled=True)  3.7 us
  transfers between devices with their start and end apart: 7, of which 6 were waited for; matrix products, arithmetic and copies ran while one was open for 1% of the time, Pallas kernels for 0%

profile of v3, /device:TPU:1, one launch (start us, length us, event | category | flops | bytes accessed | tf_op | source)
XLA Modules:
  0.0 123.5 jit_solution(4939609266469573304)
XLA Ops:
  0.6 19.7 %all_to_all.15 = bf16[4,16,16,768]{3,2,1,0:T(8,128)(2,1)S(1)} all-to-all(bf16[4,16,16,768]{3,2,1,0:T(8,128)(2,1)} %bitcast.8), channel_id=1, replica_groups=mesh['dp'=4,'y'=4,'zh'=4,'zl'=4,'core'=2] {'dp'}, dimensions={0} | all-to-all | bytes 3145728 | tf_op jit(solution)/shard_map/all_to_all | solution.py:268
  20.4 0.4 reduce_sum.12
  20.7 25.4 %all_to_all.16 = bf16[16,16,768]{2,1,0:T(8,128)(2,1)S(1)} all-to-all(bf16[16,16,768]{2,1,0:T(8,128)(2,1)S(1)} %reduce_sum.12), channel_id=1, replica_groups=mesh['dp'=4,'y'=4,'zh'=4,'zl'=4,'core'=2] {'y','zl'}, dimensions={0} | all-to-all | bytes 786432 | tf_op jit(solution)/shard_map/all_to_all | solution.py:270
  46.1 4.2 %collective-permute-start = (bf16[256,768]{1,0:T(8,128)(2,1)S(1)}, bf16[256,768]{1,0:T(8,128)(2,1)S(1)}, u32[]{:S(2)}, u32[]{:S(2)}) collective-permute-start(bf16[256,768]{1,0:T(8,128)(2,1)S(1)} %bitcast.5), channel_id=1, source_target_pairs={{0,1},{1,0},{2,3},{3,2},{4,5},{5,4},{6,7},{7,6},{8,9},{9,8},{10,11... | collective-permute-start | bytes 1179656 | tf_op jit(solution)/shard_map/ppermute | solution.py:244
  50.4 1.3 %collective-permute-done.other_ref = bf16[256,768]{1,0:T(8,128)(2,1)S(1)} collective-permute-done((bf16[256,768]{1,0:T(8,128)(2,1)S(1)}, bf16[256,768]{1,0:T(8,128)(2,1)S(1)}, u32[]{:S(2)}, u32[]{:S(2)}) %collective-permute-start) | collective-permute-done | bytes 393248 | tf_op jit(solution)/shard_map/ppermute | solution.py:244
  51.7 0.6 shard_map.41
  52.3 9.8 %collective-permute-start.1 = (bf16[288,256]{1,0:T(8,128)(2,1)S(1)}, bf16[288,256]{1,0:T(8,128)(2,1)S(1)}, u32[]{:S(2)}, u32[]{:S(2)}) collective-permute-start(bf16[288,256]{1,0:T(8,128)(2,1)S(1)} %slice.13), channel_id=1, source_target_pairs={{0,8},{1,25},{8,0},{9,17},{16,24},{17,9},{24,16},{25,1},{2,10},{3,... | collective-permute-start | bytes 442376 | tf_op jit(solution)/shard_map/ppermute | solution.py:254
  62.1 5.2 %collective-permute-start.3 = (bf16[304,256]{1,0:T(8,128)(2,1)S(1)}, bf16[304,256]{1,0:T(8,128)(2,1)S(1)}, u32[]{:S(2)}, u32[]{:S(2)}) collective-permute-start(bf16[304,256]{1,0:T(8,128)(2,1)S(1)} %slice.15), channel_id=1, source_target_pairs={{0,24},{1,9},{8,16},{9,1},{16,8},{17,25},{24,0},{25,17},{2,26},{3,... | collective-permute-start | bytes 466952 | tf_op jit(solution)/shard_map/ppermute | solution.py:254
  67.3 0.2 collective-permute-done.1
  67.5 15.6 %collective-permute-start.2 = (bf16[288,256]{1,0:T(8,128)(2,1)S(1)}, bf16[288,256]{1,0:T(8,128)(2,1)S(1)}, u32[]{:S(2)}, u32[]{:S(2)}) collective-permute-start(bf16[288,256]{1,0:T(8,128)(2,1)S(1)} %fusion.1), channel_id=1, source_target_pairs={{0,24},{1,9},{8,16},{9,1},{16,8},{17,25},{24,0},{25,17},{2,26},{3,... | collective-permute-start | bytes 442376 | tf_op jit(solution)/shard_map/ppermute | solution.py:254
  83.2 0.0 collective-permute-done.3
  83.2 1.9 %collective-permute-start.4 = (bf16[304,256]{1,0:T(8,128)(2,1)S(1)}, bf16[304,256]{1,0:T(8,128)(2,1)S(1)}, u32[]{:S(2)}, u32[]{:S(2)}) collective-permute-start(bf16[304,256]{1,0:T(8,128)(2,1)S(1)} %fusion), channel_id=1, source_target_pairs={{0,8},{1,25},{8,0},{9,17},{16,24},{17,9},{24,16},{25,1},{2,10},{3,... | collective-permute-start | bytes 466952 | tf_op jit(solution)/shard_map/ppermute | solution.py:254
  85.2 2.4 %collective-permute-done.2 = bf16[288,256]{1,0:T(8,128)(2,1)S(1)} collective-permute-done((bf16[288,256]{1,0:T(8,128)(2,1)S(1)}, bf16[288,256]{1,0:T(8,128)(2,1)S(1)}, u32[]{:S(2)}, u32[]{:S(2)}) %collective-permute-start.2) | collective-permute-done | bytes 147488 | tf_op jit(solution)/shard_map/ppermute | solution.py:254
  87.6 0.1 fusion.3
  87.6 7.1 %collective-permute-done.4 = bf16[304,256]{1,0:T(8,128)(2,1)S(1)} collective-permute-done((bf16[304,256]{1,0:T(8,128)(2,1)S(1)}, bf16[304,256]{1,0:T(8,128)(2,1)S(1)}, u32[]{:S(2)}, u32[]{:S(2)}) %collective-permute-start.4) | collective-permute-done | bytes 155680 | tf_op jit(solution)/shard_map/ppermute | solution.py:254
  94.8 0.1 fusion.4
  94.8 3.0 %collective-permute-start.5 = (bf16[592,256]{1,0:T(8,128)(2,1)S(1)}, bf16[592,256]{1,0:T(8,128)(2,1)S(1)}, u32[]{:S(2)}, u32[]{:S(2)}) collective-permute-start(bf16[592,256]{1,0:T(8,128)(2,1)S(1)} %pad_maximum_fusion.1), channel_id=1, source_target_pairs={{0,1},{1,0},{2,3},{3,2},{4,5},{5,4},{6,7},{7,6},{8,9},{9,8},{10,11... | collective-permute-start | bytes 909320 | tf_op jit(solution)/shard_map/ppermute | solution.py:244
  97.9 0.0 copy-start.1
  97.9 1.1 collective-permute-done.5.other_ref
  99.1 4.5 %shard_map.42 = bf16[16,104,128]{2,1,0:T(8,128)(2,1)} custom-call(s32[1]{0:T(128)} %bitcast.core_ref, f32[592,256]{1,0:T(8,128)S(1)} %pad_maximum_fusion.own_ref, bf16[592,256]{1,0:T(8,128)(2,1)S(1)} %collective-permute-done.5.other_ref, bf16[256,768]{1,0:T(8,128)(2,1)S(1)} %bitcast.7), custom_call_target="tpu_custom_call" | custom-call | flops 3321888768 | bytes 2555904 | tf_op jit(solution)/shard_map/pallas_call | solution.py:190
  103.5 3.7 %all-to-all-start.2 = ((bf16[16,104,128]{2,1,0:T(8,128)(2,1)}), bf16[16,104,128]{2,1,0:T(8,128)(2,1)S(1)}, u32[]{:S(2)}, u32[]{:S(2)}) async-start(bf16[16,104,128]{2,1,0:T(8,128)(2,1)} %shard_map.42), calls=%async_computation.2 | async-start | bytes 851968 | tf_op jit(solution)/shard_map/all_to_all | solution.py:283
  107.3 0.0 copy-done.1
  107.3 0.1 fusion.2
  107.4 0.7 copy.4.hit_ref
  108.0 12.9 %all-to-all-done.2.back_ref = bf16[16,104,128]{2,1,0:T(8,128)(2,1)S(1)} async-done(((bf16[16,104,128]{2,1,0:T(8,128)(2,1)}), bf16[16,104,128]{2,1,0:T(8,128)(2,1)S(1)}, u32[]{:S(2)}, u32[]{:S(2)}) %all-to-all-start.2) | async-done | bytes 426016 | tf_op jit(solution)/shard_map/all_to_all | solution.py:283
  120.9 0.0 copy-start
  120.9 0.7 copy-done
  121.6 1.8 %shard_map.43 = (bf16[16,16,768]{2,1,0:T(8,128)(2,1)}, f32[1,1]{1,0:T(1,128)}) custom-call(bf16[16,104,128]{2,1,0:T(8,128)(2,1)} %copy-done, s32[16,1,1]{2,1,0:T(1,128)} %copy.4.hit_ref), custom_call_target="tpu_custom_call" | custom-call | tf_op jit(solution)/shard_map/pallas_call | solution.py:226
  (6 shorter events, 0.2 us)
Async XLA Ops:
  46.1 5.5 %collective-permute-start = (bf16[256,768]{1,0:T(8,128)(2,1)S(1)}, bf16[256,768]{1,0:T(8,128)(2,1)S(1)}, u32[]{:S(2)}, u32[]{:S(2)}) collective-permute-start(bf16[256,768]{1,0:T(8,128)(2,1)S(1)} %bitcast.5), channel_id=1, source_target_pairs={{0,1},{1,0},{2,3},{3,2},{4,5},{5,4},{6,7},{7,6},{8,9},{9,8},{10,11... | collective-permute-start | bytes 1179656 | tf_op jit(solution)/shard_map/ppermute | solution.py:244
  52.3 15.2 %collective-permute-start.1 = (bf16[288,256]{1,0:T(8,128)(2,1)S(1)}, bf16[288,256]{1,0:T(8,128)(2,1)S(1)}, u32[]{:S(2)}, u32[]{:S(2)}) collective-permute-start(bf16[288,256]{1,0:T(8,128)(2,1)S(1)} %slice.13), channel_id=1, source_target_pairs={{0,8},{1,25},{8,0},{9,17},{16,24},{17,9},{24,16},{25,1},{2,10},{3,... | collective-permute-start | bytes 442376 | tf_op jit(solution)/shard_map/ppermute | solution.py:254
  62.1 21.1 %collective-permute-start.3 = (bf16[304,256]{1,0:T(8,128)(2,1)S(1)}, bf16[304,256]{1,0:T(8,128)(2,1)S(1)}, u32[]{:S(2)}, u32[]{:S(2)}) collective-permute-start(bf16[304,256]{1,0:T(8,128)(2,1)S(1)} %slice.15), channel_id=1, source_target_pairs={{0,24},{1,9},{8,16},{9,1},{16,8},{17,25},{24,0},{25,17},{2,26},{3,... | collective-permute-start | bytes 466952 | tf_op jit(solution)/shard_map/ppermute | solution.py:254
  67.5 20.0 %collective-permute-start.2 = (bf16[288,256]{1,0:T(8,128)(2,1)S(1)}, bf16[288,256]{1,0:T(8,128)(2,1)S(1)}, u32[]{:S(2)}, u32[]{:S(2)}) collective-permute-start(bf16[288,256]{1,0:T(8,128)(2,1)S(1)} %fusion.1), channel_id=1, source_target_pairs={{0,24},{1,9},{8,16},{9,1},{16,8},{17,25},{24,0},{25,17},{2,26},{3,... | collective-permute-start | bytes 442376 | tf_op jit(solution)/shard_map/ppermute | solution.py:254
  83.2 11.5 %collective-permute-start.4 = (bf16[304,256]{1,0:T(8,128)(2,1)S(1)}, bf16[304,256]{1,0:T(8,128)(2,1)S(1)}, u32[]{:S(2)}, u32[]{:S(2)}) collective-permute-start(bf16[304,256]{1,0:T(8,128)(2,1)S(1)} %fusion), channel_id=1, source_target_pairs={{0,8},{1,25},{8,0},{9,17},{16,24},{17,9},{24,16},{25,1},{2,10},{3,... | collective-permute-start | bytes 466952 | tf_op jit(solution)/shard_map/ppermute | solution.py:254
  94.8 4.2 %collective-permute-start.5 = (bf16[592,256]{1,0:T(8,128)(2,1)S(1)}, bf16[592,256]{1,0:T(8,128)(2,1)S(1)}, u32[]{:S(2)}, u32[]{:S(2)}) collective-permute-start(bf16[592,256]{1,0:T(8,128)(2,1)S(1)} %pad_maximum_fusion.1), channel_id=1, source_target_pairs={{0,1},{1,0},{2,3},{3,2},{4,5},{5,4},{6,7},{7,6},{8,9},{9,8},{10,11... | collective-permute-start | bytes 909320 | tf_op jit(solution)/shard_map/ppermute | solution.py:244
  97.9 9.3 %copy-start.1 = (s32[64]{0:T(128)S(1)}, s32[64]{0:T(128)}, u32[]{:S(2)}) copy-start(s32[64]{0:T(128)} %param.3) | copy-start | bytes 772
  103.5 17.4 %all-to-all-start.2 = ((bf16[16,104,128]{2,1,0:T(8,128)(2,1)}), bf16[16,104,128]{2,1,0:T(8,128)(2,1)S(1)}, u32[]{:S(2)}, u32[]{:S(2)}) async-start(bf16[16,104,128]{2,1,0:T(8,128)(2,1)} %shard_map.42), calls=%async_computation.2 | async-start | bytes 851968 | tf_op jit(solution)/shard_map/all_to_all | solution.py:283
  120.9 0.8 copy-start

commit v4 on v3

--- a/solution.py
+++ b/solution.py
@@ -19,6 +19,7 @@
 VMEM = pl.BlockSpec(memory_space=pltpu.VMEM)
 SMEM = pl.BlockSpec(memory_space=pltpu.SMEM)
 TILE = 256
+FSDP = ("y", "zh", "zm", "zb", "core")
 LANES = 128
 NOTE = 8
 
@@ -67,10 +68,11 @@
 HALF = 2 * TILE + SMALL // 2 + SPARE
 
 
-def gram_kernel(core_ref, mine_ref, other_ref, wide_ref, sent_ref, stack):
-    rows = mine_ref.shape[0]
-    stack[:rows, :] = mine_ref[...]
-    stack[rows:, :] = other_ref[...]
+def gram_kernel(core_ref, *refs):
+    *pieces, wide_ref, sent_ref, stack = refs
+    rows = pieces[0].shape[0]
+    for i, piece in enumerate(pieces):
+        stack[i * rows : (i + 1) * rows, :] = piece[...]
     first = core_ref[0] == 0
     one, two, three = (stack[:, i * TILE : (i + 1) * TILE] for i in range(3))
     below = gram_of(stack[:, TILE:], one)
@@ -96,23 +98,23 @@
     store(span, slice(SMALL, TILE), jnp.broadcast_to(jnp.where(first, 0.0, right), (SPARE, SMALL)))
 
 
-def half_gram(core, mine, other):
-    rows, width = mine.shape
+def half_gram(core, pieces):
+    rows, width = pieces[0].shape
     assert width == 3 * TILE
     shape = (HALF, TILE)
     return pl.pallas_call(
         gram_kernel,
         out_shape=(jax.ShapeDtypeStruct(shape, F32), jax.ShapeDtypeStruct(shape, BF16)),
-        in_specs=[SMEM, VMEM, VMEM],
+        in_specs=[SMEM] + [VMEM] * len(pieces),
         out_specs=(VMEM, VMEM),
-        scratch_shapes=[pltpu.VMEM((2 * rows, width), BF16)],
+        scratch_shapes=[pltpu.VMEM((len(pieces) * rows, width), BF16)],
         compiler_params=pltpu.CompilerParams(vmem_limit_bytes=32 * 2**20),
         cost_estimate=pl.CostEstimate(
-            flops=2 * rows * width * width,
-            bytes_accessed=rows * width * 4 + shape[0] * TILE * 6,
+            flops=len(pieces) * rows * width * width,
+            bytes_accessed=len(pieces) * rows * width * 2 + shape[0] * TILE * 6,
             transcendentals=0,
         ),
-    )(core, mine, other)
+    )(core, *pieces)
 
 
 def polynomial_kernel(scale, core_ref, own_ref, other_ref, x_ref, slab_ref, wide, g, p, s):
@@ -257,33 +259,42 @@
 def on_device(grads, owners):
     block = grads[0]
     mats, rows_dev, width = block.shape
-    dp_n = lax.axis_size("dp")
-    y_n, core_n = lax.axis_size("y"), lax.axis_size("core")
-    zh_n, zl_n = lax.axis_size("zh"), lax.axis_size("zl")
-    z_n = y_n * zl_n
+    dp_n, y_n, core_n = lax.axis_size("dp"), lax.axis_size("y"), lax.axis_size("core")
+    far_n, mid_n, near_n = lax.axis_size("zh"), lax.axis_size("zm"), lax.axis_size("zb")
     mats_dp = mats // dp_n
-    full_rows = zh_n * z_n * core_n * rows_dev
-
-    slabs = block.reshape(dp_n, mats_dp, rows_dev, width)
-    replicas = lax.all_to_all(slabs, "dp", 0, 0, tiled=True)
-    summed = jnp.sum(replicas.astype(F32), axis=0).astype(BF16)
-    mine = lax.all_to_all(summed, ("y", "zl"), 0, 0, tiled=True).reshape(z_n * rows_dev, width)
-
+    full_rows = y_n * far_n * mid_n * near_n * core_n * rows_dev
     core = lax.axis_index("core").astype(jnp.int32).reshape(1)
-    total, sent = half_gram(core, mine, shift(mine, "core", 1))
+    mid = lax.axis_index("zm")
+
+    slabs = block.reshape(dp_n * y_n * near_n, mid_n, rows_dev, width)
+    slabs = lax.all_to_all(slabs, ("dp", "y", "zb"), 0, 0, tiled=True)
+    slabs = slabs.reshape(dp_n, y_n * near_n, mid_n, rows_dev, width)
+
+    def summed(which):
+        part = lax.dynamic_index_in_dim(slabs, which, 2, keepdims=False)
+        return jnp.sum(part.astype(F32), axis=0).astype(BF16)
+
+    away = shift(summed(1 - mid), "zm", 1)
+    here = summed(mid)
+    mine = jnp.stack([jnp.where(mid == 0, here, away), jnp.where(mid == 0, away, here)], axis=1)
+    mine = mine.reshape(mats_dp * rows_dev, width)
+    pieces = [part.reshape(-1, width) for part in (here, away)]
+    pieces += [shift(part, "core", 1) for part in pieces]
+    total, sent = half_gram(core, pieces)
     cut = HALF // 2 // SPARE * SPARE
     totals = [total[:cut], total[cut:]]
     sents = [sent[:cut], sent[cut:]]
     for turn in range(2):
-        came = [neighbour(part, "zh", turn + i) for i, part in enumerate(sents)]
+        came = [neighbour(part, "zh", turn) for part in sents]
         totals = [part + other.astype(F32) for part, other in zip(totals, came)]
         sents = [part.astype(BF16) for part in totals]
     total, sent = jnp.concatenate(totals), jnp.concatenate(sents)
-    slab = polynomial(core, total, shift(sent, "core", 1), mine, full_rows, z_n)
-    back = lax.all_to_all(slab, ("y", "zl"), 0, 0, tiled=True)
-
-    index = (lax.axis_index("y") * zh_n + lax.axis_index("zh")) * zl_n + lax.axis_index("zl")
-    index = index * core_n + lax.axis_index("core")
+    slab = polynomial(core, total, shift(sent, "core", 1), mine, full_rows, mats_dp)
+    back = lax.all_to_all(slab, ("y", "zb", "zm"), 0, 0, tiled=True)
+
+    index = jnp.zeros((), jnp.int32)
+    for axis in FSDP:
+        index = index * lax.axis_size(axis) + lax.axis_index(axis)
     owned = lax.dynamic_slice_in_dim(owners, lax.axis_index("dp") * mats_dp, mats_dp)
     hits = owned == index - index % core_n
     return place(back, hits, rows_dev, width, full_rows)
@@ -291,10 +302,10 @@
 
 def solution(mesh):
     dp_n, fsdp_n = mesh.devices.shape
-    grid = Mesh(mesh.devices.reshape(dp_n, 4, 4, fsdp_n // 32, 2), ("dp", "y", "zh", "zl", "core"))
-    fsdp = ("y", "zh", "zl", "core")
-    in_specs = (P("dp", None, fsdp, None), P())
-    out_specs = (P("dp", fsdp, None), P("dp", fsdp))
+    shape = (dp_n, 4, fsdp_n // 32, 2, 2, 2)
+    grid = Mesh(mesh.devices.reshape(shape), ("dp", *FSDP))
+    in_specs = (P("dp", None, FSDP, None), P())
+    out_specs = (P("dp", FSDP, None), P("dp", FSDP))
     return jax.shard_map(
         on_device, mesh=grid, in_specs=in_specs, out_specs=out_specs, check_vma=False
     )

time: 124 us -> 122 us (0.984)
  blocking collectives: 45.2 us -> 0 us
  waiting for transfers between devices: 25.1 us -> 50.8 us
  starting transfers between devices: 43.4 us -> 59.4 us
    all_to_all x2 -> x0, blocking collectives: 45.2 us -> none  [the longest x1 25.4 us: on_device(): lax.all_to_all(summed, ('y', 'zl'), 0, 0, tiled=True)]
    all_to_all x1 -> x2, waiting for transfers between devices: 12.9 us -> 33.1 us  [the longest x1 22.3 us: on_device(): slabs = lax.all_to_all(slabs, ('dp', 'y', 'zb'), 0, 0, tiled=True)]
    ppermute x2 -> x4, starting transfers between devices: 7.22 us -> 20.9 us  [shift(): lax.ppermute(value, axis, [(i, (i + distance) % n) for i in range(n)])]
    all_to_all x1 -> x2, starting transfers between devices: 3.7 us -> 13.5 us  [the longest x1 9.24 us: on_device(): slabs = lax.all_to_all(slabs, ('dp', 'y', 'zb'), 0, 0, tiled=True)]
    ppermute x4, starting transfers between devices: 32.5 us -> 25 us  [neighbour(): return lax.ppermute(value, (axis, 'core'), pairs)]
    ppermute x4, waiting for transfers between devices: 9.75 us -> 13.4 us  [neighbour(): return lax.ppermute(value, (axis, 'core'), pairs)]
    ppermute x2 -> x4, waiting for transfers between devices: 2.46 us -> 4.38 us  [shift(): lax.ppermute(value, axis, [(i, (i + distance) % n) for i in range(n)])]
  transfers between devices with their start and end apart: 7 -> 10, of which waited for: 6 -> 8; matrix products, arithmetic and copies ran while one was open for 1% -> 1% of each run, Pallas kernels for 0% -> 0%
where the time goes in v4:
time: 122 us; the launch traced here: 120 us
  starting transfers between devices  59.4 us (49%)
  waiting for transfers between devices  50.8 us (42%)
  Pallas kernels  6.93 us (6%)
  local copies, waits for them, and re-layouts  1.45 us (1%)
    ppermute x4, starting transfers between devices, neighbour(): return lax.ppermute(value, (axis, 'core'), pairs)  25 us
    all_to_all x1, waiting for transfers between devices, on_device(): slabs = lax.all_to_all(slabs, ('dp', 'y', 'zb'), 0, 0, tiled=True)  22.3 us
    ppermute x4, starting transfers between devices, shift(): lax.ppermute(value, axis, [(i, (i + distance) % n) for i in range(n)])  20.9 us
    ppermute x4, waiting for transfers between devices, neighbour(): return lax.ppermute(value, (axis, 'core'), pairs)  13.4 us
    all_to_all x1, waiting for transfers between devices, on_device(): back = lax.all_to_all(slab, ('y', 'zb', 'zm'), 0, 0, tiled=True)  10.8 us
    all_to_all x1, starting transfers between devices, on_device(): slabs = lax.all_to_all(slabs, ('dp', 'y', 'zb'), 0, 0, tiled=True)  9.24 us
    pallas_call x1, Pallas kernels, polynomial(): pl.pallas_call(functools.partial(polynomial_kernel, math.sqrt(full_rows))...  4.5 us
    ppermute x4, waiting for transfers between devices, shift(): lax.ppermute(value, axis, [(i, (i + distance) % n) for i in range(n)])  4.38 us
  transfers between devices with their start and end apart: 10, of which 8 were waited for; matrix products, arithmetic and copies ran while one was open for 1% of the time, Pallas kernels for 0%

profile of v4, /device:TPU:1, one launch (start us, length us, event | category | flops | bytes accessed | tf_op | source)
XLA Modules:
  0.0 120.3 jit_solution(11443846937096147092)
XLA Ops:
  0.6 9.2 %all-to-all-start = ((bf16[32,2,16,768]{3,2,1,0:T(8,128)(2,1)}), bf16[32,2,16,768]{3,2,1,0:T(8,128)(2,1)S(1)}, u32[]{:S(2)}, u32[]{:S(2)}) async-start(bf16[32,2,16,768]{3,2,1,0:T(8,128)(2,1)} %bitcast.20), calls=%async_computation | async-start | bytes 3145728 | tf_op jit(solution)/shard_map/all_to_all | solution.py:270
  9.9 22.3 %all-to-all-done = bf16[32,2,16,768]{3,2,1,0:T(8,128)(2,1)S(1)} async-done(((bf16[32,2,16,768]{3,2,1,0:T(8,128)(2,1)}), bf16[32,2,16,768]{3,2,1,0:T(8,128)(2,1)S(1)}, u32[]{:S(2)}, u32[]{:S(2)}) %all-to-all-start) | async-done | bytes 1572896 | tf_op jit(solution)/shard_map/all_to_all | solution.py:270
  32.1 0.4 dynamic-slice_reduce_fusion
  32.6 6.7 %collective-permute-start = (bf16[8,16,768]{2,1,0:T(8,128)(2,1)S(1)}, bf16[8,16,768]{2,1,0:T(8,128)(2,1)S(1)}, u32[]{:S(2)}, u32[]{:S(2)}) collective-permute-start(bf16[8,16,768]{2,1,0:T(8,128)(2,1)S(1)} %get-tuple-element.6), channel_id=1, source_target_pairs={{0,4},{4,0},{1,5},{5,1},{2,6},{6,2},{3,7},{7,3},{8,12},{12,8},{9,1... | collective-permute-start | bytes 589832 | tf_op jit(solution)/shard_map/ppermute | solution.py:246
  39.2 4.4 %collective-permute-start.1 = (bf16[128,768]{1,0:T(8,128)(2,1)S(1)}, bf16[128,768]{1,0:T(8,128)(2,1)S(1)}, u32[]{:S(2)}, u32[]{:S(2)}) collective-permute-start(bf16[128,768]{1,0:T(8,128)(2,1)S(1)} %bitcast.14), channel_id=1, source_target_pairs={{0,1},{1,0},{2,3},{3,2},{4,5},{5,4},{6,7},{7,6},{8,9},{9,8},{10,11... | collective-permute-start | bytes 589832 | tf_op jit(solution)/shard_map/ppermute | solution.py:246
  43.7 2.3 %collective-permute-done = bf16[8,16,768]{2,1,0:T(8,128)(2,1)S(1)} collective-permute-done((bf16[8,16,768]{2,1,0:T(8,128)(2,1)S(1)}, bf16[8,16,768]{2,1,0:T(8,128)(2,1)S(1)}, u32[]{:S(2)}, u32[]{:S(2)}) %collective-permute-start) | collective-permute-done | bytes 196640 | tf_op jit(solution)/shard_map/ppermute | solution.py:246
  46.0 3.5 %collective-permute-start.2 = (bf16[128,768]{1,0:T(8,128)(2,1)S(1)}, bf16[128,768]{1,0:T(8,128)(2,1)S(1)}, u32[]{:S(2)}, u32[]{:S(2)}) collective-permute-start(bf16[128,768]{1,0:T(8,128)(2,1)S(1)} %bitcast.17), channel_id=1, source_target_pairs={{0,1},{1,0},{2,3},{3,2},{4,5},{5,4},{6,7},{7,6},{8,9},{9,8},{10,11... | collective-permute-start | bytes 589832 | tf_op jit(solution)/shard_map/ppermute | solution.py:246
  49.5 0.0 collective-permute-done.1.refs_2_
  49.5 1.0 collective-permute-done.2.refs_3_
  50.5 0.6 shard_map.41
  51.2 10.9 %collective-permute-start.3 = (bf16[288,256]{1,0:T(8,128)(2,1)S(1)}, bf16[288,256]{1,0:T(8,128)(2,1)S(1)}, u32[]{:S(2)}, u32[]{:S(2)}) collective-permute-start(bf16[288,256]{1,0:T(8,128)(2,1)S(1)} %slice.13), channel_id=1, source_target_pairs={{0,8},{1,25},{8,0},{9,17},{16,24},{17,9},{24,16},{25,1},{2,10},{3,... | collective-permute-start | bytes 442376 | tf_op jit(solution)/shard_map/ppermute | solution.py:256
  62.1 1.9 %collective-permute-start.5 = (bf16[304,256]{1,0:T(8,128)(2,1)S(1)}, bf16[304,256]{1,0:T(8,128)(2,1)S(1)}, u32[]{:S(2)}, u32[]{:S(2)}) collective-permute-start(bf16[304,256]{1,0:T(8,128)(2,1)S(1)} %slice.15), channel_id=1, source_target_pairs={{0,8},{1,25},{8,0},{9,17},{16,24},{17,9},{24,16},{25,1},{2,10},{3,... | collective-permute-start | bytes 466952 | tf_op jit(solution)/shard_map/ppermute | solution.py:256
  64.0 3.0 %collective-permute-done.3 = bf16[288,256]{1,0:T(8,128)(2,1)S(1)} collective-permute-done((bf16[288,256]{1,0:T(8,128)(2,1)S(1)}, bf16[288,256]{1,0:T(8,128)(2,1)S(1)}, u32[]{:S(2)}, u32[]{:S(2)}) %collective-permute-start.3) | collective-permute-done | bytes 147488 | tf_op jit(solution)/shard_map/ppermute | solution.py:256
  67.1 9.4 %collective-permute-start.4 = (bf16[288,256]{1,0:T(8,128)(2,1)S(1)}, bf16[288,256]{1,0:T(8,128)(2,1)S(1)}, u32[]{:S(2)}, u32[]{:S(2)}) collective-permute-start(bf16[288,256]{1,0:T(8,128)(2,1)S(1)} %fusion.1), channel_id=1, source_target_pairs={{0,24},{1,9},{8,16},{9,1},{16,8},{17,25},{24,0},{25,17},{2,26},{3,... | collective-permute-start | bytes 442376 | tf_op jit(solution)/shard_map/ppermute | solution.py:256
  76.5 0.0 collective-permute-done.5
  76.6 2.8 %collective-permute-start.6 = (bf16[304,256]{1,0:T(8,128)(2,1)S(1)}, bf16[304,256]{1,0:T(8,128)(2,1)S(1)}, u32[]{:S(2)}, u32[]{:S(2)}) collective-permute-start(bf16[304,256]{1,0:T(8,128)(2,1)S(1)} %fusion), channel_id=1, source_target_pairs={{0,24},{1,9},{8,16},{9,1},{16,8},{17,25},{24,0},{25,17},{2,26},{3,... | collective-permute-start | bytes 466952 | tf_op jit(solution)/shard_map/ppermute | solution.py:256
  79.4 3.2 %collective-permute-done.4 = bf16[288,256]{1,0:T(8,128)(2,1)S(1)} collective-permute-done((bf16[288,256]{1,0:T(8,128)(2,1)S(1)}, bf16[288,256]{1,0:T(8,128)(2,1)S(1)}, u32[]{:S(2)}, u32[]{:S(2)}) %collective-permute-start.4) | collective-permute-done | bytes 147488 | tf_op jit(solution)/shard_map/ppermute | solution.py:256
  82.6 7.2 %collective-permute-done.6 = bf16[304,256]{1,0:T(8,128)(2,1)S(1)} collective-permute-done((bf16[304,256]{1,0:T(8,128)(2,1)S(1)}, bf16[304,256]{1,0:T(8,128)(2,1)S(1)}, u32[]{:S(2)}, u32[]{:S(2)}) %collective-permute-start.6) | collective-permute-done | bytes 155680 | tf_op jit(solution)/shard_map/ppermute | solution.py:256
  89.8 0.1 fusion.4
  89.9 6.3 %collective-permute-start.7 = (bf16[592,256]{1,0:T(8,128)(2,1)S(1)}, bf16[592,256]{1,0:T(8,128)(2,1)S(1)}, u32[]{:S(2)}, u32[]{:S(2)}) collective-permute-start(bf16[592,256]{1,0:T(8,128)(2,1)S(1)} %pad_maximum_fusion.2), channel_id=1, source_target_pairs={{0,1},{1,0},{2,3},{3,2},{4,5},{5,4},{6,7},{7,6},{8,9},{9,8},{10,11... | collective-permute-start | bytes 909320 | tf_op jit(solution)/shard_map/ppermute | solution.py:246
  96.3 1.1 collective-permute-done.7.other_ref
  97.4 0.0 copy-start.1
  97.4 4.5 %shard_map.42 = bf16[16,104,128]{2,1,0:T(8,128)(2,1)} custom-call(s32[1]{0:T(128)} %bitcast.core_ref, f32[592,256]{1,0:T(8,128)S(1)} %pad_maximum_fusion.own_ref, bf16[592,256]{1,0:T(8,128)(2,1)S(1)} %collective-permute-done.7.other_ref, bf16[256,768]{1,0:T(8,128)(2,1)S(1)} %bitcast.16), custom_call_target="tpu_custom_call" | custom-call | flops 3321888768 | bytes 2555904 | tf_op jit(solution)/shard_map/pallas_call | solution.py:192
  101.9 4.2 %all-to-all-start.1 = ((bf16[16,104,128]{2,1,0:T(8,128)(2,1)}), bf16[16,104,128]{2,1,0:T(8,128)(2,1)S(1)}, u32[]{:S(2)}, u32[]{:S(2)}) async-start(bf16[16,104,128]{2,1,0:T(8,128)(2,1)} %shard_map.42), calls=%async_computation.1 | async-start | bytes 851968 | tf_op jit(solution)/shard_map/all_to_all | solution.py:293
  106.2 0.0 copy-done.1
  106.2 0.1 fusion.2
  106.2 0.7 copy.5.hit_ref
  106.9 10.8 %all-to-all-done.1.back_ref = bf16[16,104,128]{2,1,0:T(8,128)(2,1)S(1)} async-done(((bf16[16,104,128]{2,1,0:T(8,128)(2,1)}), bf16[16,104,128]{2,1,0:T(8,128)(2,1)S(1)}, u32[]{:S(2)}, u32[]{:S(2)}) %all-to-all-start.1) | async-done | bytes 426016 | tf_op jit(solution)/shard_map/all_to_all | solution.py:293
  117.7 0.0 copy-start
  117.7 0.8 copy-done
  118.5 1.8 %shard_map.43 = (bf16[16,16,768]{2,1,0:T(8,128)(2,1)}, f32[1,1]{1,0:T(1,128)}) custom-call(bf16[16,104,128]{2,1,0:T(8,128)(2,1)} %copy-done, s32[16,1,1]{2,1,0:T(1,128)} %copy.5.hit_ref), custom_call_target="tpu_custom_call" | custom-call | tf_op jit(solution)/shard_map/pallas_call | solution.py:228
  (9 shorter events, 0.3 us)
Async XLA Ops:
  0.6 31.5 %all-to-all-start = ((bf16[32,2,16,768]{3,2,1,0:T(8,128)(2,1)}), bf16[32,2,16,768]{3,2,1,0:T(8,128)(2,1)S(1)}, u32[]{:S(2)}, u32[]{:S(2)}) async-start(bf16[32,2,16,768]{3,2,1,0:T(8,128)(2,1)} %bitcast.20), calls=%async_computation | async-start | bytes 3145728 | tf_op jit(solution)/shard_map/all_to_all | solution.py:270
  32.6 13.4 %collective-permute-start = (bf16[8,16,768]{2,1,0:T(8,128)(2,1)S(1)}, bf16[8,16,768]{2,1,0:T(8,128)(2,1)S(1)}, u32[]{:S(2)}, u32[]{:S(2)}) collective-permute-start(bf16[8,16,768]{2,1,0:T(8,128)(2,1)S(1)} %get-tuple-element.6), channel_id=1, source_target_pairs={{0,4},{4,0},{1,5},{5,1},{2,6},{6,2},{3,7},{7,3},{8,12},{12,8},{9,1... | collective-permute-start | bytes 589832 | tf_op jit(solution)/shard_map/ppermute | solution.py:246
  39.2 10.2 %collective-permute-start.1 = (bf16[128,768]{1,0:T(8,128)(2,1)S(1)}, bf16[128,768]{1,0:T(8,128)(2,1)S(1)}, u32[]{:S(2)}, u32[]{:S(2)}) collective-permute-start(bf16[128,768]{1,0:T(8,128)(2,1)S(1)} %bitcast.14), channel_id=1, source_target_pairs={{0,1},{1,0},{2,3},{3,2},{4,5},{5,4},{6,7},{7,6},{8,9},{9,8},{10,11... | collective-permute-start | bytes 589832 | tf_op jit(solution)/shard_map/ppermute | solution.py:246
  46.0 4.5 %collective-permute-start.2 = (bf16[128,768]{1,0:T(8,128)(2,1)S(1)}, bf16[128,768]{1,0:T(8,128)(2,1)S(1)}, u32[]{:S(2)}, u32[]{:S(2)}) collective-permute-start(bf16[128,768]{1,0:T(8,128)(2,1)S(1)} %bitcast.17), channel_id=1, source_target_pairs={{0,1},{1,0},{2,3},{3,2},{4,5},{5,4},{6,7},{7,6},{8,9},{9,8},{10,11... | collective-permute-start | bytes 589832 | tf_op jit(solution)/shard_map/ppermute | solution.py:246
  51.2 15.9 %collective-permute-start.3 = (bf16[288,256]{1,0:T(8,128)(2,1)S(1)}, bf16[288,256]{1,0:T(8,128)(2,1)S(1)}, u32[]{:S(2)}, u32[]{:S(2)}) collective-permute-start(bf16[288,256]{1,0:T(8,128)(2,1)S(1)} %slice.13), channel_id=1, source_target_pairs={{0,8},{1,25},{8,0},{9,17},{16,24},{17,9},{24,16},{25,1},{2,10},{3,... | collective-permute-start | bytes 442376 | tf_op jit(solution)/shard_map/ppermute | solution.py:256
  62.1 14.4 %collective-permute-start.5 = (bf16[304,256]{1,0:T(8,128)(2,1)S(1)}, bf16[304,256]{1,0:T(8,128)(2,1)S(1)}, u32[]{:S(2)}, u32[]{:S(2)}) collective-permute-start(bf16[304,256]{1,0:T(8,128)(2,1)S(1)} %slice.15), channel_id=1, source_target_pairs={{0,8},{1,25},{8,0},{9,17},{16,24},{17,9},{24,16},{25,1},{2,10},{3,... | collective-permute-start | bytes 466952 | tf_op jit(solution)/shard_map/ppermute | solution.py:256
  67.1 15.5 %collective-permute-start.4 = (bf16[288,256]{1,0:T(8,128)(2,1)S(1)}, bf16[288,256]{1,0:T(8,128)(2,1)S(1)}, u32[]{:S(2)}, u32[]{:S(2)}) collective-permute-start(bf16[288,256]{1,0:T(8,128)(2,1)S(1)} %fusion.1), channel_id=1, source_target_pairs={{0,24},{1,9},{8,16},{9,1},{16,8},{17,25},{24,0},{25,17},{2,26},{3,... | collective-permute-start | bytes 442376 | tf_op jit(solution)/shard_map/ppermute | solution.py:256
  76.6 13.3 %collective-permute-start.6 = (bf16[304,256]{1,0:T(8,128)(2,1)S(1)}, bf16[304,256]{1,0:T(8,128)(2,1)S(1)}, u32[]{:S(2)}, u32[]{:S(2)}) collective-permute-start(bf16[304,256]{1,0:T(8,128)(2,1)S(1)} %fusion), channel_id=1, source_target_pairs={{0,24},{1,9},{8,16},{9,1},{16,8},{17,25},{24,0},{25,17},{2,26},{3,... | collective-permute-start | bytes 466952 | tf_op jit(solution)/shard_map/ppermute | solution.py:256
  89.9 7.5 %collective-permute-start.7 = (bf16[592,256]{1,0:T(8,128)(2,1)S(1)}, bf16[592,256]{1,0:T(8,128)(2,1)S(1)}, u32[]{:S(2)}, u32[]{:S(2)}) collective-permute-start(bf16[592,256]{1,0:T(8,128)(2,1)S(1)} %pad_maximum_fusion.2), channel_id=1, source_target_pairs={{0,1},{1,0},{2,3},{3,2},{4,5},{5,4},{6,7},{7,6},{8,9},{9,8},{10,11... | collective-permute-start | bytes 909320 | tf_op jit(solution)/shard_map/ppermute | solution.py:246
  97.4 8.8 %copy-start.1 = (s32[64]{0:T(128)S(1)}, s32[64]{0:T(128)}, u32[]{:S(2)}) copy-start(s32[64]{0:T(128)} %param.3) | copy-start | bytes 772
  101.9 15.8 %all-to-all-start.1 = ((bf16[16,104,128]{2,1,0:T(8,128)(2,1)}), bf16[16,104,128]{2,1,0:T(8,128)(2,1)S(1)}, u32[]{:S(2)}, u32[]{:S(2)}) async-start(bf16[16,104,128]{2,1,0:T(8,128)(2,1)} %shard_map.42), calls=%async_computation.1 | async-start | bytes 851968 | tf_op jit(solution)/shard_map/all_to_all | solution.py:293
  117.7 0.8 copy-start

commit v5 on v4

--- a/solution.py
+++ b/solution.py
@@ -117,12 +117,20 @@
     )(core, *pieces)
 
 
-def polynomial_kernel(scale, core_ref, own_ref, other_ref, x_ref, slab_ref, wide, g, p, s):
+def polynomial_kernel(scale, core_ref, *refs):
+    own_refs, other_refs, (x_ref, slab_ref, both, wide, g, p, s) = refs[:2], refs[2:4], refs[4:]
     width = g.shape[0]
     core = core_ref[0]
+    at = 0
+    for own_ref, other_ref in zip(own_refs, other_refs):
+        span = slice(at, at + own_ref.shape[0])
+        at = span.stop
+        own, other = own_ref[...], other_ref[...].astype(F32)
+        both[0, span, :] = jnp.where(core == 0, own, other)
+        both[1, span, :] = jnp.where(core == 0, other, own)
 
     def pick(half, span):
-        return jnp.where(core == half, own_ref[span, :], other_ref[span, :].astype(F32))
+        return both[half, span, :]
 
     def place(i, j, value, size=TILE):
         wide[i * size : i * size + value.shape[0], j * size : j * size + value.shape[1]] = value
@@ -185,23 +193,29 @@
     slab_ref[:, high - NOTE :, :] = jnp.broadcast_to(note, (blocks, NOTE, LANES))
 
 
-def polynomial(core, own, other, x, full_rows, blocks):
+def polynomial(core, owns, others, x, full_rows, blocks):
     rows, width = x.shape
     mat = pltpu.VMEM((width, width), BF16)
     high = rows // blocks * width // LANES + NOTE
     return pl.pallas_call(
         functools.partial(polynomial_kernel, math.sqrt(full_rows)),
         out_shape=jax.ShapeDtypeStruct((blocks, high, LANES), BF16),
-        in_specs=[SMEM, VMEM, VMEM, VMEM],
+        in_specs=[SMEM] + [VMEM] * 5,
         out_specs=VMEM,
-        scratch_shapes=[pltpu.VMEM((width, width), F32), mat, mat, mat],
+        scratch_shapes=[
+            pltpu.VMEM((2, HALF, TILE), F32),
+            pltpu.VMEM((width, width), F32),
+            mat,
+            mat,
+            mat,
+        ],
         compiler_params=pltpu.CompilerParams(vmem_limit_bytes=32 * 2**20),
         cost_estimate=pl.CostEstimate(
             flops=6 * width**3 + 4 * rows * width * width,
             bytes_accessed=width * width * 3 + rows * width * 4,
             transcendentals=0,
         ),
-    )(core, own, other, x)
+    )(core, *owns, *others, x)
 
 
 def place_kernel(count, back_ref, hit_ref, out_ref, rms_ref):
@@ -256,7 +270,32 @@
     return lax.ppermute(value, (axis, "core"), pairs)
 
 
-def on_device(grads, owners):
+def swap_windows(value):
+    z_n = lax.axis_size("zh") * 4
+    pairs = []
+    for z in range(z_n):
+        up = z % 4 // 2
+        for core in range(2):
+            other = z + 2 if up == core else z - 2
+            pairs.append((z * 2 + core, other % z_n * 2 + core))
+    return lax.ppermute(value, FSDP[1:], pairs)
+
+
+def window_groups(fsdp_n):
+    z_n = fsdp_n // 8
+    return [
+        [
+            (y * z_n + (first + 2 * (zm + 2 * core * (1 - zm)) + zb) % z_n) * 2 + core
+            for y in range(4)
+            for zb in range(2)
+            for zm in range(2)
+        ]
+        for first in range(0, z_n, 4)
+        for core in range(2)
+    ]
+
+
+def on_device(grads):
     block = grads[0]
     mats, rows_dev, width = block.shape
     dp_n, y_n, core_n = lax.axis_size("dp"), lax.axis_size("y"), lax.axis_size("core")
@@ -274,7 +313,7 @@
         part = lax.dynamic_index_in_dim(slabs, which, 2, keepdims=False)
         return jnp.sum(part.astype(F32), axis=0).astype(BF16)
 
-    away = shift(summed(1 - mid), "zm", 1)
+    away = swap_windows(summed(1 - mid))
     here = summed(mid)
     mine = jnp.stack([jnp.where(mid == 0, here, away), jnp.where(mid == 0, away, here)], axis=1)
     mine = mine.reshape(mats_dp * rows_dev, width)
@@ -288,15 +327,18 @@
         came = [neighbour(part, "zh", turn) for part in sents]
         totals = [part + other.astype(F32) for part, other in zip(totals, came)]
         sents = [part.astype(BF16) for part in totals]
-    total, sent = jnp.concatenate(totals), jnp.concatenate(sents)
-    slab = polynomial(core, total, shift(sent, "core", 1), mine, full_rows, mats_dp)
-    back = lax.all_to_all(slab, ("y", "zb", "zm"), 0, 0, tiled=True)
-
-    index = jnp.zeros((), jnp.int32)
-    for axis in FSDP:
-        index = index * lax.axis_size(axis) + lax.axis_index(axis)
+    others = [shift(part, "core", 1) for part in sents]
+    slab = polynomial(core, totals, others, mine, full_rows, mats_dp)
+    return slab
+
+
+def placed(slab, owners, rows_dev, width, full_rows):
+    groups = window_groups(lax.axis_size("fsdp"))
+    back = lax.all_to_all(slab, "fsdp", 0, 0, axis_index_groups=groups, tiled=True)
+    mats_dp = back.shape[0]
+    index = lax.axis_index("fsdp")
     owned = lax.dynamic_slice_in_dim(owners, lax.axis_index("dp") * mats_dp, mats_dp)
-    hits = owned == index - index % core_n
+    hits = owned == index - index % 2
     return place(back, hits, rows_dev, width, full_rows)
 
 
@@ -304,8 +346,24 @@
     dp_n, fsdp_n = mesh.devices.shape
     shape = (dp_n, 4, fsdp_n // 32, 2, 2, 2)
     grid = Mesh(mesh.devices.reshape(shape), ("dp", *FSDP))
-    in_specs = (P("dp", None, FSDP, None), P())
-    out_specs = (P("dp", FSDP, None), P("dp", FSDP))
-    return jax.shard_map(
-        on_device, mesh=grid, in_specs=in_specs, out_specs=out_specs, check_vma=False
-    )
+
+    def run(grads, owners):
+        full_rows, width = grads.shape[2:]
+        slabs = jax.shard_map(
+            on_device,
+            mesh=grid,
+            in_specs=P("dp", None, FSDP, None),
+            out_specs=P(("dp", *FSDP)),
+            check_vma=False,
+        )(grads)
+        return jax.shard_map(
+            functools.partial(
+                placed, rows_dev=full_rows // fsdp_n, width=width, full_rows=full_rows
+            ),
+            mesh=mesh,
+            in_specs=(P(("dp", "fsdp")), P()),
+            out_specs=(P("dp", "fsdp", None), P("dp", "fsdp")),
+            check_vma=False,
+        )(slabs, owners)
+
+    return run

time: 122 us -> 120 us (0.984)
  waiting for transfers between devices: 50.8 us -> 42.4 us
  starting transfers between devices: 59.4 us -> 65.8 us
    ppermute x0 -> x1, starting transfers between devices: none -> 12.4 us  [swap_windows(): return lax.ppermute(value, FSDP[1:], pairs)]
    ppermute x4, waiting for transfers between devices: 13.4 us -> 5.07 us  [neighbour(): return lax.ppermute(value, (axis, 'core'), pairs)]
    ppermute x4, starting transfers between devices: 20.9 us -> 16.3 us  [shift(): lax.ppermute(value, axis, [(i, (i + distance) % n) for i in range(n)])]
    ppermute x4, starting transfers between devices: 25 us -> 22.5 us  [neighbour(): return lax.ppermute(value, (axis, 'core'), pairs)]
    ppermute x0 -> x1, waiting for transfers between devices: none -> 2.37 us  [swap_windows(): return lax.ppermute(value, FSDP[1:], pairs)]
    ppermute x4, waiting for transfers between devices: 4.38 us -> 2.3 us  [shift(): lax.ppermute(value, axis, [(i, (i + distance) % n) for i in range(n)])]
  transfers between devices with their start and end apart: 10 -> 11, of which waited for: 8 -> 6; matrix products, arithmetic and copies ran while one was open for 1% -> 1% of each run, Pallas kernels for 0% -> 0%
where the time goes in v5:
time: 120 us; the launch traced here: 118 us
  starting transfers between devices  65.8 us (55%)
  waiting for transfers between devices  42.4 us (35%)
  Pallas kernels  7.01 us (6%)
  local copies, waits for them, and re-layouts  1.47 us (1%)
    ppermute x4, starting transfers between devices, neighbour(): return lax.ppermute(value, (axis, 'core'), pairs)  22.5 us
    all_to_all x1, waiting for transfers between devices, on_device(): slabs = lax.all_to_all(slabs, ('dp', 'y', 'zb'), 0, 0, tiled=True)  22.3 us
    ppermute x4, starting transfers between devices, shift(): lax.ppermute(value, axis, [(i, (i + distance) % n) for i in range(n)])  16.3 us
    ppermute x1, starting transfers between devices, swap_windows(): return lax.ppermute(value, FSDP[1:], pairs)  12.4 us
    all_to_all x1, waiting for transfers between devices, placed(): lax.all_to_all(slab, 'fsdp', 0, 0, axis_index_groups=groups, tiled=True)  10.4 us
    all_to_all x1, starting transfers between devices, on_device(): slabs = lax.all_to_all(slabs, ('dp', 'y', 'zb'), 0, 0, tiled=True)  9.24 us
    all_to_all x1, starting transfers between devices, placed(): lax.all_to_all(slab, 'fsdp', 0, 0, axis_index_groups=groups, tiled=True)  5.4 us
    ppermute x4, waiting for transfers between devices, neighbour(): return lax.ppermute(value, (axis, 'core'), pairs)  5.07 us
  transfers between devices with their start and end apart: 11, of which 6 were waited for; matrix products, arithmetic and copies ran while one was open for 1% of the time, Pallas kernels for 0%

profile of v5, /device:TPU:1, one launch (start us, length us, event | category | flops | bytes accessed | tf_op | source)
XLA Modules:
  0.0 118.3 jit_solution(17863914936630449442)
XLA Ops:
  0.6 9.2 %all-to-all-start = ((bf16[32,2,16,768]{3,2,1,0:T(8,128)(2,1)}), bf16[32,2,16,768]{3,2,1,0:T(8,128)(2,1)S(1)}, u32[]{:S(2)}, u32[]{:S(2)}) async-start(bf16[32,2,16,768]{3,2,1,0:T(8,128)(2,1)} %bitcast.20), calls=%async_computation | async-start | bytes 3145728 | tf_op jit(solution)/shard_map/all_to_all | solution.py:309
  9.9 22.3 %all-to-all-done = bf16[32,2,16,768]{3,2,1,0:T(8,128)(2,1)S(1)} async-done(((bf16[32,2,16,768]{3,2,1,0:T(8,128)(2,1)}), bf16[32,2,16,768]{3,2,1,0:T(8,128)(2,1)S(1)}, u32[]{:S(2)}, u32[]{:S(2)}) %all-to-all-start) | async-done | bytes 1572896 | tf_op jit(solution)/shard_map/all_to_all | solution.py:309
  32.1 0.4 dynamic-slice_reduce_fusion
  32.6 12.4 %collective-permute-start = (bf16[8,16,768]{2,1,0:T(8,128)(2,1)S(1)}, bf16[8,16,768]{2,1,0:T(8,128)(2,1)S(1)}, u32[]{:S(2)}, u32[]{:S(2)}) collective-permute-start(bf16[8,16,768]{2,1,0:T(8,128)(2,1)S(1)} %get-tuple-element.7), channel_id=1, source_target_pairs={{0,4},{1,29},{2,6},{3,31},{4,0},{5,9},{6,2},{7,11},{8,12},{9,5},{1... | collective-permute-start | bytes 589832 | tf_op jit(solution)/shard_map/ppermute | solution.py:281
  45.0 1.9 %collective-permute-start.1 = (bf16[128,768]{1,0:T(8,128)(2,1)S(1)}, bf16[128,768]{1,0:T(8,128)(2,1)S(1)}, u32[]{:S(2)}, u32[]{:S(2)}) collective-permute-start(bf16[128,768]{1,0:T(8,128)(2,1)S(1)} %bitcast.14), channel_id=1, source_target_pairs={{0,1},{1,0},{2,3},{3,2},{4,5},{5,4},{6,7},{7,6},{8,9},{9,8},{10,11... | collective-permute-start | bytes 589832 | tf_op jit(solution)/shard_map/ppermute | solution.py:260
  46.9 2.4 %collective-permute-done = bf16[8,16,768]{2,1,0:T(8,128)(2,1)S(1)} collective-permute-done((bf16[8,16,768]{2,1,0:T(8,128)(2,1)S(1)}, bf16[8,16,768]{2,1,0:T(8,128)(2,1)S(1)}, u32[]{:S(2)}, u32[]{:S(2)}) %collective-permute-start) | collective-permute-done | bytes 196640 | tf_op jit(solution)/shard_map/ppermute | solution.py:281
  49.3 1.9 %collective-permute-start.2 = (bf16[128,768]{1,0:T(8,128)(2,1)S(1)}, bf16[128,768]{1,0:T(8,128)(2,1)S(1)}, u32[]{:S(2)}, u32[]{:S(2)}) collective-permute-start(bf16[128,768]{1,0:T(8,128)(2,1)S(1)} %bitcast.17), channel_id=1, source_target_pairs={{0,1},{1,0},{2,3},{3,2},{4,5},{5,4},{6,7},{7,6},{8,9},{9,8},{10,11... | collective-permute-start | bytes 589832 | tf_op jit(solution)/shard_map/ppermute | solution.py:260
  51.2 0.0 collective-permute-done.1.refs_2_
  51.2 1.4 %collective-permute-done.2.refs_3_ = bf16[128,768]{1,0:T(8,128)(2,1)S(1)} collective-permute-done((bf16[128,768]{1,0:T(8,128)(2,1)S(1)}, bf16[128,768]{1,0:T(8,128)(2,1)S(1)}, u32[]{:S(2)}, u32[]{:S(2)}) %collective-permute-start.2) | collective-permute-done | bytes 196640 | tf_op jit(solution)/shard_map/ppermute | solution.py:260
  52.6 0.6 shard_map.58
  53.3 8.1 %collective-permute-start.3 = (bf16[288,256]{1,0:T(8,128)(2,1)S(1)}, bf16[288,256]{1,0:T(8,128)(2,1)S(1)}, u32[]{:S(2)}, u32[]{:S(2)}) collective-permute-start(bf16[288,256]{1,0:T(8,128)(2,1)S(1)} %slice.13), channel_id=1, source_target_pairs={{0,8},{1,25},{8,0},{9,17},{16,24},{17,9},{24,16},{25,1},{2,10},{3,... | collective-permute-start | bytes 442376 | tf_op jit(solution)/shard_map/ppermute | solution.py:270
  61.4 1.9 %collective-permute-start.5 = (bf16[304,256]{1,0:T(8,128)(2,1)S(1)}, bf16[304,256]{1,0:T(8,128)(2,1)S(1)}, u32[]{:S(2)}, u32[]{:S(2)}) collective-permute-start(bf16[304,256]{1,0:T(8,128)(2,1)S(1)} %slice.15), channel_id=1, source_target_pairs={{0,8},{1,25},{8,0},{9,17},{16,24},{17,9},{24,16},{25,1},{2,10},{3,... | collective-permute-start | bytes 466952 | tf_op jit(solution)/shard_map/ppermute | solution.py:270
  63.3 5.0 %collective-permute-done.3 = bf16[288,256]{1,0:T(8,128)(2,1)S(1)} collective-permute-done((bf16[288,256]{1,0:T(8,128)(2,1)S(1)}, bf16[288,256]{1,0:T(8,128)(2,1)S(1)}, u32[]{:S(2)}, u32[]{:S(2)}) %collective-permute-start.3) | collective-permute-done | bytes 147488 | tf_op jit(solution)/shard_map/ppermute | solution.py:270
  68.4 5.8 %collective-permute-start.4 = (bf16[288,256]{1,0:T(8,128)(2,1)S(1)}, bf16[288,256]{1,0:T(8,128)(2,1)S(1)}, u32[]{:S(2)}, u32[]{:S(2)}) collective-permute-start(bf16[288,256]{1,0:T(8,128)(2,1)S(1)} %fusion.1), channel_id=1, source_target_pairs={{0,24},{1,9},{8,16},{9,1},{16,8},{17,25},{24,0},{25,17},{2,26},{3,... | collective-permute-start | bytes 442376 | tf_op jit(solution)/shard_map/ppermute | solution.py:270
  74.2 0.0 collective-permute-done.5
  74.2 6.7 %collective-permute-start.6 = (bf16[304,256]{1,0:T(8,128)(2,1)S(1)}, bf16[304,256]{1,0:T(8,128)(2,1)S(1)}, u32[]{:S(2)}, u32[]{:S(2)}) collective-permute-start(bf16[304,256]{1,0:T(8,128)(2,1)S(1)} %fusion), channel_id=1, source_target_pairs={{0,24},{1,9},{8,16},{9,1},{16,8},{17,25},{24,0},{25,17},{2,26},{3,... | collective-permute-start | bytes 466952 | tf_op jit(solution)/shard_map/ppermute | solution.py:270
  80.9 0.0 collective-permute-done.4
  81.0 5.8 %collective-permute-start.7 = (bf16[288,256]{1,0:T(8,128)(2,1)S(1)}, bf16[288,256]{1,0:T(8,128)(2,1)S(1)}, u32[]{:S(2)}, u32[]{:S(2)}) collective-permute-start(bf16[288,256]{1,0:T(8,128)(2,1)S(1)} %get-tuple-element.11), channel_id=1, source_target_pairs={{0,1},{1,0},{2,3},{3,2},{4,5},{5,4},{6,7},{7,6},{8,9},{9,8},{10,11... | collective-permute-start | bytes 442376 | tf_op jit(solution)/shard_map/ppermute | solution.py:260
  86.8 0.0 collective-permute-done.6
  86.8 0.1 fusion.3
  86.9 6.7 %collective-permute-start.8 = (bf16[304,256]{1,0:T(8,128)(2,1)S(1)}, bf16[304,256]{1,0:T(8,128)(2,1)S(1)}, u32[]{:S(2)}, u32[]{:S(2)}) collective-permute-start(bf16[304,256]{1,0:T(8,128)(2,1)S(1)} %get-tuple-element.9), channel_id=1, source_target_pairs={{0,1},{1,0},{2,3},{3,2},{4,5},{5,4},{6,7},{7,6},{8,9},{9,8},{10,11... | collective-permute-start | bytes 466952 | tf_op jit(solution)/shard_map/ppermute | solution.py:260
  93.7 0.0 collective-permute-done.7.refs_2_
  93.7 0.9 collective-permute-done.8.refs_3_
  94.6 0.0 copy-start.1
  94.6 4.6 %shard_map.59 = bf16[16,104,128]{2,1,0:T(8,128)(2,1)} custom-call(s32[1]{0:T(128)} %bitcast.core_ref, f32[288,256]{1,0:T(8,128)S(1)} %get-tuple-element.12.refs_0_, f32[304,256]{1,0:T(8,128)S(1)} %get-tuple-element.10.refs_1_, bf16[288,256]{1,0:T(8,128)(2,1)S(1)} %collective-permute-done.7.refs_2_, bf16[304,256]{1,0:T(8,128)(2,1)S(1)} %collective-permute-done.8.refs_3_, ...), custom_call_target="tpu_custom_call" | custom-call | flops 3321888768 | bytes 2555904 | tf_op jit(solution)/shard_map/pallas_call | solution.py:200
  99.1 5.4 %all-to-all-start.1 = ((bf16[16,104,128]{2,1,0:T(8,128)(2,1)}), bf16[16,104,128]{2,1,0:T(8,128)(2,1)S(1)}, u32[]{:S(2)}, u32[]{:S(2)}) async-start(bf16[16,104,128]{2,1,0:T(8,128)(2,1)} %shard_map.59), calls=%async_computation.1 | async-start | bytes 851968 | tf_op jit(solution)/shard_map/all_to_all | solution.py:337
  104.6 0.0 copy-done.1
  104.6 0.1 fusion.2
  104.6 0.7 copy.7.hit_ref
  105.3 10.4 %all-to-all-done.1.back_ref = bf16[16,104,128]{2,1,0:T(8,128)(2,1)S(1)} async-done(((bf16[16,104,128]{2,1,0:T(8,128)(2,1)}), bf16[16,104,128]{2,1,0:T(8,128)(2,1)S(1)}, u32[]{:S(2)}, u32[]{:S(2)}) %all-to-all-start.1) | async-done | bytes 426016 | tf_op jit(solution)/shard_map/all_to_all | solution.py:337
  115.7 0.8 copy-done
  116.5 1.8 %shard_map.60 = (bf16[16,16,768]{2,1,0:T(8,128)(2,1)}, f32[1,1]{1,0:T(1,128)}) custom-call(bf16[16,104,128]{2,1,0:T(8,128)(2,1)} %copy-done, s32[16,1,1]{2,1,0:T(1,128)} %copy.7.hit_ref), custom_call_target="tpu_custom_call" | custom-call | tf_op jit(solution)/shard_map/pallas_call | solution.py:242
  (8 shorter events, 0.2 us)
Async XLA Ops:
  0.6 31.5 %all-to-all-start = ((bf16[32,2,16,768]{3,2,1,0:T(8,128)(2,1)}), bf16[32,2,16,768]{3,2,1,0:T(8,128)(2,1)S(1)}, u32[]{:S(2)}, u32[]{:S(2)}) async-start(bf16[32,2,16,768]{3,2,1,0:T(8,128)(2,1)} %bitcast.20), calls=%async_computation | async-start | bytes 3145728 | tf_op jit(solution)/shard_map/all_to_all | solution.py:309
  32.6 16.7 %collective-permute-start = (bf16[8,16,768]{2,1,0:T(8,128)(2,1)S(1)}, bf16[8,16,768]{2,1,0:T(8,128)(2,1)S(1)}, u32[]{:S(2)}, u32[]{:S(2)}) collective-permute-start(bf16[8,16,768]{2,1,0:T(8,128)(2,1)S(1)} %get-tuple-element.7), channel_id=1, source_target_pairs={{0,4},{1,29},{2,6},{3,31},{4,0},{5,9},{6,2},{7,11},{8,12},{9,5},{1... | collective-permute-start | bytes 589832 | tf_op jit(solution)/shard_map/ppermute | solution.py:281
  45.0 6.2 %collective-permute-start.1 = (bf16[128,768]{1,0:T(8,128)(2,1)S(1)}, bf16[128,768]{1,0:T(8,128)(2,1)S(1)}, u32[]{:S(2)}, u32[]{:S(2)}) collective-permute-start(bf16[128,768]{1,0:T(8,128)(2,1)S(1)} %bitcast.14), channel_id=1, source_target_pairs={{0,1},{1,0},{2,3},{3,2},{4,5},{5,4},{6,7},{7,6},{8,9},{9,8},{10,11... | collective-permute-start | bytes 589832 | tf_op jit(solution)/shard_map/ppermute | solution.py:260
  49.3 3.3 %collective-permute-start.2 = (bf16[128,768]{1,0:T(8,128)(2,1)S(1)}, bf16[128,768]{1,0:T(8,128)(2,1)S(1)}, u32[]{:S(2)}, u32[]{:S(2)}) collective-permute-start(bf16[128,768]{1,0:T(8,128)(2,1)S(1)} %bitcast.17), channel_id=1, source_target_pairs={{0,1},{1,0},{2,3},{3,2},{4,5},{5,4},{6,7},{7,6},{8,9},{9,8},{10,11... | collective-permute-start | bytes 589832 | tf_op jit(solution)/shard_map/ppermute | solution.py:260
  53.3 15.1 %collective-permute-start.3 = (bf16[288,256]{1,0:T(8,128)(2,1)S(1)}, bf16[288,256]{1,0:T(8,128)(2,1)S(1)}, u32[]{:S(2)}, u32[]{:S(2)}) collective-permute-start(bf16[288,256]{1,0:T(8,128)(2,1)S(1)} %slice.13), channel_id=1, source_target_pairs={{0,8},{1,25},{8,0},{9,17},{16,24},{17,9},{24,16},{25,1},{2,10},{3,... | collective-permute-start | bytes 442376 | tf_op jit(solution)/shard_map/ppermute | solution.py:270
  61.4 12.8 %collective-permute-start.5 = (bf16[304,256]{1,0:T(8,128)(2,1)S(1)}, bf16[304,256]{1,0:T(8,128)(2,1)S(1)}, u32[]{:S(2)}, u32[]{:S(2)}) collective-permute-start(bf16[304,256]{1,0:T(8,128)(2,1)S(1)} %slice.15), channel_id=1, source_target_pairs={{0,8},{1,25},{8,0},{9,17},{16,24},{17,9},{24,16},{25,1},{2,10},{3,... | collective-permute-start | bytes 466952 | tf_op jit(solution)/shard_map/ppermute | solution.py:270
  68.4 12.6 %collective-permute-start.4 = (bf16[288,256]{1,0:T(8,128)(2,1)S(1)}, bf16[288,256]{1,0:T(8,128)(2,1)S(1)}, u32[]{:S(2)}, u32[]{:S(2)}) collective-permute-start(bf16[288,256]{1,0:T(8,128)(2,1)S(1)} %fusion.1), channel_id=1, source_target_pairs={{0,24},{1,9},{8,16},{9,1},{16,8},{17,25},{24,0},{25,17},{2,26},{3,... | collective-permute-start | bytes 442376 | tf_op jit(solution)/shard_map/ppermute | solution.py:270
  74.2 12.6 %collective-permute-start.6 = (bf16[304,256]{1,0:T(8,128)(2,1)S(1)}, bf16[304,256]{1,0:T(8,128)(2,1)S(1)}, u32[]{:S(2)}, u32[]{:S(2)}) collective-permute-start(bf16[304,256]{1,0:T(8,128)(2,1)S(1)} %fusion), channel_id=1, source_target_pairs={{0,24},{1,9},{8,16},{9,1},{16,8},{17,25},{24,0},{25,17},{2,26},{3,... | collective-permute-start | bytes 466952 | tf_op jit(solution)/shard_map/ppermute | solution.py:270
  81.0 12.7 %collective-permute-start.7 = (bf16[288,256]{1,0:T(8,128)(2,1)S(1)}, bf16[288,256]{1,0:T(8,128)(2,1)S(1)}, u32[]{:S(2)}, u32[]{:S(2)}) collective-permute-start(bf16[288,256]{1,0:T(8,128)(2,1)S(1)} %get-tuple-element.11), channel_id=1, source_target_pairs={{0,1},{1,0},{2,3},{3,2},{4,5},{5,4},{6,7},{7,6},{8,9},{9,8},{10,11... | collective-permute-start | bytes 442376 | tf_op jit(solution)/shard_map/ppermute | solution.py:260
  86.9 7.7 %collective-permute-start.8 = (bf16[304,256]{1,0:T(8,128)(2,1)S(1)}, bf16[304,256]{1,0:T(8,128)(2,1)S(1)}, u32[]{:S(2)}, u32[]{:S(2)}) collective-permute-start(bf16[304,256]{1,0:T(8,128)(2,1)S(1)} %get-tuple-element.9), channel_id=1, source_target_pairs={{0,1},{1,0},{2,3},{3,2},{4,5},{5,4},{6,7},{7,6},{8,9},{9,8},{10,11... | collective-permute-start | bytes 466952 | tf_op jit(solution)/shard_map/ppermute | solution.py:260
  94.6 10.0 %copy-start.1 = (s32[64]{0:T(128)S(1)}, s32[64]{0:T(128)}, u32[]{:S(2)}) copy-start(s32[64]{0:T(128)} %param.4) | copy-start | bytes 772
  99.1 16.6 %all-to-all-start.1 = ((bf16[16,104,128]{2,1,0:T(8,128)(2,1)}), bf16[16,104,128]{2,1,0:T(8,128)(2,1)S(1)}, u32[]{:S(2)}, u32[]{:S(2)}) async-start(bf16[16,104,128]{2,1,0:T(8,128)(2,1)} %shard_map.59), calls=%async_computation.1 | async-start | bytes 851968 | tf_op jit(solution)/shard_map/all_to_all | solution.py:337
  115.7 0.8 copy-start

commit v6 on v5

--- a/solution.py
+++ b/solution.py
@@ -311,10 +311,10 @@
 
     def summed(which):
         part = lax.dynamic_index_in_dim(slabs, which, 2, keepdims=False)
-        return jnp.sum(part.astype(F32), axis=0).astype(BF16)
-
-    away = swap_windows(summed(1 - mid))
-    here = summed(mid)
+        return sum(part[i].astype(F32) for i in range(dp_n)).astype(BF16)
+
+    gone, here = lax.optimization_barrier((summed(1 - mid), summed(mid)))
+    away = swap_windows(gone)
     mine = jnp.stack([jnp.where(mid == 0, here, away), jnp.where(mid == 0, away, here)], axis=1)
     mine = mine.reshape(mats_dp * rows_dev, width)
     pieces = [part.reshape(-1, width) for part in (here, away)]

time: 120 us -> 120 us (level)
  no operation moved by 1% of the time
where the time goes in v6:
time: 120 us; the launch traced here: 118 us
  starting transfers between devices  65.8 us (55%)
  waiting for transfers between devices  42.4 us (35%)
  Pallas kernels  7.01 us (6%)
  local copies, waits for them, and re-layouts  1.51 us (1%)
    ppermute x4, starting transfers between devices, neighbour(): return lax.ppermute(value, (axis, 'core'), pairs)  22.5 us
    all_to_all x1, waiting for transfers between devices, on_device(): slabs = lax.all_to_all(slabs, ('dp', 'y', 'zb'), 0, 0, tiled=True)  22.3 us
    ppermute x4, starting transfers between devices, shift(): lax.ppermute(value, axis, [(i, (i + distance) % n) for i in range(n)])  16.3 us
    ppermute x1, starting transfers between devices, swap_windows(): return lax.ppermute(value, FSDP[1:], pairs)  12.4 us
    all_to_all x1, waiting for transfers between devices, placed(): lax.all_to_all(slab, 'fsdp', 0, 0, axis_index_groups=groups, tiled=True)  10.4 us
    all_to_all x1, starting transfers between devices, on_device(): slabs = lax.all_to_all(slabs, ('dp', 'y', 'zb'), 0, 0, tiled=True)  9.24 us
    all_to_all x1, starting transfers between devices, placed(): lax.all_to_all(slab, 'fsdp', 0, 0, axis_index_groups=groups, tiled=True)  5.41 us
    ppermute x4, waiting for transfers between devices, neighbour(): return lax.ppermute(value, (axis, 'core'), pairs)  5.07 us
  transfers between devices with their start and end apart: 11, of which 6 were waited for; matrix products, arithmetic and copies ran while one was open for 1% of the time, Pallas kernels for 0%

profile of v6, /device:TPU:1, one launch (start us, length us, event | category | flops | bytes accessed | tf_op | source)
XLA Modules:
  0.0 118.1 jit_solution(4697570789426489288)
XLA Ops:
  0.6 9.2 %all-to-all-start = ((bf16[32,2,16,768]{3,2,1,0:T(8,128)(2,1)}), bf16[32,2,16,768]{3,2,1,0:T(8,128)(2,1)S(1)}, u32[]{:S(2)}, u32[]{:S(2)}) async-start(bf16[32,2,16,768]{3,2,1,0:T(8,128)(2,1)} %bitcast.40), calls=%async_computation | async-start | bytes 3145728 | tf_op jit(solution)/shard_map/all_to_all | solution.py:309
  9.9 22.3 %all-to-all-done = bf16[32,2,16,768]{3,2,1,0:T(8,128)(2,1)S(1)} async-done(((bf16[32,2,16,768]{3,2,1,0:T(8,128)(2,1)}), bf16[32,2,16,768]{3,2,1,0:T(8,128)(2,1)S(1)}, u32[]{:S(2)}, u32[]{:S(2)}) %all-to-all-start) | async-done | bytes 1572896 | tf_op jit(solution)/shard_map/all_to_all | solution.py:309
  32.1 0.1 fusion.1
  32.3 0.1 fusion.2
  32.4 12.4 %collective-permute-start = (bf16[8,16,768]{2,1,0:T(8,128)(2,1)S(1)}, bf16[8,16,768]{2,1,0:T(8,128)(2,1)S(1)}, u32[]{:S(2)}, u32[]{:S(2)}) collective-permute-start(bf16[8,16,768]{2,1,0:T(8,128)(2,1)S(1)} %fusion.1), channel_id=1, source_target_pairs={{0,4},{1,29},{2,6},{3,31},{4,0},{5,9},{6,2},{7,11},{8,12},{9,5},{1... | collective-permute-start | bytes 589832 | tf_op jit(solution)/shard_map/ppermute | solution.py:281
  44.8 1.9 %collective-permute-start.1 = (bf16[128,768]{1,0:T(8,128)(2,1)S(1)}, bf16[128,768]{1,0:T(8,128)(2,1)S(1)}, u32[]{:S(2)}, u32[]{:S(2)}) collective-permute-start(bf16[128,768]{1,0:T(8,128)(2,1)S(1)} %bitcast.33), channel_id=1, source_target_pairs={{0,1},{1,0},{2,3},{3,2},{4,5},{5,4},{6,7},{7,6},{8,9},{9,8},{10,11... | collective-permute-start | bytes 589832 | tf_op jit(solution)/shard_map/ppermute | solution.py:260
  46.8 2.4 %collective-permute-done = bf16[8,16,768]{2,1,0:T(8,128)(2,1)S(1)} collective-permute-done((bf16[8,16,768]{2,1,0:T(8,128)(2,1)S(1)}, bf16[8,16,768]{2,1,0:T(8,128)(2,1)S(1)}, u32[]{:S(2)}, u32[]{:S(2)}) %collective-permute-start) | collective-permute-done | bytes 196640 | tf_op jit(solution)/shard_map/ppermute | solution.py:281
  49.1 1.9 %collective-permute-start.2 = (bf16[128,768]{1,0:T(8,128)(2,1)S(1)}, bf16[128,768]{1,0:T(8,128)(2,1)S(1)}, u32[]{:S(2)}, u32[]{:S(2)}) collective-permute-start(bf16[128,768]{1,0:T(8,128)(2,1)S(1)} %bitcast.36), channel_id=1, source_target_pairs={{0,1},{1,0},{2,3},{3,2},{4,5},{5,4},{6,7},{7,6},{8,9},{9,8},{10,11... | collective-permute-start | bytes 589832 | tf_op jit(solution)/shard_map/ppermute | solution.py:260
  51.0 0.0 collective-permute-done.1.refs_2_
  51.0 1.4 %collective-permute-done.2.refs_3_ = bf16[128,768]{1,0:T(8,128)(2,1)S(1)} collective-permute-done((bf16[128,768]{1,0:T(8,128)(2,1)S(1)}, bf16[128,768]{1,0:T(8,128)(2,1)S(1)}, u32[]{:S(2)}, u32[]{:S(2)}) %collective-permute-start.2) | collective-permute-done | bytes 196640 | tf_op jit(solution)/shard_map/ppermute | solution.py:260
  52.4 0.6 shard_map.58
  53.1 8.1 %collective-permute-start.3 = (bf16[288,256]{1,0:T(8,128)(2,1)S(1)}, bf16[288,256]{1,0:T(8,128)(2,1)S(1)}, u32[]{:S(2)}, u32[]{:S(2)}) collective-permute-start(bf16[288,256]{1,0:T(8,128)(2,1)S(1)} %slice.53), channel_id=1, source_target_pairs={{0,8},{1,25},{8,0},{9,17},{16,24},{17,9},{24,16},{25,1},{2,10},{3,... | collective-permute-start | bytes 442376 | tf_op jit(solution)/shard_map/ppermute | solution.py:270
  61.2 1.9 %collective-permute-start.5 = (bf16[304,256]{1,0:T(8,128)(2,1)S(1)}, bf16[304,256]{1,0:T(8,128)(2,1)S(1)}, u32[]{:S(2)}, u32[]{:S(2)}) collective-permute-start(bf16[304,256]{1,0:T(8,128)(2,1)S(1)} %slice.55), channel_id=1, source_target_pairs={{0,8},{1,25},{8,0},{9,17},{16,24},{17,9},{24,16},{25,1},{2,10},{3,... | collective-permute-start | bytes 466952 | tf_op jit(solution)/shard_map/ppermute | solution.py:270
  63.1 5.0 %collective-permute-done.3 = bf16[288,256]{1,0:T(8,128)(2,1)S(1)} collective-permute-done((bf16[288,256]{1,0:T(8,128)(2,1)S(1)}, bf16[288,256]{1,0:T(8,128)(2,1)S(1)}, u32[]{:S(2)}, u32[]{:S(2)}) %collective-permute-start.3) | collective-permute-done | bytes 147488 | tf_op jit(solution)/shard_map/ppermute | solution.py:270
  68.2 5.8 %collective-permute-start.4 = (bf16[288,256]{1,0:T(8,128)(2,1)S(1)}, bf16[288,256]{1,0:T(8,128)(2,1)S(1)}, u32[]{:S(2)}, u32[]{:S(2)}) collective-permute-start(bf16[288,256]{1,0:T(8,128)(2,1)S(1)} %fusion.3), channel_id=1, source_target_pairs={{0,24},{1,9},{8,16},{9,1},{16,8},{17,25},{24,0},{25,17},{2,26},{3,... | collective-permute-start | bytes 442376 | tf_op jit(solution)/shard_map/ppermute | solution.py:270
  74.0 0.0 collective-permute-done.5
  74.1 6.7 %collective-permute-start.6 = (bf16[304,256]{1,0:T(8,128)(2,1)S(1)}, bf16[304,256]{1,0:T(8,128)(2,1)S(1)}, u32[]{:S(2)}, u32[]{:S(2)}) collective-permute-start(bf16[304,256]{1,0:T(8,128)(2,1)S(1)} %fusion), channel_id=1, source_target_pairs={{0,24},{1,9},{8,16},{9,1},{16,8},{17,25},{24,0},{25,17},{2,26},{3,... | collective-permute-start | bytes 466952 | tf_op jit(solution)/shard_map/ppermute | solution.py:270
  80.7 0.0 collective-permute-done.4
  80.8 0.1 fusion.6
  80.8 5.9 %collective-permute-start.7 = (bf16[288,256]{1,0:T(8,128)(2,1)S(1)}, bf16[288,256]{1,0:T(8,128)(2,1)S(1)}, u32[]{:S(2)}, u32[]{:S(2)}) collective-permute-start(bf16[288,256]{1,0:T(8,128)(2,1)S(1)} %get-tuple-element.13), channel_id=1, source_target_pairs={{0,1},{1,0},{2,3},{3,2},{4,5},{5,4},{6,7},{7,6},{8,9},{9,8},{10,11... | collective-permute-start | bytes 442376 | tf_op jit(solution)/shard_map/ppermute | solution.py:260
  86.7 0.0 collective-permute-done.6
  86.7 0.1 fusion.5
  86.8 6.5 %collective-permute-start.8 = (bf16[304,256]{1,0:T(8,128)(2,1)S(1)}, bf16[304,256]{1,0:T(8,128)(2,1)S(1)}, u32[]{:S(2)}, u32[]{:S(2)}) collective-permute-start(bf16[304,256]{1,0:T(8,128)(2,1)S(1)} %get-tuple-element.11), channel_id=1, source_target_pairs={{0,1},{1,0},{2,3},{3,2},{4,5},{5,4},{6,7},{7,6},{8,9},{9,8},{10,11... | collective-permute-start | bytes 466952 | tf_op jit(solution)/shard_map/ppermute | solution.py:260
  93.5 0.0 collective-permute-done.7.refs_2_
  93.5 0.9 collective-permute-done.8.refs_3_
  94.4 4.6 %shard_map.59 = bf16[16,104,128]{2,1,0:T(8,128)(2,1)} custom-call(s32[1]{0:T(128)} %bitcast.core_ref, f32[288,256]{1,0:T(8,128)S(1)} %get-tuple-element.14.refs_0_, f32[304,256]{1,0:T(8,128)S(1)} %get-tuple-element.12.refs_1_, bf16[288,256]{1,0:T(8,128)(2,1)S(1)} %collective-permute-done.7.refs_2_, bf16[304,256]{1,0:T(8,128)(2,1)S(1)} %collective-permute-done.8.refs_3_, ...), custom_call_target="tpu_custom_call" | custom-call | flops 3321888768 | bytes 2555904 | tf_op jit(solution)/shard_map/pallas_call | solution.py:200
  98.9 5.4 %all-to-all-start.1 = ((bf16[16,104,128]{2,1,0:T(8,128)(2,1)}), bf16[16,104,128]{2,1,0:T(8,128)(2,1)S(1)}, u32[]{:S(2)}, u32[]{:S(2)}) async-start(bf16[16,104,128]{2,1,0:T(8,128)(2,1)} %shard_map.59), calls=%async_computation.1 | async-start | bytes 851968 | tf_op jit(solution)/shard_map/all_to_all | solution.py:337
  104.4 0.1 fusion.4
  104.5 0.7 copy.10.hit_ref
  105.1 10.4 %all-to-all-done.1.back_ref = bf16[16,104,128]{2,1,0:T(8,128)(2,1)S(1)} async-done(((bf16[16,104,128]{2,1,0:T(8,128)(2,1)}), bf16[16,104,128]{2,1,0:T(8,128)(2,1)S(1)}, u32[]{:S(2)}, u32[]{:S(2)}) %all-to-all-start.1) | async-done | bytes 426016 | tf_op jit(solution)/shard_map/all_to_all | solution.py:337
  115.6 0.8 copy-done
  116.3 1.8 %shard_map.60 = (bf16[16,16,768]{2,1,0:T(8,128)(2,1)}, f32[1,1]{1,0:T(1,128)}) custom-call(bf16[16,104,128]{2,1,0:T(8,128)(2,1)} %copy-done, s32[16,1,1]{2,1,0:T(1,128)} %copy.10.hit_ref), custom_call_target="tpu_custom_call" | custom-call | tf_op jit(solution)/shard_map/pallas_call | solution.py:242
  (10 shorter events, 0.2 us)
Async XLA Ops:
  0.6 31.5 %all-to-all-start = ((bf16[32,2,16,768]{3,2,1,0:T(8,128)(2,1)}), bf16[32,2,16,768]{3,2,1,0:T(8,128)(2,1)S(1)}, u32[]{:S(2)}, u32[]{:S(2)}) async-start(bf16[32,2,16,768]{3,2,1,0:T(8,128)(2,1)} %bitcast.40), calls=%async_computation | async-start | bytes 3145728 | tf_op jit(solution)/shard_map/all_to_all | solution.py:309
  32.4 16.7 %collective-permute-start = (bf16[8,16,768]{2,1,0:T(8,128)(2,1)S(1)}, bf16[8,16,768]{2,1,0:T(8,128)(2,1)S(1)}, u32[]{:S(2)}, u32[]{:S(2)}) collective-permute-start(bf16[8,16,768]{2,1,0:T(8,128)(2,1)S(1)} %fusion.1), channel_id=1, source_target_pairs={{0,4},{1,29},{2,6},{3,31},{4,0},{5,9},{6,2},{7,11},{8,12},{9,5},{1... | collective-permute-start | bytes 589832 | tf_op jit(solution)/shard_map/ppermute | solution.py:281
  44.8 6.2 %collective-permute-start.1 = (bf16[128,768]{1,0:T(8,128)(2,1)S(1)}, bf16[128,768]{1,0:T(8,128)(2,1)S(1)}, u32[]{:S(2)}, u32[]{:S(2)}) collective-permute-start(bf16[128,768]{1,0:T(8,128)(2,1)S(1)} %bitcast.33), channel_id=1, source_target_pairs={{0,1},{1,0},{2,3},{3,2},{4,5},{5,4},{6,7},{7,6},{8,9},{9,8},{10,11... | collective-permute-start | bytes 589832 | tf_op jit(solution)/shard_map/ppermute | solution.py:260
  49.1 3.3 %collective-permute-start.2 = (bf16[128,768]{1,0:T(8,128)(2,1)S(1)}, bf16[128,768]{1,0:T(8,128)(2,1)S(1)}, u32[]{:S(2)}, u32[]{:S(2)}) collective-permute-start(bf16[128,768]{1,0:T(8,128)(2,1)S(1)} %bitcast.36), channel_id=1, source_target_pairs={{0,1},{1,0},{2,3},{3,2},{4,5},{5,4},{6,7},{7,6},{8,9},{9,8},{10,11... | collective-permute-start | bytes 589832 | tf_op jit(solution)/shard_map/ppermute | solution.py:260
  53.1 15.1 %collective-permute-start.3 = (bf16[288,256]{1,0:T(8,128)(2,1)S(1)}, bf16[288,256]{1,0:T(8,128)(2,1)S(1)}, u32[]{:S(2)}, u32[]{:S(2)}) collective-permute-start(bf16[288,256]{1,0:T(8,128)(2,1)S(1)} %slice.53), channel_id=1, source_target_pairs={{0,8},{1,25},{8,0},{9,17},{16,24},{17,9},{24,16},{25,1},{2,10},{3,... | collective-permute-start | bytes 442376 | tf_op jit(solution)/shard_map/ppermute | solution.py:270
  61.2 12.8 %collective-permute-start.5 = (bf16[304,256]{1,0:T(8,128)(2,1)S(1)}, bf16[304,256]{1,0:T(8,128)(2,1)S(1)}, u32[]{:S(2)}, u32[]{:S(2)}) collective-permute-start(bf16[304,256]{1,0:T(8,128)(2,1)S(1)} %slice.55), channel_id=1, source_target_pairs={{0,8},{1,25},{8,0},{9,17},{16,24},{17,9},{24,16},{25,1},{2,10},{3,... | collective-permute-start | bytes 466952 | tf_op jit(solution)/shard_map/ppermute | solution.py:270
  68.2 12.6 %collective-permute-start.4 = (bf16[288,256]{1,0:T(8,128)(2,1)S(1)}, bf16[288,256]{1,0:T(8,128)(2,1)S(1)}, u32[]{:S(2)}, u32[]{:S(2)}) collective-permute-start(bf16[288,256]{1,0:T(8,128)(2,1)S(1)} %fusion.3), channel_id=1, source_target_pairs={{0,24},{1,9},{8,16},{9,1},{16,8},{17,25},{24,0},{25,17},{2,26},{3,... | collective-permute-start | bytes 442376 | tf_op jit(solution)/shard_map/ppermute | solution.py:270
  74.1 12.7 %collective-permute-start.6 = (bf16[304,256]{1,0:T(8,128)(2,1)S(1)}, bf16[304,256]{1,0:T(8,128)(2,1)S(1)}, u32[]{:S(2)}, u32[]{:S(2)}) collective-permute-start(bf16[304,256]{1,0:T(8,128)(2,1)S(1)} %fusion), channel_id=1, source_target_pairs={{0,24},{1,9},{8,16},{9,1},{16,8},{17,25},{24,0},{25,17},{2,26},{3,... | collective-permute-start | bytes 466952 | tf_op jit(solution)/shard_map/ppermute | solution.py:270
  80.8 12.7 %collective-permute-start.7 = (bf16[288,256]{1,0:T(8,128)(2,1)S(1)}, bf16[288,256]{1,0:T(8,128)(2,1)S(1)}, u32[]{:S(2)}, u32[]{:S(2)}) collective-permute-start(bf16[288,256]{1,0:T(8,128)(2,1)S(1)} %get-tuple-element.13), channel_id=1, source_target_pairs={{0,1},{1,0},{2,3},{3,2},{4,5},{5,4},{6,7},{7,6},{8,9},{9,8},{10,11... | collective-permute-start | bytes 442376 | tf_op jit(solution)/shard_map/ppermute | solution.py:260
  86.8 7.5 %collective-permute-start.8 = (bf16[304,256]{1,0:T(8,128)(2,1)S(1)}, bf16[304,256]{1,0:T(8,128)(2,1)S(1)}, u32[]{:S(2)}, u32[]{:S(2)}) collective-permute-start(bf16[304,256]{1,0:T(8,128)(2,1)S(1)} %get-tuple-element.11), channel_id=1, source_target_pairs={{0,1},{1,0},{2,3},{3,2},{4,5},{5,4},{6,7},{7,6},{8,9},{9,8},{10,11... | collective-permute-start | bytes 466952 | tf_op jit(solution)/shard_map/ppermute | solution.py:260
  94.4 10.0 %copy-start.1 = (s32[64]{0:T(128)S(1)}, s32[64]{0:T(128)}, u32[]{:S(2)}) copy-start(s32[64]{0:T(128)} %param.4) | copy-start | bytes 772
  98.9 16.6 %all-to-all-start.1 = ((bf16[16,104,128]{2,1,0:T(8,128)(2,1)}), bf16[16,104,128]{2,1,0:T(8,128)(2,1)S(1)}, u32[]{:S(2)}, u32[]{:S(2)}) async-start(bf16[16,104,128]{2,1,0:T(8,128)(2,1)} %shard_map.59), calls=%async_computation.1 | async-start | bytes 851968 | tf_op jit(solution)/shard_map/all_to_all | solution.py:337
  115.6 0.8 copy-start

commit v7 on v6

--- a/solution.py
+++ b/solution.py
@@ -21,7 +21,7 @@
 TILE = 256
 FSDP = ("y", "zh", "zm", "zb", "core")
 LANES = 128
-NOTE = 8
+NOTE = 16
 
 
 def dot(a, b):

time: 120 us -> 121 us (level)
  no operation moved by 1% of the time
where the time goes in v7:
time: 121 us; the launch traced here: 119 us
  starting transfers between devices  65.8 us (54%)
  waiting for transfers between devices  42.9 us (35%)
  Pallas kernels  7.02 us (6%)
  local copies, waits for them, and re-layouts  1.51 us (1%)
    ppermute x4, starting transfers between devices, neighbour(): return lax.ppermute(value, (axis, 'core'), pairs)  22.5 us
    all_to_all x1, waiting for transfers between devices, on_device(): slabs = lax.all_to_all(slabs, ('dp', 'y', 'zb'), 0, 0, tiled=True)  22.3 us
    ppermute x4, starting transfers between devices, shift(): lax.ppermute(value, axis, [(i, (i + distance) % n) for i in range(n)])  16.3 us
    ppermute x1, starting transfers between devices, swap_windows(): return lax.ppermute(value, FSDP[1:], pairs)  12.4 us
    all_to_all x1, waiting for transfers between devices, placed(): lax.all_to_all(slab, 'fsdp', 0, 0, axis_index_groups=groups, tiled=True)  10.9 us
    all_to_all x1, starting transfers between devices, on_device(): slabs = lax.all_to_all(slabs, ('dp', 'y', 'zb'), 0, 0, tiled=True)  9.24 us
    all_to_all x1, starting transfers between devices, placed(): lax.all_to_all(slab, 'fsdp', 0, 0, axis_index_groups=groups, tiled=True)  5.41 us
    ppermute x4, waiting for transfers between devices, neighbour(): return lax.ppermute(value, (axis, 'core'), pairs)  5.07 us
  transfers between devices with their start and end apart: 11, of which 6 were waited for; matrix products, arithmetic and copies ran while one was open for 1% of the time, Pallas kernels for 0%

profile of v7, /device:TPU:1, one launch (start us, length us, event | category | flops | bytes accessed | tf_op | source)
XLA Modules:
  0.0 118.6 jit_solution(7155716082775446025)
XLA Ops:
  0.6 9.2 %all-to-all-start = ((bf16[32,2,16,768]{3,2,1,0:T(8,128)(2,1)}), bf16[32,2,16,768]{3,2,1,0:T(8,128)(2,1)S(1)}, u32[]{:S(2)}, u32[]{:S(2)}) async-start(bf16[32,2,16,768]{3,2,1,0:T(8,128)(2,1)} %bitcast.40), calls=%async_computation | async-start | bytes 3145728 | tf_op jit(solution)/shard_map/all_to_all | solution.py:309
  9.9 22.3 %all-to-all-done = bf16[32,2,16,768]{3,2,1,0:T(8,128)(2,1)S(1)} async-done(((bf16[32,2,16,768]{3,2,1,0:T(8,128)(2,1)}), bf16[32,2,16,768]{3,2,1,0:T(8,128)(2,1)S(1)}, u32[]{:S(2)}, u32[]{:S(2)}) %all-to-all-start) | async-done | bytes 1572896 | tf_op jit(solution)/shard_map/all_to_all | solution.py:309
  32.1 0.1 fusion.1
  32.3 0.1 fusion.2
  32.4 12.4 %collective-permute-start = (bf16[8,16,768]{2,1,0:T(8,128)(2,1)S(1)}, bf16[8,16,768]{2,1,0:T(8,128)(2,1)S(1)}, u32[]{:S(2)}, u32[]{:S(2)}) collective-permute-start(bf16[8,16,768]{2,1,0:T(8,128)(2,1)S(1)} %fusion.1), channel_id=1, source_target_pairs={{0,4},{1,29},{2,6},{3,31},{4,0},{5,9},{6,2},{7,11},{8,12},{9,5},{1... | collective-permute-start | bytes 589832 | tf_op jit(solution)/shard_map/ppermute | solution.py:281
  44.8 1.9 %collective-permute-start.1 = (bf16[128,768]{1,0:T(8,128)(2,1)S(1)}, bf16[128,768]{1,0:T(8,128)(2,1)S(1)}, u32[]{:S(2)}, u32[]{:S(2)}) collective-permute-start(bf16[128,768]{1,0:T(8,128)(2,1)S(1)} %bitcast.33), channel_id=1, source_target_pairs={{0,1},{1,0},{2,3},{3,2},{4,5},{5,4},{6,7},{7,6},{8,9},{9,8},{10,11... | collective-permute-start | bytes 589832 | tf_op jit(solution)/shard_map/ppermute | solution.py:260
  46.8 2.4 %collective-permute-done = bf16[8,16,768]{2,1,0:T(8,128)(2,1)S(1)} collective-permute-done((bf16[8,16,768]{2,1,0:T(8,128)(2,1)S(1)}, bf16[8,16,768]{2,1,0:T(8,128)(2,1)S(1)}, u32[]{:S(2)}, u32[]{:S(2)}) %collective-permute-start) | collective-permute-done | bytes 196640 | tf_op jit(solution)/shard_map/ppermute | solution.py:281
  49.1 1.9 %collective-permute-start.2 = (bf16[128,768]{1,0:T(8,128)(2,1)S(1)}, bf16[128,768]{1,0:T(8,128)(2,1)S(1)}, u32[]{:S(2)}, u32[]{:S(2)}) collective-permute-start(bf16[128,768]{1,0:T(8,128)(2,1)S(1)} %bitcast.36), channel_id=1, source_target_pairs={{0,1},{1,0},{2,3},{3,2},{4,5},{5,4},{6,7},{7,6},{8,9},{9,8},{10,11... | collective-permute-start | bytes 589832 | tf_op jit(solution)/shard_map/ppermute | solution.py:260
  51.0 0.0 collective-permute-done.1.refs_2_
  51.0 1.4 %collective-permute-done.2.refs_3_ = bf16[128,768]{1,0:T(8,128)(2,1)S(1)} collective-permute-done((bf16[128,768]{1,0:T(8,128)(2,1)S(1)}, bf16[128,768]{1,0:T(8,128)(2,1)S(1)}, u32[]{:S(2)}, u32[]{:S(2)}) %collective-permute-start.2) | collective-permute-done | bytes 196640 | tf_op jit(solution)/shard_map/ppermute | solution.py:260
  52.4 0.6 shard_map.58
  53.1 8.1 %collective-permute-start.3 = (bf16[288,256]{1,0:T(8,128)(2,1)S(1)}, bf16[288,256]{1,0:T(8,128)(2,1)S(1)}, u32[]{:S(2)}, u32[]{:S(2)}) collective-permute-start(bf16[288,256]{1,0:T(8,128)(2,1)S(1)} %slice.53), channel_id=1, source_target_pairs={{0,8},{1,25},{8,0},{9,17},{16,24},{17,9},{24,16},{25,1},{2,10},{3,... | collective-permute-start | bytes 442376 | tf_op jit(solution)/shard_map/ppermute | solution.py:270
  61.2 1.9 %collective-permute-start.5 = (bf16[304,256]{1,0:T(8,128)(2,1)S(1)}, bf16[304,256]{1,0:T(8,128)(2,1)S(1)}, u32[]{:S(2)}, u32[]{:S(2)}) collective-permute-start(bf16[304,256]{1,0:T(8,128)(2,1)S(1)} %slice.55), channel_id=1, source_target_pairs={{0,8},{1,25},{8,0},{9,17},{16,24},{17,9},{24,16},{25,1},{2,10},{3,... | collective-permute-start | bytes 466952 | tf_op jit(solution)/shard_map/ppermute | solution.py:270
  63.1 5.0 %collective-permute-done.3 = bf16[288,256]{1,0:T(8,128)(2,1)S(1)} collective-permute-done((bf16[288,256]{1,0:T(8,128)(2,1)S(1)}, bf16[288,256]{1,0:T(8,128)(2,1)S(1)}, u32[]{:S(2)}, u32[]{:S(2)}) %collective-permute-start.3) | collective-permute-done | bytes 147488 | tf_op jit(solution)/shard_map/ppermute | solution.py:270
  68.2 5.8 %collective-permute-start.4 = (bf16[288,256]{1,0:T(8,128)(2,1)S(1)}, bf16[288,256]{1,0:T(8,128)(2,1)S(1)}, u32[]{:S(2)}, u32[]{:S(2)}) collective-permute-start(bf16[288,256]{1,0:T(8,128)(2,1)S(1)} %fusion.3), channel_id=1, source_target_pairs={{0,24},{1,9},{8,16},{9,1},{16,8},{17,25},{24,0},{25,17},{2,26},{3,... | collective-permute-start | bytes 442376 | tf_op jit(solution)/shard_map/ppermute | solution.py:270
  74.0 0.0 collective-permute-done.5
  74.1 6.7 %collective-permute-start.6 = (bf16[304,256]{1,0:T(8,128)(2,1)S(1)}, bf16[304,256]{1,0:T(8,128)(2,1)S(1)}, u32[]{:S(2)}, u32[]{:S(2)}) collective-permute-start(bf16[304,256]{1,0:T(8,128)(2,1)S(1)} %fusion), channel_id=1, source_target_pairs={{0,24},{1,9},{8,16},{9,1},{16,8},{17,25},{24,0},{25,17},{2,26},{3,... | collective-permute-start | bytes 466952 | tf_op jit(solution)/shard_map/ppermute | solution.py:270
  80.7 0.0 collective-permute-done.4
  80.8 0.1 fusion.6
  80.8 5.9 %collective-permute-start.7 = (bf16[288,256]{1,0:T(8,128)(2,1)S(1)}, bf16[288,256]{1,0:T(8,128)(2,1)S(1)}, u32[]{:S(2)}, u32[]{:S(2)}) collective-permute-start(bf16[288,256]{1,0:T(8,128)(2,1)S(1)} %get-tuple-element.13), channel_id=1, source_target_pairs={{0,1},{1,0},{2,3},{3,2},{4,5},{5,4},{6,7},{7,6},{8,9},{9,8},{10,11... | collective-permute-start | bytes 442376 | tf_op jit(solution)/shard_map/ppermute | solution.py:260
  86.7 0.0 collective-permute-done.6
  86.7 0.1 fusion.5
  86.8 6.5 %collective-permute-start.8 = (bf16[304,256]{1,0:T(8,128)(2,1)S(1)}, bf16[304,256]{1,0:T(8,128)(2,1)S(1)}, u32[]{:S(2)}, u32[]{:S(2)}) collective-permute-start(bf16[304,256]{1,0:T(8,128)(2,1)S(1)} %get-tuple-element.11), channel_id=1, source_target_pairs={{0,1},{1,0},{2,3},{3,2},{4,5},{5,4},{6,7},{7,6},{8,9},{9,8},{10,11... | collective-permute-start | bytes 466952 | tf_op jit(solution)/shard_map/ppermute | solution.py:260
  93.5 0.0 collective-permute-done.7.refs_2_
  93.5 0.9 collective-permute-done.8.refs_3_
  94.4 4.6 %shard_map.59 = bf16[16,112,128]{2,1,0:T(8,128)(2,1)} custom-call(s32[1]{0:T(128)} %bitcast.core_ref, f32[288,256]{1,0:T(8,128)S(1)} %get-tuple-element.14.refs_0_, f32[304,256]{1,0:T(8,128)S(1)} %get-tuple-element.12.refs_1_, bf16[288,256]{1,0:T(8,128)(2,1)S(1)} %collective-permute-done.7.refs_2_, bf16[304,256]{1,0:T(8,128)(2,1)S(1)} %collective-permute-done.8.refs_3_, ...), custom_call_target="tpu_custom_call" | custom-call | flops 3321888768 | bytes 2555904 | tf_op jit(solution)/shard_map/pallas_call | solution.py:200
  98.9 5.4 %all-to-all-start.1 = ((bf16[16,112,128]{2,1,0:T(8,128)(2,1)}), bf16[16,112,128]{2,1,0:T(8,128)(2,1)S(1)}, u32[]{:S(2)}, u32[]{:S(2)}) async-start(bf16[16,112,128]{2,1,0:T(8,128)(2,1)} %shard_map.59), calls=%async_computation.1 | async-start | bytes 917504 | tf_op jit(solution)/shard_map/all_to_all | solution.py:337
  104.4 0.1 fusion.4
  104.5 0.7 copy.10.hit_ref
  105.1 10.9 %all-to-all-done.1.back_ref = bf16[16,112,128]{2,1,0:T(8,128)(2,1)S(1)} async-done(((bf16[16,112,128]{2,1,0:T(8,128)(2,1)}), bf16[16,112,128]{2,1,0:T(8,128)(2,1)S(1)}, u32[]{:S(2)}, u32[]{:S(2)}) %all-to-all-start.1) | async-done | bytes 458784 | tf_op jit(solution)/shard_map/all_to_all | solution.py:337
  116.0 0.8 copy-done
  116.8 1.8 %shard_map.60 = (bf16[16,16,768]{2,1,0:T(8,128)(2,1)}, f32[1,1]{1,0:T(1,128)}) custom-call(bf16[16,112,128]{2,1,0:T(8,128)(2,1)} %copy-done, s32[16,1,1]{2,1,0:T(1,128)} %copy.10.hit_ref), custom_call_target="tpu_custom_call" | custom-call | tf_op jit(solution)/shard_map/pallas_call | solution.py:242
  (10 shorter events, 0.2 us)
Async XLA Ops:
  0.6 31.5 %all-to-all-start = ((bf16[32,2,16,768]{3,2,1,0:T(8,128)(2,1)}), bf16[32,2,16,768]{3,2,1,0:T(8,128)(2,1)S(1)}, u32[]{:S(2)}, u32[]{:S(2)}) async-start(bf16[32,2,16,768]{3,2,1,0:T(8,128)(2,1)} %bitcast.40), calls=%async_computation | async-start | bytes 3145728 | tf_op jit(solution)/shard_map/all_to_all | solution.py:309
  32.4 16.7 %collective-permute-start = (bf16[8,16,768]{2,1,0:T(8,128)(2,1)S(1)}, bf16[8,16,768]{2,1,0:T(8,128)(2,1)S(1)}, u32[]{:S(2)}, u32[]{:S(2)}) collective-permute-start(bf16[8,16,768]{2,1,0:T(8,128)(2,1)S(1)} %fusion.1), channel_id=1, source_target_pairs={{0,4},{1,29},{2,6},{3,31},{4,0},{5,9},{6,2},{7,11},{8,12},{9,5},{1... | collective-permute-start | bytes 589832 | tf_op jit(solution)/shard_map/ppermute | solution.py:281
  44.8 6.2 %collective-permute-start.1 = (bf16[128,768]{1,0:T(8,128)(2,1)S(1)}, bf16[128,768]{1,0:T(8,128)(2,1)S(1)}, u32[]{:S(2)}, u32[]{:S(2)}) collective-permute-start(bf16[128,768]{1,0:T(8,128)(2,1)S(1)} %bitcast.33), channel_id=1, source_target_pairs={{0,1},{1,0},{2,3},{3,2},{4,5},{5,4},{6,7},{7,6},{8,9},{9,8},{10,11... | collective-permute-start | bytes 589832 | tf_op jit(solution)/shard_map/ppermute | solution.py:260
  49.1 3.3 %collective-permute-start.2 = (bf16[128,768]{1,0:T(8,128)(2,1)S(1)}, bf16[128,768]{1,0:T(8,128)(2,1)S(1)}, u32[]{:S(2)}, u32[]{:S(2)}) collective-permute-start(bf16[128,768]{1,0:T(8,128)(2,1)S(1)} %bitcast.36), channel_id=1, source_target_pairs={{0,1},{1,0},{2,3},{3,2},{4,5},{5,4},{6,7},{7,6},{8,9},{9,8},{10,11... | collective-permute-start | bytes 589832 | tf_op jit(solution)/shard_map/ppermute | solution.py:260
  53.1 15.1 %collective-permute-start.3 = (bf16[288,256]{1,0:T(8,128)(2,1)S(1)}, bf16[288,256]{1,0:T(8,128)(2,1)S(1)}, u32[]{:S(2)}, u32[]{:S(2)}) collective-permute-start(bf16[288,256]{1,0:T(8,128)(2,1)S(1)} %slice.53), channel_id=1, source_target_pairs={{0,8},{1,25},{8,0},{9,17},{16,24},{17,9},{24,16},{25,1},{2,10},{3,... | collective-permute-start | bytes 442376 | tf_op jit(solution)/shard_map/ppermute | solution.py:270
  61.2 12.8 %collective-permute-start.5 = (bf16[304,256]{1,0:T(8,128)(2,1)S(1)}, bf16[304,256]{1,0:T(8,128)(2,1)S(1)}, u32[]{:S(2)}, u32[]{:S(2)}) collective-permute-start(bf16[304,256]{1,0:T(8,128)(2,1)S(1)} %slice.55), channel_id=1, source_target_pairs={{0,8},{1,25},{8,0},{9,17},{16,24},{17,9},{24,16},{25,1},{2,10},{3,... | collective-permute-start | bytes 466952 | tf_op jit(solution)/shard_map/ppermute | solution.py:270
  68.2 12.6 %collective-permute-start.4 = (bf16[288,256]{1,0:T(8,128)(2,1)S(1)}, bf16[288,256]{1,0:T(8,128)(2,1)S(1)}, u32[]{:S(2)}, u32[]{:S(2)}) collective-permute-start(bf16[288,256]{1,0:T(8,128)(2,1)S(1)} %fusion.3), channel_id=1, source_target_pairs={{0,24},{1,9},{8,16},{9,1},{16,8},{17,25},{24,0},{25,17},{2,26},{3,... | collective-permute-start | bytes 442376 | tf_op jit(solution)/shard_map/ppermute | solution.py:270
  74.1 12.7 %collective-permute-start.6 = (bf16[304,256]{1,0:T(8,128)(2,1)S(1)}, bf16[304,256]{1,0:T(8,128)(2,1)S(1)}, u32[]{:S(2)}, u32[]{:S(2)}) collective-permute-start(bf16[304,256]{1,0:T(8,128)(2,1)S(1)} %fusion), channel_id=1, source_target_pairs={{0,24},{1,9},{8,16},{9,1},{16,8},{17,25},{24,0},{25,17},{2,26},{3,... | collective-permute-start | bytes 466952 | tf_op jit(solution)/shard_map/ppermute | solution.py:270
  80.8 12.7 %collective-permute-start.7 = (bf16[288,256]{1,0:T(8,128)(2,1)S(1)}, bf16[288,256]{1,0:T(8,128)(2,1)S(1)}, u32[]{:S(2)}, u32[]{:S(2)}) collective-permute-start(bf16[288,256]{1,0:T(8,128)(2,1)S(1)} %get-tuple-element.13), channel_id=1, source_target_pairs={{0,1},{1,0},{2,3},{3,2},{4,5},{5,4},{6,7},{7,6},{8,9},{9,8},{10,11... | collective-permute-start | bytes 442376 | tf_op jit(solution)/shard_map/ppermute | solution.py:260
  86.8 7.5 %collective-permute-start.8 = (bf16[304,256]{1,0:T(8,128)(2,1)S(1)}, bf16[304,256]{1,0:T(8,128)(2,1)S(1)}, u32[]{:S(2)}, u32[]{:S(2)}) collective-permute-start(bf16[304,256]{1,0:T(8,128)(2,1)S(1)} %get-tuple-element.11), channel_id=1, source_target_pairs={{0,1},{1,0},{2,3},{3,2},{4,5},{5,4},{6,7},{7,6},{8,9},{9,8},{10,11... | collective-permute-start | bytes 466952 | tf_op jit(solution)/shard_map/ppermute | solution.py:260
  94.4 10.0 %copy-start.1 = (s32[64]{0:T(128)S(1)}, s32[64]{0:T(128)}, u32[]{:S(2)}) copy-start(s32[64]{0:T(128)} %param.4) | copy-start | bytes 772
  98.9 17.1 %all-to-all-start.1 = ((bf16[16,112,128]{2,1,0:T(8,128)(2,1)}), bf16[16,112,128]{2,1,0:T(8,128)(2,1)S(1)}, u32[]{:S(2)}, u32[]{:S(2)}) async-start(bf16[16,112,128]{2,1,0:T(8,128)(2,1)} %shard_map.59), calls=%async_computation.1 | async-start | bytes 917504 | tf_op jit(solution)/shard_map/all_to_all | solution.py:337
  116.0 0.8 copy-start

commit v8 on v6

--- a/solution.py
+++ b/solution.py
@@ -317,9 +317,7 @@
     away = swap_windows(gone)
     mine = jnp.stack([jnp.where(mid == 0, here, away), jnp.where(mid == 0, away, here)], axis=1)
     mine = mine.reshape(mats_dp * rows_dev, width)
-    pieces = [part.reshape(-1, width) for part in (here, away)]
-    pieces += [shift(part, "core", 1) for part in pieces]
-    total, sent = half_gram(core, pieces)
+    total, sent = half_gram(core, [mine, shift(mine, "core", 1)])
     cut = HALF // 2 // SPARE * SPARE
     totals = [total[:cut], total[cut:]]
     sents = [sent[:cut], sent[cut:]]

time: 120 us -> 120 us (level)
  waiting for transfers between devices: 42.4 us -> 46.1 us
  starting transfers between devices: 65.8 us -> 62.9 us
    ppermute x4 -> x3, starting transfers between devices: 16.3 us -> 13.7 us  [shift(): lax.ppermute(value, axis, [(i, (i + distance) % n) for i in range(n)])]
    ppermute x1, waiting for transfers between devices: 2.37 us -> 4.29 us  [swap_windows(): return lax.ppermute(value, FSDP[1:], pairs)]
    ppermute x4 -> x3, waiting for transfers between devices: 2.26 us -> 2.68 us  [shift(): lax.ppermute(value, axis, [(i, (i + distance) % n) for i in range(n)])]
  transfers between devices with their start and end apart: 11 -> 10, of which waited for: 6 -> 7; matrix products, arithmetic and copies ran while one was open for 1% -> 1% of each run, Pallas kernels for 0% -> 0%
where the time goes in v8:
time: 120 us; the launch traced here: 119 us
  starting transfers between devices  62.9 us (52%)
  waiting for transfers between devices  46.1 us (38%)
  Pallas kernels  6.98 us (6%)
  local copies, waits for them, and re-layouts  1.48 us (1%)
    all_to_all x1, waiting for transfers between devices, on_device(): slabs = lax.all_to_all(slabs, ('dp', 'y', 'zb'), 0, 0, tiled=True)  22.3 us
    ppermute x4, starting transfers between devices, neighbour(): return lax.ppermute(value, (axis, 'core'), pairs)  22 us
    ppermute x3, starting transfers between devices, shift(): lax.ppermute(value, axis, [(i, (i + distance) % n) for i in range(n)])  13.7 us
    ppermute x1, starting transfers between devices, swap_windows(): return lax.ppermute(value, FSDP[1:], pairs)  12.4 us
    all_to_all x1, waiting for transfers between devices, placed(): lax.all_to_all(slab, 'fsdp', 0, 0, axis_index_groups=groups, tiled=True)  10.7 us
    all_to_all x1, starting transfers between devices, on_device(): slabs = lax.all_to_all(slabs, ('dp', 'y', 'zb'), 0, 0, tiled=True)  9.24 us
    ppermute x4, waiting for transfers between devices, neighbour(): return lax.ppermute(value, (axis, 'core'), pairs)  6.17 us
    all_to_all x1, starting transfers between devices, placed(): lax.all_to_all(slab, 'fsdp', 0, 0, axis_index_groups=groups, tiled=True)  5.51 us
  transfers between devices with their start and end apart: 10, of which 7 were waited for; matrix products, arithmetic and copies ran while one was open for 1% of the time, Pallas kernels for 0%

profile of v8, /device:TPU:1, one launch (start us, length us, event | category | flops | bytes accessed | tf_op | source)
XLA Modules:
  0.0 118.9 jit_solution(11889285061689372539)
XLA Ops:
  0.6 9.2 %all-to-all-start = ((bf16[32,2,16,768]{3,2,1,0:T(8,128)(2,1)}), bf16[32,2,16,768]{3,2,1,0:T(8,128)(2,1)S(1)}, u32[]{:S(2)}, u32[]{:S(2)}) async-start(bf16[32,2,16,768]{3,2,1,0:T(8,128)(2,1)} %bitcast.36), calls=%async_computation | async-start | bytes 3145728 | tf_op jit(solution)/shard_map/all_to_all | solution.py:309
  9.9 22.3 %all-to-all-done = bf16[32,2,16,768]{3,2,1,0:T(8,128)(2,1)S(1)} async-done(((bf16[32,2,16,768]{3,2,1,0:T(8,128)(2,1)}), bf16[32,2,16,768]{3,2,1,0:T(8,128)(2,1)S(1)}, u32[]{:S(2)}, u32[]{:S(2)}) %all-to-all-start) | async-done | bytes 1572896 | tf_op jit(solution)/shard_map/all_to_all | solution.py:309
  32.1 0.1 fusion.1
  32.3 0.1 fusion.2
  32.4 12.4 %collective-permute-start = (bf16[8,16,768]{2,1,0:T(8,128)(2,1)S(1)}, bf16[8,16,768]{2,1,0:T(8,128)(2,1)S(1)}, u32[]{:S(2)}, u32[]{:S(2)}) collective-permute-start(bf16[8,16,768]{2,1,0:T(8,128)(2,1)S(1)} %fusion.1), channel_id=1, source_target_pairs={{0,4},{1,29},{2,6},{3,31},{4,0},{5,9},{6,2},{7,11},{8,12},{9,5},{1... | collective-permute-start | bytes 589832 | tf_op jit(solution)/shard_map/ppermute | solution.py:281
  44.8 4.3 %collective-permute-done = bf16[8,16,768]{2,1,0:T(8,128)(2,1)S(1)} collective-permute-done((bf16[8,16,768]{2,1,0:T(8,128)(2,1)S(1)}, bf16[8,16,768]{2,1,0:T(8,128)(2,1)S(1)}, u32[]{:S(2)}, u32[]{:S(2)}) %collective-permute-start) | collective-permute-done | bytes 196640 | tf_op jit(solution)/shard_map/ppermute | solution.py:281
  49.2 1.9 %collective-permute-start.1 = (bf16[256,768]{1,0:T(8,128)(2,1)S(1)}, bf16[256,768]{1,0:T(8,128)(2,1)S(1)}, u32[]{:S(2)}, u32[]{:S(2)}) collective-permute-start(bf16[256,768]{1,0:T(8,128)(2,1)S(1)} %bitcast.31), channel_id=1, source_target_pairs={{0,1},{1,0},{2,3},{3,2},{4,5},{5,4},{6,7},{7,6},{8,9},{9,8},{10,11... | collective-permute-start | bytes 1179656 | tf_op jit(solution)/shard_map/ppermute | solution.py:260
  51.2 1.7 %collective-permute-done.1.refs_1_ = bf16[256,768]{1,0:T(8,128)(2,1)S(1)} collective-permute-done((bf16[256,768]{1,0:T(8,128)(2,1)S(1)}, bf16[256,768]{1,0:T(8,128)(2,1)S(1)}, u32[]{:S(2)}, u32[]{:S(2)}) %collective-permute-start.1) | collective-permute-done | bytes 393248 | tf_op jit(solution)/shard_map/ppermute | solution.py:260
  52.9 0.6 shard_map.58
  53.5 8.1 %collective-permute-start.4 = (bf16[304,256]{1,0:T(8,128)(2,1)S(1)}, bf16[304,256]{1,0:T(8,128)(2,1)S(1)}, u32[]{:S(2)}, u32[]{:S(2)}) collective-permute-start(bf16[304,256]{1,0:T(8,128)(2,1)S(1)} %slice.55), channel_id=1, source_target_pairs={{0,8},{1,25},{8,0},{9,17},{16,24},{17,9},{24,16},{25,1},{2,10},{3,... | collective-permute-start | bytes 466952 | tf_op jit(solution)/shard_map/ppermute | solution.py:270
  61.6 1.9 %collective-permute-start.2 = (bf16[288,256]{1,0:T(8,128)(2,1)S(1)}, bf16[288,256]{1,0:T(8,128)(2,1)S(1)}, u32[]{:S(2)}, u32[]{:S(2)}) collective-permute-start(bf16[288,256]{1,0:T(8,128)(2,1)S(1)} %slice.53), channel_id=1, source_target_pairs={{0,8},{1,25},{8,0},{9,17},{16,24},{17,9},{24,16},{25,1},{2,10},{3,... | collective-permute-start | bytes 442376 | tf_op jit(solution)/shard_map/ppermute | solution.py:270
  63.5 5.3 %collective-permute-done.4 = bf16[304,256]{1,0:T(8,128)(2,1)S(1)} collective-permute-done((bf16[304,256]{1,0:T(8,128)(2,1)S(1)}, bf16[304,256]{1,0:T(8,128)(2,1)S(1)}, u32[]{:S(2)}, u32[]{:S(2)}) %collective-permute-start.4) | collective-permute-done | bytes 155680 | tf_op jit(solution)/shard_map/ppermute | solution.py:270
  68.9 5.9 %collective-permute-start.5 = (bf16[304,256]{1,0:T(8,128)(2,1)S(1)}, bf16[304,256]{1,0:T(8,128)(2,1)S(1)}, u32[]{:S(2)}, u32[]{:S(2)}) collective-permute-start(bf16[304,256]{1,0:T(8,128)(2,1)S(1)} %fusion), channel_id=1, source_target_pairs={{0,24},{1,9},{8,16},{9,1},{16,8},{17,25},{24,0},{25,17},{2,26},{3,... | collective-permute-start | bytes 466952 | tf_op jit(solution)/shard_map/ppermute | solution.py:270
  74.8 0.0 collective-permute-done.2
  74.8 6.1 %collective-permute-start.3 = (bf16[288,256]{1,0:T(8,128)(2,1)S(1)}, bf16[288,256]{1,0:T(8,128)(2,1)S(1)}, u32[]{:S(2)}, u32[]{:S(2)}) collective-permute-start(bf16[288,256]{1,0:T(8,128)(2,1)S(1)} %fusion.3), channel_id=1, source_target_pairs={{0,24},{1,9},{8,16},{9,1},{16,8},{17,25},{24,0},{25,17},{2,26},{3,... | collective-permute-start | bytes 442376 | tf_op jit(solution)/shard_map/ppermute | solution.py:270
  80.9 0.9 collective-permute-done.5
  81.8 0.1 fusion.5
  81.9 4.9 %collective-permute-start.7 = (bf16[304,256]{1,0:T(8,128)(2,1)S(1)}, bf16[304,256]{1,0:T(8,128)(2,1)S(1)}, u32[]{:S(2)}, u32[]{:S(2)}) collective-permute-start(bf16[304,256]{1,0:T(8,128)(2,1)S(1)} %get-tuple-element.11), channel_id=1, source_target_pairs={{0,1},{1,0},{2,3},{3,2},{4,5},{5,4},{6,7},{7,6},{8,9},{9,8},{10,11... | collective-permute-start | bytes 466952 | tf_op jit(solution)/shard_map/ppermute | solution.py:260
  86.8 0.0 collective-permute-done.3
  86.8 0.1 fusion.6
  86.9 6.9 %collective-permute-start.6 = (bf16[288,256]{1,0:T(8,128)(2,1)S(1)}, bf16[288,256]{1,0:T(8,128)(2,1)S(1)}, u32[]{:S(2)}, u32[]{:S(2)}) collective-permute-start(bf16[288,256]{1,0:T(8,128)(2,1)S(1)} %get-tuple-element.13), channel_id=1, source_target_pairs={{0,1},{1,0},{2,3},{3,2},{4,5},{5,4},{6,7},{7,6},{8,9},{9,8},{10,11... | collective-permute-start | bytes 442376 | tf_op jit(solution)/shard_map/ppermute | solution.py:260
  93.8 1.0 collective-permute-done.6.refs_2_
  94.7 0.0 collective-permute-done.7.refs_3_
  94.8 0.0 copy-start.1
  94.8 4.5 %shard_map.59 = bf16[16,104,128]{2,1,0:T(8,128)(2,1)} custom-call(s32[1]{0:T(128)} %bitcast.core_ref, f32[288,256]{1,0:T(8,128)S(1)} %get-tuple-element.14.refs_0_, f32[304,256]{1,0:T(8,128)S(1)} %get-tuple-element.12.refs_1_, bf16[288,256]{1,0:T(8,128)(2,1)S(1)} %collective-permute-done.6.refs_2_, bf16[304,256]{1,0:T(8,128)(2,1)S(1)} %collective-permute-done.7.refs_3_, ...), custom_call_target="tpu_custom_call" | custom-call | flops 3321888768 | bytes 2555904 | tf_op jit(solution)/shard_map/pallas_call | solution.py:200
  99.3 5.5 %all-to-all-start.1 = ((bf16[16,104,128]{2,1,0:T(8,128)(2,1)}), bf16[16,104,128]{2,1,0:T(8,128)(2,1)S(1)}, u32[]{:S(2)}, u32[]{:S(2)}) async-start(bf16[16,104,128]{2,1,0:T(8,128)(2,1)} %shard_map.59), calls=%async_computation.1 | async-start | bytes 851968 | tf_op jit(solution)/shard_map/all_to_all | solution.py:335
  104.8 0.0 copy-done.1
  104.8 0.1 fusion.4
  104.9 0.7 copy.10.hit_ref
  105.6 10.7 %all-to-all-done.1.back_ref = bf16[16,104,128]{2,1,0:T(8,128)(2,1)S(1)} async-done(((bf16[16,104,128]{2,1,0:T(8,128)(2,1)}), bf16[16,104,128]{2,1,0:T(8,128)(2,1)S(1)}, u32[]{:S(2)}, u32[]{:S(2)}) %all-to-all-start.1) | async-done | bytes 426016 | tf_op jit(solution)/shard_map/all_to_all | solution.py:335
  116.3 0.8 copy-done
  117.1 1.8 %shard_map.60 = (bf16[16,16,768]{2,1,0:T(8,128)(2,1)}, f32[1,1]{1,0:T(1,128)}) custom-call(bf16[16,104,128]{2,1,0:T(8,128)(2,1)} %copy-done, s32[16,1,1]{2,1,0:T(1,128)} %copy.10.hit_ref), custom_call_target="tpu_custom_call" | custom-call | tf_op jit(solution)/shard_map/pallas_call | solution.py:242
  (8 shorter events, 0.2 us)
Async XLA Ops:
  0.6 31.5 %all-to-all-start = ((bf16[32,2,16,768]{3,2,1,0:T(8,128)(2,1)}), bf16[32,2,16,768]{3,2,1,0:T(8,128)(2,1)S(1)}, u32[]{:S(2)}, u32[]{:S(2)}) async-start(bf16[32,2,16,768]{3,2,1,0:T(8,128)(2,1)} %bitcast.36), calls=%async_computation | async-start | bytes 3145728 | tf_op jit(solution)/shard_map/all_to_all | solution.py:309
  32.4 16.7 %collective-permute-start = (bf16[8,16,768]{2,1,0:T(8,128)(2,1)S(1)}, bf16[8,16,768]{2,1,0:T(8,128)(2,1)S(1)}, u32[]{:S(2)}, u32[]{:S(2)}) collective-permute-start(bf16[8,16,768]{2,1,0:T(8,128)(2,1)S(1)} %fusion.1), channel_id=1, source_target_pairs={{0,4},{1,29},{2,6},{3,31},{4,0},{5,9},{6,2},{7,11},{8,12},{9,5},{1... | collective-permute-start | bytes 589832 | tf_op jit(solution)/shard_map/ppermute | solution.py:281
  49.2 3.6 %collective-permute-start.1 = (bf16[256,768]{1,0:T(8,128)(2,1)S(1)}, bf16[256,768]{1,0:T(8,128)(2,1)S(1)}, u32[]{:S(2)}, u32[]{:S(2)}) collective-permute-start(bf16[256,768]{1,0:T(8,128)(2,1)S(1)} %bitcast.31), channel_id=1, source_target_pairs={{0,1},{1,0},{2,3},{3,2},{4,5},{5,4},{6,7},{7,6},{8,9},{9,8},{10,11... | collective-permute-start | bytes 1179656 | tf_op jit(solution)/shard_map/ppermute | solution.py:260
  53.5 15.3 %collective-permute-start.4 = (bf16[304,256]{1,0:T(8,128)(2,1)S(1)}, bf16[304,256]{1,0:T(8,128)(2,1)S(1)}, u32[]{:S(2)}, u32[]{:S(2)}) collective-permute-start(bf16[304,256]{1,0:T(8,128)(2,1)S(1)} %slice.55), channel_id=1, source_target_pairs={{0,8},{1,25},{8,0},{9,17},{16,24},{17,9},{24,16},{25,1},{2,10},{3,... | collective-permute-start | bytes 466952 | tf_op jit(solution)/shard_map/ppermute | solution.py:270
  61.6 13.2 %collective-permute-start.2 = (bf16[288,256]{1,0:T(8,128)(2,1)S(1)}, bf16[288,256]{1,0:T(8,128)(2,1)S(1)}, u32[]{:S(2)}, u32[]{:S(2)}) collective-permute-start(bf16[288,256]{1,0:T(8,128)(2,1)S(1)} %slice.53), channel_id=1, source_target_pairs={{0,8},{1,25},{8,0},{9,17},{16,24},{17,9},{24,16},{25,1},{2,10},{3,... | collective-permute-start | bytes 442376 | tf_op jit(solution)/shard_map/ppermute | solution.py:270
  68.9 12.9 %collective-permute-start.5 = (bf16[304,256]{1,0:T(8,128)(2,1)S(1)}, bf16[304,256]{1,0:T(8,128)(2,1)S(1)}, u32[]{:S(2)}, u32[]{:S(2)}) collective-permute-start(bf16[304,256]{1,0:T(8,128)(2,1)S(1)} %fusion), channel_id=1, source_target_pairs={{0,24},{1,9},{8,16},{9,1},{16,8},{17,25},{24,0},{25,17},{2,26},{3,... | collective-permute-start | bytes 466952 | tf_op jit(solution)/shard_map/ppermute | solution.py:270
  74.8 12.0 %collective-permute-start.3 = (bf16[288,256]{1,0:T(8,128)(2,1)S(1)}, bf16[288,256]{1,0:T(8,128)(2,1)S(1)}, u32[]{:S(2)}, u32[]{:S(2)}) collective-permute-start(bf16[288,256]{1,0:T(8,128)(2,1)S(1)} %fusion.3), channel_id=1, source_target_pairs={{0,24},{1,9},{8,16},{9,1},{16,8},{17,25},{24,0},{25,17},{2,26},{3,... | collective-permute-start | bytes 442376 | tf_op jit(solution)/shard_map/ppermute | solution.py:270
  81.9 12.9 %collective-permute-start.7 = (bf16[304,256]{1,0:T(8,128)(2,1)S(1)}, bf16[304,256]{1,0:T(8,128)(2,1)S(1)}, u32[]{:S(2)}, u32[]{:S(2)}) collective-permute-start(bf16[304,256]{1,0:T(8,128)(2,1)S(1)} %get-tuple-element.11), channel_id=1, source_target_pairs={{0,1},{1,0},{2,3},{3,2},{4,5},{5,4},{6,7},{7,6},{8,9},{9,8},{10,11... | collective-permute-start | bytes 466952 | tf_op jit(solution)/shard_map/ppermute | solution.py:260
  86.9 7.9 %collective-permute-start.6 = (bf16[288,256]{1,0:T(8,128)(2,1)S(1)}, bf16[288,256]{1,0:T(8,128)(2,1)S(1)}, u32[]{:S(2)}, u32[]{:S(2)}) collective-permute-start(bf16[288,256]{1,0:T(8,128)(2,1)S(1)} %get-tuple-element.13), channel_id=1, source_target_pairs={{0,1},{1,0},{2,3},{3,2},{4,5},{5,4},{6,7},{7,6},{8,9},{9,8},{10,11... | collective-permute-start | bytes 442376 | tf_op jit(solution)/shard_map/ppermute | solution.py:260
  94.8 10.1 %copy-start.1 = (s32[64]{0:T(128)S(1)}, s32[64]{0:T(128)}, u32[]{:S(2)}) copy-start(s32[64]{0:T(128)} %param.4) | copy-start | bytes 772
  99.3 17.0 %all-to-all-start.1 = ((bf16[16,104,128]{2,1,0:T(8,128)(2,1)}), bf16[16,104,128]{2,1,0:T(8,128)(2,1)S(1)}, u32[]{:S(2)}, u32[]{:S(2)}) async-start(bf16[16,104,128]{2,1,0:T(8,128)(2,1)} %shard_map.59), calls=%async_computation.1 | async-start | bytes 851968 | tf_op jit(solution)/shard_map/all_to_all | solution.py:335
  116.3 0.8 copy-start
